TPU v7x, 1024 devices: a whole 4x4x32 slice. The times are simulated.
1024 devices in a mesh: wide: 128 (over y, z), narrow: 8 (over x, core).
Axes of the slice: x: 4, y: 4, z: 32, core: 2. Of those that a mesh axis runs over, the one named last changes fastest.
Arguments:
- features: float32 [262144, 128], P(('wide', 'narrow')), may hold values from -6 to 6
- columns: int32 [4096, 16], P(('wide', 'narrow')), may hold values from 0 to 4095, as said below
- counts: int32 [4096], P(('wide', 'narrow')), may hold values from 1 to 16, as said below
- blocks: float32 [4096, 64, 1024], P(('wide', 'narrow')), may hold values from -0.1875 to 0.1875
- weight: float32 [128, 256], replicated, may hold values from -0.5 to 0.5
- bias: float32 [256], replicated, may hold values from -3 to 3
- cotangent: float32 [262144, 256], P(('wide', 'narrow')), may hold values from -24 to 24
Outputs:
- hidden: float32 [262144, 256], P(('wide', 'narrow'))
- weight_grad: float32 [128, 256], replicated
- bias_grad: float32 [256], replicated
- feature_grad: float32 [262144, 128], P(('wide', 'narrow'))
Inputs may be any that keep to these rules, and one draw needn't show every extreme that they name: The block column of any slot of block row r lies in stripes r // 32 - 1 to r // 32 + 1, where stripe t holds block columns t * 32 to (t + 1) * 32 - 1. `counts`: among the 4 block rows of each device one has all 16 slots in use.
All inputs are finite; a program needn't handle non-finite values.
Results may differ from a plain program's by a relative error of at most 0.0003.
Values sent between devices are 32-bit elements; how exact they have to be, the bound alone decides.
No kernel may reach another device: no remote copies, remote signals or barrier semaphores. Data moves between devices by JAX's collectives and lax.ppermute only.
A program may use at most 32 MiB of HBM per device.

v0:
```python
import jax
import jax.numpy as jnp
from jax import lax
from jax.sharding import PartitionSpec as P

BLK = 64


def with_halo(cells, sides, width):
    for axis, dim in sides:
        count = lax.axis_size(axis)
        ends = count - 1
        head = lax.slice_in_dim(cells, 0, width, axis=dim)
        tail = lax.slice_in_dim(cells, cells.shape[dim] - width, cells.shape[dim], axis=dim)
        cells = jnp.concatenate(
            [
                lax.ppermute(tail, axis, [(i, (i + 1) % count) for i in range(ends)]),
                cells,
                lax.ppermute(head, axis, [((i + 1) % count, i) for i in range(ends)]),
            ],
            axis=dim,
        )
    return cells


def from_behind(block, axis, distance):
    devices = range(lax.axis_size(axis))
    route = [(i - distance, i) for i in devices if i - distance in devices]
    return lax.ppermute(block, axis, route)


def activate(value):
    return jax.nn.gelu(value, approximate=True)


def body(features, columns, counts, blocks, weight, bias, cotangent):
    hi = lax.Precision.HIGHEST
    rows = features.shape[0]
    width = features.shape[1]
    block_rows = columns.shape[0]
    slots = columns.shape[1]
    span = block_rows * lax.axis_size("narrow")
    stripe_index = lax.axis_index("wide")
    local = columns - (stripe_index - 1) * span
    stripe = lax.all_gather(features, "narrow", axis=0, tiled=True)
    band = with_halo(stripe, (("wide", 0),), stripe.shape[0])
    band_blocks = band.reshape(3 * span, BLK, width)
    slot_of = (jnp.arange(slots * BLK, dtype=jnp.int32) // BLK)[None, :]
    usage = (slot_of < counts[:, None]).astype(jnp.float32)
    masked = blocks * usage[:, None, :]
    picked = jnp.take(band_blocks, local.reshape(-1), axis=0).reshape(
        block_rows, slots * BLK, width
    )
    aggregated = jnp.einsum("rim,rmf->rif", masked, picked, precision=hi).reshape(rows, width)
    preact = jnp.dot(aggregated, weight, precision=hi) + bias
    hidden, pullback = jax.vjp(activate, preact)
    dpre = pullback(cotangent)[0]
    weight_part = jnp.dot(aggregated.T, dpre, precision=hi)
    bias_part = jnp.sum(dpre, axis=0)
    weight_grad, bias_grad = lax.psum((weight_part, bias_part), ("wide", "narrow"))
    dagg = jnp.dot(dpre, weight.T, precision=hi).reshape(block_rows, BLK, width)
    terms = jnp.einsum("rim,rif->rmf", masked, dagg, precision=hi).reshape(
        block_rows * slots, BLK * width
    )
    targets = jnp.arange(3 * span, dtype=jnp.int32)[None, :]
    onehot = (local.reshape(-1)[:, None] == targets).astype(jnp.float32)
    gathered_terms = jnp.dot(onehot.T, terms, precision=hi)
    parts = gathered_terms.reshape(3, span * BLK, width)
    own = parts[1]
    for offset, piece in ((-1, parts[0]), (1, parts[2])):
        own = own + from_behind(piece, "wide", offset)
    feature_grad = lax.psum_scatter(own, "narrow", scatter_dimension=0, tiled=True)
    return (hidden, weight_grad, bias_grad, feature_grad)


def solution(mesh):
    placed = (
        P(("wide", "narrow"), None),
        P(("wide", "narrow"), None),
        P(("wide", "narrow")),
        P(("wide", "narrow"), None, None),
        P(),
        P(),
        P(("wide", "narrow"), None),
    )
    return jax.shard_map(
        body,
        mesh=mesh,
        in_specs=placed,
        out_specs=(P(("wide", "narrow"), None), P(), P(), P(("wide", "narrow"), None)),
        check_vma=False,
    )
```

profile of v0, /device:TPU:1, one launch (start us, length us, event | category | flops | bytes accessed | tf_op | source)
XLA Modules:
  0.0 1018.4 jit_solution(9986572818544681479)
XLA Ops:
  7.2 0.0 copy-start
  7.2 0.0 all-gather.2.cloned.1.call-start
  7.2 0.7 all-gather.2.cloned.1.call-update
  7.9 0.0 all-reduce.2.cloned.1.call-start
  8.0 53.0 %all-gather.2.cloned.1.call-done = f32[2048,128]{1,0:T(8,128)} async-done(((f32[256,128]{1,0:T(8,128)}), f32[2048,128]{1,0:T(8,128)}) %all-gather.2.cloned.1.call-update) | async-done | bytes 1048592 | tf_op jit(solution)/shard_map/all_gather | solution.py:45
  60.9 1.3 collective-permute-start.1
  62.2 5.0 collective-permute-start
  67.2 0.7 compare_and_fusion
  67.9 0.1 reshape.111
  68.0 0.1 reshape.113
  68.1 0.1 broadcast_in_dim.19
  68.1 0.1 broadcast_in_dim.20
  68.3 0.7 compare_convert_fusion
  69.0 18.5 %collective-permute-done.1 = f32[2048,128]{1,0:T(8,128)S(1)} collective-permute-done((f32[2048,128]{1,0:T(8,128)}, f32[2048,128]{1,0:T(8,128)S(1)}, u32[]{:S(2)}, u32[]{:S(2)}) %collective-permute-start.1) | collective-permute-done | bytes 1048608 | tf_op jit(solution)/shard_map/ppermute | solution.py:19
  87.5 0.0 copy-start.3
  87.5 1.0 copy-done.3
  88.5 0.0 collective-permute-done
  88.6 2.1 pad_maximum_fusion
  90.6 2.0 gather_fusion
  92.6 0.0 copy-start.1
  92.6 2.8 bitcast_select_fusion
  95.5 0.0 copy-done.1
  95.5 0.0 copy-start.5
  95.5 0.0 copy-start.6
  95.5 1.5 fusion.2
  97.0 0.0 copy-start.4
  97.0 0.0 copy-done
  97.0 0.0 copy-done.5
  97.0 0.0 copy-done.6
  97.0 1.2 fusion.18
  98.2 0.4 fusion.22
  98.6 0.0 copy-done.4
  98.6 3.4 fusion
  102.1 1.5 reshape.115
  103.6 3.1 fusion.12
  106.8 0.2 fusion.20
  107.0 1.1 squeeze.10
  108.1 0.0 copy-start.2
  108.1 1.2 squeeze.11
  109.3 5.0 collective-permute-start.3
  114.3 0.0 copy-done.2
  114.3 1.3 collective-permute-start.2
  115.6 2.0 fusion.21
  117.6 0.0 all-reduce.2.cloned.1.call-update
  117.6 0.0 reduce-scatter.2.cloned.1.call-start
  117.7 0.2 squeeze.9
  117.8 16.9 %collective-permute-done.3 = f32[2048,128]{1,0:T(8,128)} collective-permute-done((f32[2048,128]{1,0:T(8,128)}, f32[2048,128]{1,0:T(8,128)}, u32[]{:S(2)}, u32[]{:S(2)}) %collective-permute-start.3) | collective-permute-done | bytes 1048608 | tf_op jit(solution)/shard_map/ppermute | solution.py:29
  134.7 4.6 collective-permute-done.2
  139.3 2.7 add_add_fusion
  142.0 0.0 reduce-scatter.2.cloned.1.call-update
  142.0 163.1 %psum.15 = f32[256]{0:T(256)} all-reduce(f32[256]{0:T(256)S(1)} %get-tuple-element.4), channel_id=1, replica_groups=mesh['wide'=128,'narrow'=8] {'wide','narrow'}, use_global_device_ids=true, to_apply=%region_2.3 | all-reduce | flops 256 | bytes 2048 | tf_op jit(solution)/shard_map/psum | solution.py:60
  305.2 669.3 %all-reduce.2.cloned.1.call-done = f32[128,256]{1,0:T(8,128)} async-done(((f32[128,256]{1,0:T(8,128)}), f32[128,256]{1,0:T(8,128)}) %all-reduce.2.cloned.1.call-update) | async-done | bytes 131088 | tf_op jit(solution)/shard_map/psum | solution.py:60
  974.4 35.9 %reduce-scatter.2.cloned.1.call-done = f32[256,128]{1,0:T(8,128)} async-done(((f32[2048,128]{1,0:T(8,128)}), f32[256,128]{1,0:T(8,128)}) %reduce-scatter.2.cloned.1.call-update) | async-done | bytes 131088 | tf_op jit(solution)/shard_map/reduce_scatter | solution.py:72
  1010.3 1.6 copy.12
  (3 shorter events, 0.0 us)
Async XLA Ops:
  7.2 89.8 %copy-start = (f32[128,256]{1,0:T(8,128)S(1)}, f32[128,256]{1,0:T(8,128)}, u32[]{:S(2)}) copy-start(f32[128,256]{1,0:T(8,128)} %param.11) | copy-start | bytes 393220
  7.2 53.8 %all-gather.2.cloned.1.call-start = ((), (), s32[]{:S(2)}) async-start(), calls=%async_computation.1 | async-start | bytes 1179648 | tf_op jit(solution)/shard_map/all_gather | solution.py:45
  7.9 966.5 %all-reduce.2.cloned.1.call-start = ((), (), s32[]{:S(2)}) async-start(), calls=%async_computation.2 | async-start | bytes 262144 | tf_op jit(solution)/shard_map/psum | solution.py:60
  60.9 26.6 %collective-permute-start.1 = (f32[2048,128]{1,0:T(8,128)}, f32[2048,128]{1,0:T(8,128)S(1)}, u32[]{:S(2)}, u32[]{:S(2)}) collective-permute-start(f32[2048,128]{1,0:T(8,128)} %all-gather.2.cloned.1.call-done), channel_id=1, source_target_pairs={{8,0},{16,8},{24,16},{32,24},{40,32},{48,40},{56,48},{64,56},{72,6... | collective-permute-start | bytes 3145736 | tf_op jit(solution)/shard_map/ppermute | solution.py:19
  62.2 26.3 %collective-permute-start = (f32[2048,128]{1,0:T(8,128)}, f32[2048,128]{1,0:T(8,128)}, u32[]{:S(2)}, u32[]{:S(2)}) collective-permute-start(f32[2048,128]{1,0:T(8,128)} %all-gather.2.cloned.1.call-done), channel_id=1, source_target_pairs={{0,8},{8,16},{16,24},{24,32},{32,40},{40,48},{48,56},{56,64},{64,7... | collective-permute-start | bytes 3145736 | tf_op jit(solution)/shard_map/ppermute | solution.py:17
  87.5 1.0 copy-start.3
  92.6 2.8 copy-start.1
  95.5 1.5 copy-start.5
  95.5 1.5 copy-start.6
  97.0 1.7 copy-start.4
  108.1 6.2 copy-start.2
  109.3 25.4 %collective-permute-start.3 = (f32[2048,128]{1,0:T(8,128)}, f32[2048,128]{1,0:T(8,128)}, u32[]{:S(2)}, u32[]{:S(2)}) collective-permute-start(f32[2048,128]{1,0:T(8,128)} %squeeze.11), channel_id=1, source_target_pairs={{0,8},{8,16},{16,24},{24,32},{32,40},{40,48},{48,56},{56,64},{64,7... | collective-permute-start | bytes 3145736 | tf_op jit(solution)/shard_map/ppermute | solution.py:29
  114.3 25.0 %collective-permute-start.2 = (f32[2048,128]{1,0:T(8,128)S(1)}, f32[2048,128]{1,0:T(8,128)}, u32[]{:S(2)}, u32[]{:S(2)}) collective-permute-start(f32[2048,128]{1,0:T(8,128)S(1)} %copy-done.2), channel_id=1, source_target_pairs={{8,0},{16,8},{24,16},{32,24},{40,32},{48,40},{56,48},{64,56},{72,6... | collective-permute-start | bytes 3145736 | tf_op jit(solution)/shard_map/ppermute | solution.py:29
  117.6 892.7 %reduce-scatter.2.cloned.1.call-start = ((), (), s32[]{:S(2)}) async-start(), calls=%async_computation.3 | async-start | bytes 1179648 | tf_op jit(solution)/shard_map/reduce_scatter | solution.py:72
Sparse Core Ops, SparseCore 0:
  10.7 50.1 all-gather.1
  117.7 856.6 all-reduce.1
  978.8 31.4 reduce-scatter.1
where the time goes:
time: 1020 us
  waiting for transfers between devices  799 us (78%)
  blocking collectives  163 us (16%)
  between operations  13.9 us (1%)
  starting transfers between devices  12.7 us (1%)
  matrix products  11.6 us (1%)
    psum x1, waiting for transfers between devices, body(): lax.psum((weight_part, bias_part), ('wide', 'narrow'))  669 us
    psum x1, blocking collectives, body(): lax.psum((weight_part, bias_part), ('wide', 'narrow'))  163 us
    all_gather x1, waiting for transfers between devices, body(): stripe = lax.all_gather(features, 'narrow', axis=0, tiled=True)  53 us
    reduce_scatter x1, waiting for transfers between devices, body(): lax.psum_scatter(own, 'narrow', scatter_dimension=0, tiled=True)  35.9 us
    ppermute x2, waiting for transfers between devices, from_behind(): return lax.ppermute(block, axis, route)  21.5 us
  transfers between devices with their start and end apart: 7, of which 6 were waited for; matrix products, arithmetic and copies ran while one was open for 1% of the time, Pallas kernels for 0%

commit v1 on v0

v1 whole, which is shorter than its diff:
```python
import math

import jax
import jax.numpy as jnp
from jax import lax
from jax.experimental import pallas as pl
from jax.experimental.pallas import tpu as pltpu
from jax.sharding import Mesh, PartitionSpec as P

BLK = 64
LANES = 128
VMEM_LIMIT = 40 * 1024 * 1024
PLANE = ("y", "x", "core")
WIDE = ("y", "z")
ALL = ("y", "z", "x", "core")
C0 = math.sqrt(2.0 / math.pi)
C1 = 0.044715


def split(value):
    high = value.astype(jnp.bfloat16)
    low = (value - high.astype(jnp.float32)).astype(jnp.bfloat16)
    return high, low


def dot(lhs, rhs, dims=((1,), (0,))):
    return lax.dot_general(lhs, rhs, (dims, ((), ())), preferred_element_type=jnp.float32)


def vmem(count):
    return [pl.BlockSpec(memory_space=pltpu.VMEM)] * count


def params():
    return pltpu.CompilerParams(vmem_limit_bytes=VMEM_LIMIT)


def prepare_kernel(counts, blocks, weight, stacked, turned, weight_rows, weight_low, weight_turned):
    rows, _, width = blocks.shape
    slot = lax.broadcasted_iota(jnp.int32, (BLK, width), 1) // BLK
    for r in range(rows):
        masked = jnp.where(slot < counts[r], blocks[r], 0.0)
        high, low = split(masked)
        stacked[r, :BLK, :] = high
        stacked[r, BLK:, :] = low
        both = jnp.concatenate([masked, masked - high.astype(jnp.float32)], axis=0)
        turned[r] = both.T.astype(jnp.bfloat16)
    high, low = split(weight[...])
    depth = weight.shape[0]
    weight_rows[:depth, :] = high
    weight_rows[depth:, :] = high
    weight_low[...] = low
    turned_high, turned_low = split(weight[...].T)
    weight_turned[:, :depth] = turned_high
    weight_turned[:, depth:] = turned_low


def prepare(counts, blocks, weight):
    rows, _, width = blocks.shape
    depth, hid = weight.shape
    half = jnp.bfloat16
    return pl.pallas_call(
        prepare_kernel,
        out_shape=(
            jax.ShapeDtypeStruct((rows, 2 * BLK, width), half),
            jax.ShapeDtypeStruct((rows, width, 2 * BLK), half),
            jax.ShapeDtypeStruct((2 * depth, hid), half),
            jax.ShapeDtypeStruct((depth, hid), half),
            jax.ShapeDtypeStruct((hid, 2 * depth), half),
        ),
        in_specs=[pl.BlockSpec(memory_space=pltpu.SMEM)] + vmem(2),
        out_specs=vmem(5),
        compiler_params=params(),
        cost_estimate=pl.CostEstimate(flops=2_000_000, bytes_accessed=4_000_000, transcendentals=0),
        name="prepare",
    )(counts, blocks, weight)


def layer_kernel(
    places, stacked, p0, p1, p2, p3, p4, p5, weight_rows, weight_low, weight_turned, bias, cotangent,
    hidden, sums, grads, band, picked, aggregated, sems,
):
    pieces = (p0, p1, p2, p3, p4, p5)
    span = p0.shape[0]
    copies = [
        pltpu.make_async_copy(piece, band.at[pl.ds(i * span, span)], sems.at[i])
        for i, piece in enumerate(pieces)
    ]
    for copy in copies:
        copy.start()
    for copy in copies:
        copy.wait()
    rows, _, width = stacked.shape
    slots = width // BLK
    depth = aggregated.shape[1]
    for r in range(rows):
        for k in range(slots):
            start = pl.multiple_of(places[r * slots + k] * BLK, BLK)
            high, low = split(band[pl.ds(start, BLK), :])
            picked[r % 2, k * BLK:(k + 1) * BLK, :depth] = high
            picked[r % 2, k * BLK:(k + 1) * BLK, depth:] = low
        product = dot(stacked[r], picked[r % 2])
        product = product[:BLK] + product[BLK:]
        aggregated[r * BLK:(r + 1) * BLK, :] = product[:, :depth] + product[:, depth:]
    value = aggregated[...]
    high, low = split(value)
    preact = dot(jnp.concatenate([high, low], axis=1), weight_rows[...]) + dot(high, weight_low[...])
    preact = preact + bias[...]
    square = preact * preact
    slope = jnp.tanh(C0 * (preact + C1 * (square * preact)))
    hidden[...] = 0.5 * preact * (1.0 + slope)
    local = 0.5 * (1.0 + slope) + 0.5 * preact * (1.0 - slope * slope) * (C0 * (1.0 + 3.0 * C1 * square))
    dpre = cotangent[...] * local
    dhigh, dlow = split(dpre)
    hid = dpre.shape[1]
    over_rows = ((0,), (0,))
    outer = dot(jnp.concatenate([value, value - high.astype(jnp.float32)], axis=1).T.astype(jnp.bfloat16), dhigh)
    outer = outer[:depth] + outer[depth:] + dot(value.T.astype(jnp.bfloat16), dlow)
    total = jnp.sum(dpre, axis=0, keepdims=True)
    shards = sums.shape[0]
    per = LANES * 2 // shards
    sums[:, :, per * LANES:] = jnp.zeros((shards, 1, LANES), jnp.float32)
    for d in range(shards):
        for j in range(per):
            row = d * per + j
            side, at = row // depth, row % depth
            sums[d, :, j * LANES:(j + 1) * LANES] = outer[at:at + 1, side * LANES:(side + 1) * LANES]
    for side in range(2):
        sums[side, :, per * LANES:] = total[:, side * LANES:(side + 1) * LANES]
    back = dot(jnp.concatenate([dhigh, dlow], axis=0), weight_turned[...])
    count = dpre.shape[0]
    back = back[:count] + back[count:]
    back = back[:, :depth] + back[:, depth:]
    bhigh, blow = split(back)
    for r in range(rows):
        for top in (0, BLK):
            grads[r, top:top + BLK, :depth] = bhigh[r * BLK:(r + 1) * BLK]
            grads[r, top:top + BLK, depth:] = blow[r * BLK:(r + 1) * BLK]


def layer(places, stacked, pieces, weight_rows, weight_low, weight_turned, bias, cotangent, shards):
    rows, _, width = stacked.shape
    span, depth = pieces[0].shape
    count, hid = cotangent.shape
    return pl.pallas_call(
        layer_kernel,
        out_shape=(
            jax.ShapeDtypeStruct((count, hid), jnp.float32),
            jax.ShapeDtypeStruct((shards, 1, depth * hid // shards + LANES), jnp.float32),
            jax.ShapeDtypeStruct((rows, 2 * BLK, 2 * depth), jnp.bfloat16),
        ),
        in_specs=[pl.BlockSpec(memory_space=pltpu.SMEM)] + vmem(1)
        + [pl.BlockSpec(memory_space=pl.ANY)] * 6 + vmem(5),
        out_specs=vmem(3),
        scratch_shapes=[
            pltpu.VMEM((6 * span, depth), jnp.float32),
            pltpu.VMEM((2, width, 2 * depth), jnp.bfloat16),
            pltpu.VMEM((count, depth), jnp.float32),
            pltpu.SemaphoreType.DMA((6,)),
        ],
        compiler_params=params(),
        cost_estimate=pl.CostEstimate(flops=400_000_000, bytes_accessed=6_000_000, transcendentals=65536),
        name="layer",
    )(places, stacked, *pieces, weight_rows, weight_low, weight_turned, bias, cotangent)


def spread_kernel(places, turned, grads, other, before, own, after, band, sems):
    rows, width, _ = turned.shape
    slots = width // BLK
    depth = band.shape[1]
    span = before.shape[0]
    band[...] = jnp.zeros_like(band)
    for r in range(rows):
        product = dot(turned[r], grads[r])
        product = product[:, :depth] + product[:, depth:]
        for k in range(slots):
            start = pl.multiple_of(places[r * slots + k] * BLK, BLK)
            where = pl.ds(start, BLK)
            band[where, :] = band[where, :] + product[k * BLK:(k + 1) * BLK]
    copies = [pltpu.make_async_copy(band.at[pl.ds(0, 3 * span)], other, sems.at[0])] + [
        pltpu.make_async_copy(band.at[pl.ds((3 + i) * span, span)], piece, sems.at[1 + i])
        for i, piece in enumerate((before, own, after))
    ]
    for copy in copies:
        copy.start()
    for copy in copies:
        copy.wait()


def spread(places, turned, grads, span, depth):
    piece = jax.ShapeDtypeStruct((span, depth), jnp.float32)
    return pl.pallas_call(
        spread_kernel,
        out_shape=(jax.ShapeDtypeStruct((3 * span, depth), jnp.float32), piece, piece, piece),
        in_specs=[pl.BlockSpec(memory_space=pltpu.SMEM)] + vmem(2),
        out_specs=[pl.BlockSpec(memory_space=pl.ANY)] * 4,
        scratch_shapes=[
            pltpu.VMEM((6 * span, depth), jnp.float32),
            pltpu.SemaphoreType.DMA((4,)),
        ],
        compiler_params=params(),
        cost_estimate=pl.CostEstimate(flops=300_000_000, bytes_accessed=5_000_000, transcendentals=0),
        name="spread",
    )(places, turned, grads)


def sum_kernel(parts, out):
    out[...] = jnp.broadcast_to(jnp.sum(parts[...], axis=0, keepdims=True), out.shape)


def sum_for_all(parts, shards):
    return pl.pallas_call(
        sum_kernel,
        out_shape=jax.ShapeDtypeStruct((shards,) + parts.shape[1:], parts.dtype),
        in_specs=vmem(1),
        out_specs=pl.BlockSpec(memory_space=pltpu.VMEM),
        compiler_params=params(),
        name="sum_for_all",
    )(parts)


def unpack_kernel(parts, outer, total):
    shards = parts.shape[0]
    depth = outer.shape[0]
    per = LANES * 2 // shards
    for d in range(shards):
        for j in range(per):
            row = d * per + j
            side, at = row // depth, row % depth
            outer[at:at + 1, side * LANES:(side + 1) * LANES] = parts[d, :, j * LANES:(j + 1) * LANES]
    for side in range(2):
        total[:, side * LANES:(side + 1) * LANES] = parts[side, :, per * LANES:]


def unpack(parts, depth, hid):
    return pl.pallas_call(
        unpack_kernel,
        out_shape=(
            jax.ShapeDtypeStruct((depth, hid), jnp.float32),
            jax.ShapeDtypeStruct((1, hid), jnp.float32),
        ),
        in_specs=vmem(1),
        out_specs=vmem(2),
        compiler_params=params(),
        name="unpack",
    )(parts)


def swap_cores(value):
    return lax.ppermute(value, "core", [(0, 1), (1, 0)])


def along_wide(value, step):
    count = lax.axis_size(WIDE)
    route = [(i, i + step) for i in range(count) if 0 <= i + step < count]
    return lax.ppermute(value, WIDE, route)


def body(features, columns, counts, blocks, weight, bias, cotangent):
    rows, depth = features.shape
    hid = weight.shape[1]
    chips = lax.axis_size("x")
    cores = lax.axis_size("core")
    shards = lax.axis_size(PLANE)
    levels = lax.axis_size("z")
    block_rows = columns.shape[0]
    stripe = block_rows * chips * cores
    span = chips * rows

    local = columns - (lax.axis_index(WIDE) - 1) * stripe
    part = local // stripe
    within = local % stripe
    device = within // block_rows
    foreign = (device % cores) ^ lax.axis_index("core")
    piece = (1 - foreign) * 3 + part
    places = (piece * (chips * block_rows) + (device // cores) * block_rows + within % block_rows).reshape(-1)

    row_of_chips = jnp.broadcast_to(features[None], (chips, rows, depth))
    own = lax.all_to_all(row_of_chips, "x", 0, 0).reshape(span, depth)
    before = along_wide(own, 1)
    after = along_wide(own, -1)
    own_other = swap_cores(own)
    before_other = swap_cores(before)
    after_other = swap_cores(after)
    stacked, turned, weight_rows, weight_low, weight_turned = prepare(counts, blocks, weight)
    pieces = (before_other, own_other, after_other, before, own, after)
    hidden, sums, grads = layer(
        places, stacked, pieces, weight_rows, weight_low, weight_turned, bias[None], cotangent, shards
    )

    other, to_before, to_own, to_after = spread(places, turned, grads, span, depth)
    from_core = swap_cores(other)
    from_after = along_wide(to_before + from_core[:span], -1)
    from_before = along_wide(to_after + from_core[2 * span:], 1)
    total = to_own + from_core[span:2 * span] + from_after + from_before
    shares = lax.all_to_all(total.reshape(chips, rows, depth), "x", 0, 0)
    feature_grad = jnp.sum(shares, axis=0)

    scattered = lax.all_to_all(sums, PLANE, 0, 0)
    scattered = lax.all_to_all(sum_for_all(scattered, levels), "z", 0, 0)
    gathered = lax.all_to_all(sum_for_all(scattered, shards), PLANE, 0, 0)
    weight_grad, bias_grad = unpack(gathered, depth, hid)
    return (hidden, weight_grad, bias_grad.reshape(hid), feature_grad)


def solution(mesh):
    wide, narrow = mesh.devices.shape
    levels = 32 if wide % 32 == 0 else wide // 2
    fine = Mesh(mesh.devices.reshape(wide // levels, levels, narrow // 2, 2), ALL)
    nodes = P(ALL, None)
    return jax.shard_map(
        body,
        mesh=fine,
        in_specs=(nodes, nodes, P(ALL), P(ALL, None, None), P(), P(), nodes),
        out_specs=(nodes, P(), P(), nodes),
        check_vma=False,
    )
```

time: 1020 us -> 148 us (0.15)
  waiting for transfers between devices: 799 us -> 40.1 us
  blocking collectives: 163 us -> 36.7 us
  starting transfers between devices: 12.7 us -> 56.2 us
  between operations: 13.9 us -> 0.87 us
  matrix products: 11.6 us -> 0 us
    psum x1 -> x0, waiting for transfers between devices: 669 us -> none  [body(): lax.psum((weight_part, bias_part), ('wide', 'narrow'))]
    psum x1 -> x0, blocking collectives: 163 us -> none  [body(): lax.psum((weight_part, bias_part), ('wide', 'narrow'))]
    all_gather x1 -> x0, waiting for transfers between devices: 53 us -> none  [body(): stripe = lax.all_gather(features, 'narrow', axis=0, tiled=True)]
    all_to_all x0 -> x3, waiting for transfers between devices: none -> 39.2 us  [the longest x1 24.7 us: body(): scattered = lax.all_to_all(sum_for_all(scattered, levels), 'z', 0, 0)]
    ppermute x4 -> x8, waiting for transfers between devices: 40 us -> 0.91 us  [the longest x4 0.9 us: swap_cores(): return lax.ppermute(value, 'core', [(0, 1), (1, 0)])]
    all_to_all x0 -> x2, blocking collectives: none -> 36.7 us  [the longest x1 25.2 us: body(): scattered = lax.all_to_all(sums, PLANE, 0, 0)]
    reduce_scatter x1 -> x0, waiting for transfers between devices: 35.9 us -> none  [body(): lax.psum_scatter(own, 'narrow', scatter_dimension=0, tiled=True)]
    ppermute x4 -> x8, starting transfers between devices: 12.6 us -> 35.3 us  [the longest x4 22.8 us: swap_cores(): return lax.ppermute(value, 'core', [(0, 1), (1, 0)])]
  transfers between devices with their start and end apart: 7 -> 11, of which waited for: 6 -> 4; matrix products, arithmetic and copies ran while one was open for 1% -> 2% of each run, Pallas kernels for 0% -> 2%
where the time goes in v1:
time: 148 us
  starting transfers between devices  56.2 us (38%)
  waiting for transfers between devices  40.1 us (27%)
  blocking collectives  36.7 us (25%)
  Pallas kernels  8.55 us (6%)
  other arithmetic  3.97 us (3%)
    all_to_all x1, blocking collectives, body(): scattered = lax.all_to_all(sums, PLANE, 0, 0)  25.2 us
    all_to_all x1, waiting for transfers between devices, body(): scattered = lax.all_to_all(sum_for_all(scattered, levels), 'z', 0, 0)  24.7 us
    ppermute x4, starting transfers between devices, swap_cores(): return lax.ppermute(value, 'core', [(0, 1), (1, 0)])  22.8 us
    ppermute x4, starting transfers between devices, along_wide(): return lax.ppermute(value, WIDE, route)  12.4 us
    all_to_all x1, blocking collectives, body(): own = lax.all_to_all(row_of_chips, 'x', 0, 0).reshape(span, depth)  11.6 us
    all_to_all x1, starting transfers between devices, body(): scattered = lax.all_to_all(sum_for_all(scattered, levels), 'z', 0, 0)  11.1 us
    all_to_all x1, waiting for transfers between devices, body(): shares = lax.all_to_all(total.reshape(chips, rows, depth), 'x', 0, 0)  8.57 us
    all_to_all x1, starting transfers between devices, body(): gathered = lax.all_to_all(sum_for_all(scattered, shards), PLANE, 0, 0)  6.38 us
  transfers between devices with their start and end apart: 11, of which 4 were waited for; matrix products, arithmetic and copies ran while one was open for 2% of the time, Pallas kernels for 2%

profile of v1, /device:TPU:1, one launch (start us, length us, event | category | flops | bytes accessed | tf_op | source)
XLA Modules:
  0.0 147.5 jit_solution(944814086993164363)
XLA Ops:
  0.6 0.0 copy-start.5
  0.6 0.0 copy-start.2
  0.7 0.0 copy-start
  0.7 0.0 copy-start.4
  0.7 0.0 copy-start.1
  0.7 0.0 copy-start.3
  0.7 1.0 broadcast_in_dim.4
  1.7 11.6 %all_to_all.25 = f32[4,256,128]{2,1,0:T(8,128)S(1)} all-to-all(f32[4,256,128]{2,1,0:T(8,128)S(1)} %broadcast_in_dim.4), channel_id=1, replica_groups=mesh['y'=4,'z'=32,'x'=4,'core'=2] {'x'}, dimensions={0} | all-to-all | bytes 1048576 | tf_op jit(solution)/shard_map/all_to_all | solution.py:279
  13.3 1.3 collective-permute-start.3
  14.6 5.8 %collective-permute-start = (f32[1024,128]{1,0:T(8,128)S(1)}, f32[1024,128]{1,0:T(8,128)S(1)}, u32[]{:S(2)}, u32[]{:S(2)}) collective-permute-start(f32[1024,128]{1,0:T(8,128)S(1)} %bitcast.5), channel_id=1, source_target_pairs={{0,8},{8,16},{16,24},{24,32},{32,40},{40,48},{48,56},{56,64},{64,7... | collective-permute-start | bytes 1572872 | tf_op jit(solution)/shard_map/ppermute | solution.py:256
  20.5 13.7 %collective-permute-start.2 = (f32[1024,128]{1,0:T(8,128)S(1)}, f32[1024,128]{1,0:T(8,128)S(1)}, u32[]{:S(2)}, u32[]{:S(2)}) collective-permute-start(f32[1024,128]{1,0:T(8,128)S(1)} %bitcast.6), channel_id=1, source_target_pairs={{0,1},{1,0},{2,3},{3,2},{4,5},{5,4},{6,7},{7,6},{8,9},{9,8},{10,11... | collective-permute-start | bytes 1572872 | tf_op jit(solution)/shard_map/ppermute | solution.py:250
  34.2 0.0 collective-permute-done.3.p5
  34.2 5.2 %collective-permute-start.4 = (f32[1024,128]{1,0:T(8,128)S(1)}, f32[1024,128]{1,0:T(8,128)}, u32[]{:S(2)}, u32[]{:S(2)}) collective-permute-start(f32[1024,128]{1,0:T(8,128)S(1)} %collective-permute-done.3.p5), channel_id=1, source_target_pairs={{0,1},{1,0},{2,3},{3,2},{4,5},{5,4},{6,7},{7,6},{8,9},{9,8},{10,11... | collective-permute-start | bytes 1572872 | tf_op jit(solution)/shard_map/ppermute | solution.py:250
  39.3 0.0 collective-permute-done.p3
  39.4 1.9 %collective-permute-start.1 = (f32[1024,128]{1,0:T(8,128)S(1)}, f32[1024,128]{1,0:T(8,128)}, u32[]{:S(2)}, u32[]{:S(2)}) collective-permute-start(f32[1024,128]{1,0:T(8,128)S(1)} %collective-permute-done.p3), channel_id=1, source_target_pairs={{0,1},{1,0},{2,3},{3,2},{4,5},{5,4},{6,7},{7,6},{8,9},{9,8},{10,11... | collective-permute-start | bytes 1572872 | tf_op jit(solution)/shard_map/ppermute | solution.py:250
  41.3 0.0 copy-done.5
  41.3 0.1 reshape.21.places
  41.4 0.0 copy-done.2
  41.4 0.0 copy-done
  41.4 0.0 copy-done.4
  41.4 0.9 prepare.1
  42.4 0.0 collective-permute-done.2.p1
  42.4 0.0 collective-permute-done.4.p2
  42.4 0.9 collective-permute-done.1.p0
  43.3 0.0 copy-done.1
  43.3 0.0 copy-done.3
  43.3 3.7 %layer.1 = (f32[256,256]{1,0:T(8,128)}, f32[32,1,1152]{2,1,0:T(1,128)S(1)}, bf16[4,128,256]{2,1,0:T(8,128)(2,1)S(1)}) custom-call(s32[64]{0:T(128)S(1)} %reshape.21.places, bf16[4,128,1024]{2,1,0:T(8,128)(2,1)S(1)} %get-tuple-element.18.stacked, f32[1024,128]{1,0:T(8,128)} %collective-permute-done.1.p0, f32[1024,128]{1,0:T(8,128)S(1)} %collective-permute-done.2.p1, ...), custom_call_target="tpu_custom_call" | custom-call | flops 400000000 | bytes 6000000 | tf_op jit(solution)/shard_map/layer/pallas_call | solution.py:145
  47.0 1.7 %spread.1 = (f32[3072,128]{1,0:T(8,128)S(1)}, f32[1024,128]{1,0:T(8,128)S(1)}, f32[1024,128]{1,0:T(8,128)S(1)}, f32[1024,128]{1,0:T(8,128)S(1)}) custom-call(s32[64]{0:T(128)S(1)} %reshape.21.places, bf16[4,1024,128]{2,1,0:T(8,128)(2,1)S(1)} %get-tuple-element.26.turned, bf16[4,128,256]{2,1,0:T(8,128)(2,1)S(1)} %get-tuple-element.27.grads), custom_call_target="tpu_custom_call" | custom-call | flops 300000000 | bytes 5000000 | tf_op jit(solution)/shard_map/spread/pallas_call | solution.py:192
  48.7 2.0 %collective-permute-start.5 = (f32[3072,128]{1,0:T(8,128)S(1)}, f32[3072,128]{1,0:T(8,128)}, u32[]{:S(2)}, u32[]{:S(2)}) collective-permute-start(f32[3072,128]{1,0:T(8,128)S(1)} %get-tuple-element.29), channel_id=1, source_target_pairs={{0,1},{1,0},{2,3},{3,2},{4,5},{5,4},{6,7},{7,6},{8,9},{9,8},{10,11... | collective-permute-start | bytes 4718600 | tf_op jit(solution)/shard_map/ppermute | solution.py:250
  50.8 25.2 %all_to_all.26.parts = f32[32,1,1152]{2,1,0:T(1,128)S(1)} all-to-all(f32[32,1,1152]{2,1,0:T(1,128)S(1)} %get-tuple-element.23), channel_id=1, replica_groups=mesh['y'=4,'z'=32,'x'=4,'core'=2] {'y','x','core'}, dimensions={0} | all-to-all | bytes 294912 | tf_op jit(solution)/shard_map/all_to_all | solution.py:299
  75.9 0.8 sum_for_all.2
  76.7 11.1 %all-to-all-start.2 = ((f32[32,1,1152]{2,1,0:T(1,128)}), f32[32,1,1152]{2,1,0:T(1,128)S(1)}, u32[]{:S(2)}, u32[]{:S(2)}) async-start(f32[32,1,1152]{2,1,0:T(1,128)} %sum_for_all.2), calls=%async_computation.2 | async-start | bytes 294912 | tf_op jit(solution)/shard_map/all_to_all | solution.py:300
  87.8 0.0 collective-permute-done.5
  87.8 1.3 slice_add_fusion.1
  89.1 1.3 collective-permute-start.6
  90.4 4.0 %collective-permute-start.7 = (f32[1024,128]{1,0:T(8,128)S(1)}, f32[1024,128]{1,0:T(8,128)S(1)}, u32[]{:S(2)}, u32[]{:S(2)}) collective-permute-start(f32[1024,128]{1,0:T(8,128)S(1)} %get-tuple-element.33), channel_id=1, source_target_pairs={{0,8},{8,16},{16,24},{24,32},{32,40},{40,48},{48,56},{56,64},{64,7... | collective-permute-start | bytes 1572872 | tf_op jit(solution)/shard_map/ppermute | solution.py:256
  94.4 24.7 %all-to-all-done.2.parts = f32[32,1,1152]{2,1,0:T(1,128)S(1)} async-done(((f32[32,1,1152]{2,1,0:T(1,128)}), f32[32,1,1152]{2,1,0:T(1,128)S(1)}, u32[]{:S(2)}, u32[]{:S(2)}) %all-to-all-start.2) | async-done | bytes 147488 | tf_op jit(solution)/shard_map/all_to_all | solution.py:300
  119.1 0.8 sum_for_all.3
  119.9 6.4 %all-to-all-start.3 = ((f32[32,1,1152]{2,1,0:T(1,128)}), f32[32,1,1152]{2,1,0:T(1,128)S(1)}, u32[]{:S(2)}, u32[]{:S(2)}) async-start(f32[32,1,1152]{2,1,0:T(1,128)} %sum_for_all.3), calls=%async_computation.3 | async-start | bytes 294912 | tf_op jit(solution)/shard_map/all_to_all | solution.py:301
  126.2 0.0 collective-permute-done.6
  126.3 0.0 collective-permute-done.7
  126.3 2.0 %fusion.1 = f32[1024,128]{1,0:T(8,128)} fusion(f32[1024,128]{1,0:T(8,128)S(1)} %collective-permute-done.7, f32[1024,128]{1,0:T(8,128)S(1)} %collective-permute-done.6, f32[1024,128]{1,0:T(8,128)S(1)} %get-tuple-element.28, f32[3072,128]{1,0:T(8,128)} %collective-permute-done.5), kind=kLoop, calls=%fused_computation.4 | loop fusion | flops 393216 | bytes 2621440 | tf_op jit(solution)/shard_map/add | solution.py:295
  128.2 5.9 %all-to-all-done.3.parts = f32[32,1,1152]{2,1,0:T(1,128)S(1)} async-done(((f32[32,1,1152]{2,1,0:T(1,128)}), f32[32,1,1152]{2,1,0:T(1,128)S(1)}, u32[]{:S(2)}, u32[]{:S(2)}) %all-to-all-start.3) | async-done | bytes 147488 | tf_op jit(solution)/shard_map/all_to_all | solution.py:301
  134.1 3.5 %all-to-all-start.4 = ((f32[4,256,128]{2,1,0:T(8,128)}), f32[4,256,128]{2,1,0:T(8,128)S(1)}, u32[]{:S(2)}, u32[]{:S(2)}) async-start(f32[4,256,128]{2,1,0:T(8,128)} %bitcast.3), calls=%async_computation.4 | async-start | bytes 1048576 | tf_op jit(solution)/shard_map/all_to_all | solution.py:296
  137.6 0.7 unpack.1
  138.3 8.6 %all-to-all-done.4 = f32[4,256,128]{2,1,0:T(8,128)S(1)} async-done(((f32[4,256,128]{2,1,0:T(8,128)}), f32[4,256,128]{2,1,0:T(8,128)S(1)}, u32[]{:S(2)}, u32[]{:S(2)}) %all-to-all-start.4) | async-done | bytes 524320 | tf_op jit(solution)/shard_map/all_to_all | solution.py:296
  146.9 0.7 reduce_sum.9
  (1 shorter events, 0.0 us)
Async XLA Ops:
  0.6 40.7 %copy-start.5 = (s32[4,16]{1,0:T(4,128)S(1)}, s32[4,16]{1,0:T(4,128)}, u32[]{:S(2)}) copy-start(s32[4,16]{1,0:T(4,128)} %param.8) | copy-start | bytes 772
  0.6 40.8 %copy-start.2 = (f32[128,256]{1,0:T(8,128)S(1)}, f32[128,256]{1,0:T(8,128)}, u32[]{:S(2)}) copy-start(f32[128,256]{1,0:T(8,128)} %weight.1) | copy-start | bytes 393220
  0.7 40.8 %copy-start = (f32[4,64,1024]{2,1,0:T(8,128)S(1)}, f32[4,64,1024]{2,1,0:T(8,128)}, u32[]{:S(2)}) copy-start(f32[4,64,1024]{2,1,0:T(8,128)} %blocks.1) | copy-start | bytes 3145732
  0.7 40.8 %copy-start.4 = (s32[4]{0:T(128)S(1)}, s32[4]{0:T(128)}, u32[]{:S(2)}) copy-start(s32[4]{0:T(128)} %counts.1) | copy-start | bytes 52
  0.7 42.6 %copy-start.1 = (f32[256,256]{1,0:T(8,128)S(1)}, f32[256,256]{1,0:T(8,128)}, u32[]{:S(2)}) copy-start(f32[256,256]{1,0:T(8,128)} %cotangent.1) | copy-start | bytes 786436
  0.7 42.6 %copy-start.3 = (f32[256]{0:T(256)S(1)}, f32[256]{0:T(256)}, u32[]{:S(2)}) copy-start(f32[256]{0:T(256)} %param.12) | copy-start | bytes 3076
  13.3 20.9 %collective-permute-start.3 = (f32[1024,128]{1,0:T(8,128)S(1)}, f32[1024,128]{1,0:T(8,128)S(1)}, u32[]{:S(2)}, u32[]{:S(2)}) collective-permute-start(f32[1024,128]{1,0:T(8,128)S(1)} %bitcast.4), channel_id=1, source_target_pairs={{8,0},{16,8},{24,16},{32,24},{40,32},{48,40},{56,48},{64,56},{72,6... | collective-permute-start | bytes 1572872 | tf_op jit(solution)/shard_map/ppermute | solution.py:256
  14.6 24.7 %collective-permute-start = (f32[1024,128]{1,0:T(8,128)S(1)}, f32[1024,128]{1,0:T(8,128)S(1)}, u32[]{:S(2)}, u32[]{:S(2)}) collective-permute-start(f32[1024,128]{1,0:T(8,128)S(1)} %bitcast.5), channel_id=1, source_target_pairs={{0,8},{8,16},{16,24},{24,32},{32,40},{40,48},{48,56},{56,64},{64,7... | collective-permute-start | bytes 1572872 | tf_op jit(solution)/shard_map/ppermute | solution.py:256
  20.5 21.9 %collective-permute-start.2 = (f32[1024,128]{1,0:T(8,128)S(1)}, f32[1024,128]{1,0:T(8,128)S(1)}, u32[]{:S(2)}, u32[]{:S(2)}) collective-permute-start(f32[1024,128]{1,0:T(8,128)S(1)} %bitcast.6), channel_id=1, source_target_pairs={{0,1},{1,0},{2,3},{3,2},{4,5},{5,4},{6,7},{7,6},{8,9},{9,8},{10,11... | collective-permute-start | bytes 1572872 | tf_op jit(solution)/shard_map/ppermute | solution.py:250
  34.2 8.2 %collective-permute-start.4 = (f32[1024,128]{1,0:T(8,128)S(1)}, f32[1024,128]{1,0:T(8,128)}, u32[]{:S(2)}, u32[]{:S(2)}) collective-permute-start(f32[1024,128]{1,0:T(8,128)S(1)} %collective-permute-done.3.p5), channel_id=1, source_target_pairs={{0,1},{1,0},{2,3},{3,2},{4,5},{5,4},{6,7},{7,6},{8,9},{9,8},{10,11... | collective-permute-start | bytes 1572872 | tf_op jit(solution)/shard_map/ppermute | solution.py:250
  39.4 3.9 %collective-permute-start.1 = (f32[1024,128]{1,0:T(8,128)S(1)}, f32[1024,128]{1,0:T(8,128)}, u32[]{:S(2)}, u32[]{:S(2)}) collective-permute-start(f32[1024,128]{1,0:T(8,128)S(1)} %collective-permute-done.p3), channel_id=1, source_target_pairs={{0,1},{1,0},{2,3},{3,2},{4,5},{5,4},{6,7},{7,6},{8,9},{9,8},{10,11... | collective-permute-start | bytes 1572872 | tf_op jit(solution)/shard_map/ppermute | solution.py:250
  48.7 39.1 %collective-permute-start.5 = (f32[3072,128]{1,0:T(8,128)S(1)}, f32[3072,128]{1,0:T(8,128)}, u32[]{:S(2)}, u32[]{:S(2)}) collective-permute-start(f32[3072,128]{1,0:T(8,128)S(1)} %get-tuple-element.29), channel_id=1, source_target_pairs={{0,1},{1,0},{2,3},{3,2},{4,5},{5,4},{6,7},{7,6},{8,9},{9,8},{10,11... | collective-permute-start | bytes 4718600 | tf_op jit(solution)/shard_map/ppermute | solution.py:250
  76.7 42.4 %all-to-all-start.2 = ((f32[32,1,1152]{2,1,0:T(1,128)}), f32[32,1,1152]{2,1,0:T(1,128)S(1)}, u32[]{:S(2)}, u32[]{:S(2)}) async-start(f32[32,1,1152]{2,1,0:T(1,128)} %sum_for_all.2), calls=%async_computation.2 | async-start | bytes 294912 | tf_op jit(solution)/shard_map/all_to_all | solution.py:300
  89.1 37.1 %collective-permute-start.6 = (f32[1024,128]{1,0:T(8,128)S(1)}, f32[1024,128]{1,0:T(8,128)S(1)}, u32[]{:S(2)}, u32[]{:S(2)}) collective-permute-start(f32[1024,128]{1,0:T(8,128)S(1)} %get-tuple-element.32), channel_id=1, source_target_pairs={{8,0},{16,8},{24,16},{32,24},{40,32},{48,40},{56,48},{64,56},{72,6... | collective-permute-start | bytes 1572872 | tf_op jit(solution)/shard_map/ppermute | solution.py:256
  90.4 35.9 %collective-permute-start.7 = (f32[1024,128]{1,0:T(8,128)S(1)}, f32[1024,128]{1,0:T(8,128)S(1)}, u32[]{:S(2)}, u32[]{:S(2)}) collective-permute-start(f32[1024,128]{1,0:T(8,128)S(1)} %get-tuple-element.33), channel_id=1, source_target_pairs={{0,8},{8,16},{16,24},{24,32},{32,40},{40,48},{48,56},{56,64},{64,7... | collective-permute-start | bytes 1572872 | tf_op jit(solution)/shard_map/ppermute | solution.py:256
  119.9 14.3 %all-to-all-start.3 = ((f32[32,1,1152]{2,1,0:T(1,128)}), f32[32,1,1152]{2,1,0:T(1,128)S(1)}, u32[]{:S(2)}, u32[]{:S(2)}) async-start(f32[32,1,1152]{2,1,0:T(1,128)} %sum_for_all.3), calls=%async_computation.3 | async-start | bytes 294912 | tf_op jit(solution)/shard_map/all_to_all | solution.py:301
  134.1 12.7 %all-to-all-start.4 = ((f32[4,256,128]{2,1,0:T(8,128)}), f32[4,256,128]{2,1,0:T(8,128)S(1)}, u32[]{:S(2)}, u32[]{:S(2)}) async-start(f32[4,256,128]{2,1,0:T(8,128)} %bitcast.3), calls=%async_computation.4 | async-start | bytes 1048576 | tf_op jit(solution)/shard_map/all_to_all | solution.py:296

commit v2 on v1

--- a/solution.py
+++ b/solution.py
@@ -10,9 +10,9 @@
 BLK = 64
 LANES = 128
 VMEM_LIMIT = 40 * 1024 * 1024
-PLANE = ("y", "x", "core")
-WIDE = ("y", "z")
-ALL = ("y", "z", "x", "core")
+WIDE = ("y", "far", "near")
+ALL = ("y", "far", "near", "x", "core")
+GROUP = ("y", "near", "x", "core")
 C0 = math.sqrt(2.0 / math.pi)
 C1 = 0.044715
 
@@ -164,22 +164,21 @@
     )(places, stacked, *pieces, weight_rows, weight_low, weight_turned, bias, cotangent)
 
 
-def spread_kernel(places, turned, grads, other, before, own, after, band, sems):
+def spread_kernel(targets, turned, grads, other, mine, band, sems):
     rows, width, _ = turned.shape
     slots = width // BLK
-    depth = band.shape[1]
-    span = before.shape[0]
+    half, depth = mine.shape
     band[...] = jnp.zeros_like(band)
     for r in range(rows):
         product = dot(turned[r], grads[r])
         product = product[:, :depth] + product[:, depth:]
         for k in range(slots):
-            start = pl.multiple_of(places[r * slots + k] * BLK, BLK)
+            start = pl.multiple_of(targets[r * slots + k] * BLK, BLK)
             where = pl.ds(start, BLK)
             band[where, :] = band[where, :] + product[k * BLK:(k + 1) * BLK]
-    copies = [pltpu.make_async_copy(band.at[pl.ds(0, 3 * span)], other, sems.at[0])] + [
-        pltpu.make_async_copy(band.at[pl.ds((3 + i) * span, span)], piece, sems.at[1 + i])
-        for i, piece in enumerate((before, own, after))
+    copies = [
+        pltpu.make_async_copy(band.at[pl.ds(i * half, half)], piece, sems.at[i])
+        for i, piece in enumerate((other, mine))
     ]
     for copy in copies:
         copy.start()
@@ -187,21 +186,21 @@
         copy.wait()
 
 
-def spread(places, turned, grads, span, depth):
-    piece = jax.ShapeDtypeStruct((span, depth), jnp.float32)
+def spread(targets, turned, grads, half, depth):
+    piece = jax.ShapeDtypeStruct((half, depth), jnp.float32)
     return pl.pallas_call(
         spread_kernel,
-        out_shape=(jax.ShapeDtypeStruct((3 * span, depth), jnp.float32), piece, piece, piece),
+        out_shape=(piece, piece),
         in_specs=[pl.BlockSpec(memory_space=pltpu.SMEM)] + vmem(2),
-        out_specs=[pl.BlockSpec(memory_space=pl.ANY)] * 4,
+        out_specs=[pl.BlockSpec(memory_space=pl.ANY)] * 2,
         scratch_shapes=[
-            pltpu.VMEM((6 * span, depth), jnp.float32),
-            pltpu.SemaphoreType.DMA((4,)),
+            pltpu.VMEM((2 * half, depth), jnp.float32),
+            pltpu.SemaphoreType.DMA((2,)),
         ],
         compiler_params=params(),
         cost_estimate=pl.CostEstimate(flops=300_000_000, bytes_accessed=5_000_000, transcendentals=0),
         name="spread",
-    )(places, turned, grads)
+    )(targets, turned, grads)
 
 
 def sum_kernel(parts, out):
@@ -261,8 +260,8 @@
     hid = weight.shape[1]
     chips = lax.axis_size("x")
     cores = lax.axis_size("core")
-    shards = lax.axis_size(PLANE)
-    levels = lax.axis_size("z")
+    shards = lax.axis_size(GROUP)
+    levels = lax.axis_size("far")
     block_rows = columns.shape[0]
     stripe = block_rows * chips * cores
     span = chips * rows
@@ -271,9 +270,11 @@
     part = local // stripe
     within = local % stripe
     device = within // block_rows
-    foreign = (device % cores) ^ lax.axis_index("core")
-    piece = (1 - foreign) * 3 + part
-    places = (piece * (chips * block_rows) + (device // cores) * block_rows + within % block_rows).reshape(-1)
+    block = within % block_rows
+    chip = device // cores
+    mine = 1 - ((device % cores) ^ lax.axis_index("core"))
+    places = (((mine * 3 + part) * chips + chip) * block_rows + block).reshape(-1)
+    targets = (((mine * chips + chip) * 3 + part) * block_rows + block).reshape(-1)
 
     row_of_chips = jnp.broadcast_to(features[None], (chips, rows, depth))
     own = lax.all_to_all(row_of_chips, "x", 0, 0).reshape(span, depth)
@@ -288,25 +289,24 @@
         places, stacked, pieces, weight_rows, weight_low, weight_turned, bias[None], cotangent, shards
     )
 
-    other, to_before, to_own, to_after = spread(places, turned, grads, span, depth)
-    from_core = swap_cores(other)
-    from_after = along_wide(to_before + from_core[:span], -1)
-    from_before = along_wide(to_after + from_core[2 * span:], 1)
-    total = to_own + from_core[span:2 * span] + from_after + from_before
-    shares = lax.all_to_all(total.reshape(chips, rows, depth), "x", 0, 0)
-    feature_grad = jnp.sum(shares, axis=0)
-
-    scattered = lax.all_to_all(sums, PLANE, 0, 0)
-    scattered = lax.all_to_all(sum_for_all(scattered, levels), "z", 0, 0)
-    gathered = lax.all_to_all(sum_for_all(scattered, shards), PLANE, 0, 0)
+    scattered = lax.all_to_all(sums, GROUP, 0, 0)
+    scattered = lax.all_to_all(sum_for_all(scattered, levels), "far", 0, 0)
+    gathered = lax.all_to_all(sum_for_all(scattered, shards), GROUP, 0, 0)
     weight_grad, bias_grad = unpack(gathered, depth, hid)
+
+    to_other, to_mine = spread(targets, turned, grads, 3 * span, depth)
+    total = to_mine + swap_cores(to_other)
+    share = lax.psum_scatter(total, "x", scatter_dimension=0, tiled=True)
+    from_after = along_wide(share[:rows], -1)
+    from_before = along_wide(share[2 * rows:], 1)
+    feature_grad = share[rows:2 * rows] + from_after + from_before
     return (hidden, weight_grad, bias_grad.reshape(hid), feature_grad)
 
 
 def solution(mesh):
     wide, narrow = mesh.devices.shape
     levels = 32 if wide % 32 == 0 else wide // 2
-    fine = Mesh(mesh.devices.reshape(wide // levels, levels, narrow // 2, 2), ALL)
+    fine = Mesh(mesh.devices.reshape(wide // levels, levels // 2, 2, narrow // 2, 2), ALL)
     nodes = P(ALL, None)
     return jax.shard_map(
         body,

time: 148 us -> 150 us (1.014)
  the two profiles are of different devices: /device:TPU:1 before, /device:TPU:24 now
where the time goes in v2:
time: 150 us; the launch traced here: 149 us
  blocking collectives  59.4 us (40%)
  starting transfers between devices  41.4 us (28%)
  waiting for transfers between devices  20.1 us (13%)
  between operations  14.3 us (10%)
  Pallas kernels  7.79 us (5%)
  other arithmetic  3.52 us (2%)
  local copies, waits for them, and re-layouts  2.9 us (2%)
    all_to_all x1, blocking collectives, body(): scattered = lax.all_to_all(sum_for_all(scattered, levels), 'far', 0, 0)  33.3 us
    ppermute x4, starting transfers between devices, along_wide(): return lax.ppermute(value, WIDE, route)  26.6 us
    ppermute x4, waiting for transfers between devices, along_wide(): return lax.ppermute(value, WIDE, route)  17.1 us
    all_to_all x1, blocking collectives, body(): own = lax.all_to_all(row_of_chips, 'x', 0, 0).reshape(span, depth)  13.6 us
    all_to_all x1, blocking collectives, body(): scattered = lax.all_to_all(sums, GROUP, 0, 0)  12.5 us
    ppermute x4, starting transfers between devices, swap_cores(): return lax.ppermute(value, 'core', [(0, 1), (1, 0)])  8.14 us
    all_to_all x1, starting transfers between devices, body(): gathered = lax.all_to_all(sum_for_all(scattered, shards), GROUP, 0, 0)  6.57 us
    pallas_call x1, Pallas kernels, layer(): pl.pallas_call(layer_kernel, out_shape=(jax.ShapeDtypeStruct((count, hid)...  3.66 us
  transfers between devices with their start and end apart: 10, of which 5 were waited for; matrix products, arithmetic and copies ran while one was open for 2% of the time, Pallas kernels for 2%

profile of v2, /device:TPU:24, one launch (start us, length us, event | category | flops | bytes accessed | tf_op | source)
XLA Modules:
  0.0 149.3 jit_solution(7086314894604798574)
XLA Ops:
  7.2 0.0 copy-start.5
  7.2 0.0 copy-start.2
  7.2 0.0 copy-start
  7.2 0.0 copy-start.4
  7.2 0.0 copy-start.1
  7.2 0.0 copy-start.3
  7.2 0.0 reduce-scatter.2.cloned.1.call-start
  7.3 1.0 broadcast_in_dim.4
  8.3 13.6 %all_to_all.20 = f32[4,256,128]{2,1,0:T(8,128)S(1)} all-to-all(f32[4,256,128]{2,1,0:T(8,128)S(1)} %broadcast_in_dim.4), channel_id=1, replica_groups=mesh['y'=4,'far'=16,'near'=2,'x'=4,'core'=2] {'x'}, dimensions={0} | all-to-all | bytes 1048576 | tf_op jit(solution)/shard_map/all_to_all | solution.py:280
  21.9 18.8 %collective-permute-start.3 = (f32[1024,128]{1,0:T(8,128)S(1)}, f32[1024,128]{1,0:T(8,128)S(1)}, u32[]{:S(2)}, u32[]{:S(2)}) collective-permute-start(f32[1024,128]{1,0:T(8,128)S(1)} %bitcast.3), channel_id=1, source_target_pairs={{8,0},{16,8},{24,16},{32,24},{40,32},{48,40},{56,48},{64,56},{72,6... | collective-permute-start | bytes 1572872 | tf_op jit(solution)/shard_map/ppermute | solution.py:255
  40.7 1.9 %collective-permute-start = (f32[1024,128]{1,0:T(8,128)S(1)}, f32[1024,128]{1,0:T(8,128)S(1)}, u32[]{:S(2)}, u32[]{:S(2)}) collective-permute-start(f32[1024,128]{1,0:T(8,128)S(1)} %bitcast.4), channel_id=1, source_target_pairs={{0,8},{8,16},{16,24},{24,32},{32,40},{40,48},{48,56},{56,64},{64,7... | collective-permute-start | bytes 1572872 | tf_op jit(solution)/shard_map/ppermute | solution.py:255
  42.7 1.9 %collective-permute-start.2 = (f32[1024,128]{1,0:T(8,128)S(1)}, f32[1024,128]{1,0:T(8,128)S(1)}, u32[]{:S(2)}, u32[]{:S(2)}) collective-permute-start(f32[1024,128]{1,0:T(8,128)S(1)} %bitcast.5), channel_id=1, source_target_pairs={{0,1},{1,0},{2,3},{3,2},{4,5},{5,4},{6,7},{7,6},{8,9},{9,8},{10,11... | collective-permute-start | bytes 1572872 | tf_op jit(solution)/shard_map/ppermute | solution.py:249
  44.6 6.1 %collective-permute-done.3.p5 = f32[1024,128]{1,0:T(8,128)S(1)} collective-permute-done((f32[1024,128]{1,0:T(8,128)S(1)}, f32[1024,128]{1,0:T(8,128)S(1)}, u32[]{:S(2)}, u32[]{:S(2)}) %collective-permute-start.3) | collective-permute-done | bytes 524320 | tf_op jit(solution)/shard_map/ppermute | solution.py:255
  50.7 1.9 %collective-permute-start.4 = (f32[1024,128]{1,0:T(8,128)S(1)}, f32[1024,128]{1,0:T(8,128)}, u32[]{:S(2)}, u32[]{:S(2)}) collective-permute-start(f32[1024,128]{1,0:T(8,128)S(1)} %collective-permute-done.3.p5), channel_id=1, source_target_pairs={{0,1},{1,0},{2,3},{3,2},{4,5},{5,4},{6,7},{7,6},{8,9},{9,8},{10,11... | collective-permute-start | bytes 1572872 | tf_op jit(solution)/shard_map/ppermute | solution.py:249
  52.6 4.3 %collective-permute-done.p3 = f32[1024,128]{1,0:T(8,128)S(1)} collective-permute-done((f32[1024,128]{1,0:T(8,128)S(1)}, f32[1024,128]{1,0:T(8,128)S(1)}, u32[]{:S(2)}, u32[]{:S(2)}) %collective-permute-start) | collective-permute-done | bytes 524320 | tf_op jit(solution)/shard_map/ppermute | solution.py:255
  56.9 1.9 %collective-permute-start.1 = (f32[1024,128]{1,0:T(8,128)S(1)}, f32[1024,128]{1,0:T(8,128)}, u32[]{:S(2)}, u32[]{:S(2)}) collective-permute-start(f32[1024,128]{1,0:T(8,128)S(1)} %collective-permute-done.p3), channel_id=1, source_target_pairs={{0,1},{1,0},{2,3},{3,2},{4,5},{5,4},{6,7},{7,6},{8,9},{9,8},{10,11... | collective-permute-start | bytes 1572872 | tf_op jit(solution)/shard_map/ppermute | solution.py:249
  58.9 0.0 copy-done.5
  58.9 0.6 multiply_add_fusion
  59.5 0.1 reshape.24.targets
  59.6 0.8 reshape.21.places
  60.3 0.0 copy-done.2
  60.3 0.0 copy-done
  60.3 0.0 copy-done.4
  60.3 0.9 prepare.1
  61.3 0.0 collective-permute-done.2.p1
  61.3 0.0 collective-permute-done.4.p2
  61.3 0.0 collective-permute-done.1.p0
  61.3 0.0 copy-done.1
  61.3 0.0 copy-done.3
  61.3 3.7 %layer.1 = (f32[256,256]{1,0:T(8,128)}, f32[64,1,640]{2,1,0:T(1,128)S(1)}, bf16[4,128,256]{2,1,0:T(8,128)(2,1)S(1)}) custom-call(s32[64]{0:T(128)S(1)} %reshape.21.places, bf16[4,128,1024]{2,1,0:T(8,128)(2,1)S(1)} %get-tuple-element.16.stacked, f32[1024,128]{1,0:T(8,128)} %collective-permute-done.1.p0, f32[1024,128]{1,0:T(8,128)S(1)} %collective-permute-done.2.p1, ...), custom_call_target="tpu_custom_call" | custom-call | flops 400000000 | bytes 6000000 | tf_op jit(solution)/shard_map/layer/pallas_call | solution.py:145
  65.0 1.7 %spread.1 = (f32[3072,128]{1,0:T(8,128)S(1)}, f32[3072,128]{1,0:T(8,128)S(1)}) custom-call(s32[64]{0:T(128)S(1)} %reshape.24.targets, bf16[4,1024,128]{2,1,0:T(8,128)(2,1)S(1)} %get-tuple-element.24.turned, bf16[4,128,256]{2,1,0:T(8,128)(2,1)S(1)} %get-tuple-element.25.grads), custom_call_target="tpu_custom_call" | custom-call | flops 300000000 | bytes 5000000 | tf_op jit(solution)/shard_map/spread/pallas_call | solution.py:191
  66.7 2.4 %collective-permute-start.5 = (f32[3072,128]{1,0:T(8,128)S(1)}, f32[3072,128]{1,0:T(8,128)S(1)}, u32[]{:S(2)}, u32[]{:S(2)}) collective-permute-start(f32[3072,128]{1,0:T(8,128)S(1)} %get-tuple-element.27), channel_id=1, source_target_pairs={{0,1},{1,0},{2,3},{3,2},{4,5},{5,4},{6,7},{7,6},{8,9},{9,8},{10,11... | collective-permute-start | bytes 4718600 | tf_op jit(solution)/shard_map/ppermute | solution.py:249
  69.1 3.0 %collective-permute-done.5 = f32[3072,128]{1,0:T(8,128)S(1)} collective-permute-done((f32[3072,128]{1,0:T(8,128)S(1)}, f32[3072,128]{1,0:T(8,128)S(1)}, u32[]{:S(2)}, u32[]{:S(2)}) %collective-permute-start.5) | collective-permute-done | bytes 1572896 | tf_op jit(solution)/shard_map/ppermute | solution.py:249
  72.1 1.3 add.64
  73.4 0.0 reduce-scatter.2.cloned.1.call-update
  73.5 12.5 %all_to_all.21.parts = f32[64,1,640]{2,1,0:T(1,128)S(1)} all-to-all(f32[64,1,640]{2,1,0:T(1,128)S(1)} %get-tuple-element.21), channel_id=1, replica_groups=mesh['y'=4,'far'=16,'near'=2,'x'=4,'core'=2] {'y','near','x','core'}, dimensions={0} | all-to-all | bytes 327680 | tf_op jit(solution)/shard_map/all_to_all | solution.py:292
  86.0 0.1 sum_for_all.2
  86.1 33.3 %all_to_all.22.parts = f32[16,1,640]{2,1,0:T(1,128)S(1)} all-to-all(f32[16,1,640]{2,1,0:T(1,128)S(1)} %sum_for_all.2), channel_id=1, replica_groups=mesh['y'=4,'far'=16,'near'=2,'x'=4,'core'=2] {'far'}, dimensions={0} | all-to-all | bytes 81920 | tf_op jit(solution)/shard_map/all_to_all | solution.py:293
  119.4 0.7 sum_for_all.3
  120.1 6.6 %all-to-all-start.3 = ((f32[64,1,640]{2,1,0:T(1,128)}), f32[64,1,640]{2,1,0:T(1,128)S(1)}, u32[]{:S(2)}, u32[]{:S(2)}) async-start(f32[64,1,640]{2,1,0:T(1,128)} %sum_for_all.3), calls=%async_computation.3 | async-start | bytes 327680 | tf_op jit(solution)/shard_map/all_to_all | solution.py:294
  126.7 0.0 reduce-scatter.2.cloned.1.call-done
  126.7 1.0 fusion.6
  127.7 3.9 %collective-permute-start.6 = (f32[256,128]{1,0:T(8,128)S(1)}, f32[256,128]{1,0:T(8,128)S(1)}, u32[]{:S(2)}, u32[]{:S(2)}) collective-permute-start(f32[256,128]{1,0:T(8,128)S(1)} %get-tuple-element.28), channel_id=1, source_target_pairs={{8,0},{16,8},{24,16},{32,24},{40,32},{48,40},{56,48},{64,56},{72,6... | collective-permute-start | bytes 393224 | tf_op jit(solution)/shard_map/ppermute | solution.py:255
  131.6 1.9 %collective-permute-start.7 = (f32[256,128]{1,0:T(8,128)S(1)}, f32[256,128]{1,0:T(8,128)S(1)}, u32[]{:S(2)}, u32[]{:S(2)}) collective-permute-start(f32[256,128]{1,0:T(8,128)S(1)} %get-tuple-element.29), channel_id=1, source_target_pairs={{0,8},{8,16},{16,24},{24,32},{32,40},{40,48},{48,56},{56,64},{64,7... | collective-permute-start | bytes 393224 | tf_op jit(solution)/shard_map/ppermute | solution.py:255
  133.6 0.0 all-to-all-done.3.parts
  133.6 0.7 unpack.1
  134.2 0.9 collective-permute-done.6
  135.1 5.7 %collective-permute-done.7 = f32[256,128]{1,0:T(8,128)S(1)} collective-permute-done((f32[256,128]{1,0:T(8,128)S(1)}, f32[256,128]{1,0:T(8,128)S(1)}, u32[]{:S(2)}, u32[]{:S(2)}) %collective-permute-start.7) | collective-permute-done | bytes 131104 | tf_op jit(solution)/shard_map/ppermute | solution.py:255
  140.9 1.6 %fusion = f32[256,128]{1,0:T(8,128)} fusion(f32[256,128]{1,0:T(8,128)S(1)} %collective-permute-done.7, f32[256,128]{1,0:T(8,128)S(1)} %collective-permute-done.6, f32[768,128]{1,0:T(8,128)} %reduce-scatter.2.cloned.1.call-done), kind=kLoop, calls=%fused_computation.1 | loop fusion | flops 65536 | bytes 524288 | tf_op jit(solution)/shard_map/add | solution.py:302
Async XLA Ops:
  7.2 51.7 %copy-start.5 = (s32[4,16]{1,0:T(4,128)S(1)}, s32[4,16]{1,0:T(4,128)}, u32[]{:S(2)}) copy-start(s32[4,16]{1,0:T(4,128)} %param.8) | copy-start | bytes 772
  7.2 53.2 %copy-start.2 = (f32[128,256]{1,0:T(8,128)S(1)}, f32[128,256]{1,0:T(8,128)}, u32[]{:S(2)}) copy-start(f32[128,256]{1,0:T(8,128)} %weight.1) | copy-start | bytes 393220
  7.2 53.2 %copy-start = (f32[4,64,1024]{2,1,0:T(8,128)S(1)}, f32[4,64,1024]{2,1,0:T(8,128)}, u32[]{:S(2)}) copy-start(f32[4,64,1024]{2,1,0:T(8,128)} %blocks.1) | copy-start | bytes 3145732
  7.2 53.1 %copy-start.4 = (s32[4]{0:T(128)S(1)}, s32[4]{0:T(128)}, u32[]{:S(2)}) copy-start(s32[4]{0:T(128)} %counts.1) | copy-start | bytes 52
  7.2 54.1 %copy-start.1 = (f32[256,256]{1,0:T(8,128)S(1)}, f32[256,256]{1,0:T(8,128)}, u32[]{:S(2)}) copy-start(f32[256,256]{1,0:T(8,128)} %cotangent.1) | copy-start | bytes 786436
  7.2 54.1 %copy-start.3 = (f32[256]{0:T(256)S(1)}, f32[256]{0:T(256)}, u32[]{:S(2)}) copy-start(f32[256]{0:T(256)} %param.12) | copy-start | bytes 3076
  7.2 119.5 %reduce-scatter.2.cloned.1.call-start = ((), (), s32[]{:S(2)}) async-start(), calls=%async_computation.5 | async-start | bytes 1966080 | tf_op jit(solution)/shard_map/reduce_scatter | solution.py:299
  21.9 28.8 %collective-permute-start.3 = (f32[1024,128]{1,0:T(8,128)S(1)}, f32[1024,128]{1,0:T(8,128)S(1)}, u32[]{:S(2)}, u32[]{:S(2)}) collective-permute-start(f32[1024,128]{1,0:T(8,128)S(1)} %bitcast.3), channel_id=1, source_target_pairs={{8,0},{16,8},{24,16},{32,24},{40,32},{48,40},{56,48},{64,56},{72,6... | collective-permute-start | bytes 1572872 | tf_op jit(solution)/shard_map/ppermute | solution.py:255
  40.7 16.2 %collective-permute-start = (f32[1024,128]{1,0:T(8,128)S(1)}, f32[1024,128]{1,0:T(8,128)S(1)}, u32[]{:S(2)}, u32[]{:S(2)}) collective-permute-start(f32[1024,128]{1,0:T(8,128)S(1)} %bitcast.4), channel_id=1, source_target_pairs={{0,8},{8,16},{16,24},{24,32},{32,40},{40,48},{48,56},{56,64},{64,7... | collective-permute-start | bytes 1572872 | tf_op jit(solution)/shard_map/ppermute | solution.py:255
  42.7 18.6 %collective-permute-start.2 = (f32[1024,128]{1,0:T(8,128)S(1)}, f32[1024,128]{1,0:T(8,128)S(1)}, u32[]{:S(2)}, u32[]{:S(2)}) collective-permute-start(f32[1024,128]{1,0:T(8,128)S(1)} %bitcast.5), channel_id=1, source_target_pairs={{0,1},{1,0},{2,3},{3,2},{4,5},{5,4},{6,7},{7,6},{8,9},{9,8},{10,11... | collective-permute-start | bytes 1572872 | tf_op jit(solution)/shard_map/ppermute | solution.py:249
  50.7 10.6 %collective-permute-start.4 = (f32[1024,128]{1,0:T(8,128)S(1)}, f32[1024,128]{1,0:T(8,128)}, u32[]{:S(2)}, u32[]{:S(2)}) collective-permute-start(f32[1024,128]{1,0:T(8,128)S(1)} %collective-permute-done.3.p5), channel_id=1, source_target_pairs={{0,1},{1,0},{2,3},{3,2},{4,5},{5,4},{6,7},{7,6},{8,9},{9,8},{10,11... | collective-permute-start | bytes 1572872 | tf_op jit(solution)/shard_map/ppermute | solution.py:249
  56.9 4.4 %collective-permute-start.1 = (f32[1024,128]{1,0:T(8,128)S(1)}, f32[1024,128]{1,0:T(8,128)}, u32[]{:S(2)}, u32[]{:S(2)}) collective-permute-start(f32[1024,128]{1,0:T(8,128)S(1)} %collective-permute-done.p3), channel_id=1, source_target_pairs={{0,1},{1,0},{2,3},{3,2},{4,5},{5,4},{6,7},{7,6},{8,9},{9,8},{10,11... | collective-permute-start | bytes 1572872 | tf_op jit(solution)/shard_map/ppermute | solution.py:249
  66.7 5.4 %collective-permute-start.5 = (f32[3072,128]{1,0:T(8,128)S(1)}, f32[3072,128]{1,0:T(8,128)S(1)}, u32[]{:S(2)}, u32[]{:S(2)}) collective-permute-start(f32[3072,128]{1,0:T(8,128)S(1)} %get-tuple-element.27), channel_id=1, source_target_pairs={{0,1},{1,0},{2,3},{3,2},{4,5},{5,4},{6,7},{7,6},{8,9},{9,8},{10,11... | collective-permute-start | bytes 4718600 | tf_op jit(solution)/shard_map/ppermute | solution.py:249
  120.1 13.5 %all-to-all-start.3 = ((f32[64,1,640]{2,1,0:T(1,128)}), f32[64,1,640]{2,1,0:T(1,128)S(1)}, u32[]{:S(2)}, u32[]{:S(2)}) async-start(f32[64,1,640]{2,1,0:T(1,128)} %sum_for_all.3), calls=%async_computation.3 | async-start | bytes 327680 | tf_op jit(solution)/shard_map/all_to_all | solution.py:294
  127.7 7.4 %collective-permute-start.6 = (f32[256,128]{1,0:T(8,128)S(1)}, f32[256,128]{1,0:T(8,128)S(1)}, u32[]{:S(2)}, u32[]{:S(2)}) collective-permute-start(f32[256,128]{1,0:T(8,128)S(1)} %get-tuple-element.28), channel_id=1, source_target_pairs={{8,0},{16,8},{24,16},{32,24},{40,32},{48,40},{56,48},{64,56},{72,6... | collective-permute-start | bytes 393224 | tf_op jit(solution)/shard_map/ppermute | solution.py:255
  131.6 9.3 %collective-permute-start.7 = (f32[256,128]{1,0:T(8,128)S(1)}, f32[256,128]{1,0:T(8,128)S(1)}, u32[]{:S(2)}, u32[]{:S(2)}) collective-permute-start(f32[256,128]{1,0:T(8,128)S(1)} %get-tuple-element.29), channel_id=1, source_target_pairs={{0,8},{8,16},{16,24},{24,32},{32,40},{40,48},{48,56},{56,64},{64,7... | collective-permute-start | bytes 393224 | tf_op jit(solution)/shard_map/ppermute | solution.py:255
Sparse Core Ops, SparseCore 0:
  73.6 31.3 reduce-scatter.1

commit v3 on v2

--- a/solution.py
+++ b/solution.py
@@ -203,19 +203,20 @@
     )(targets, turned, grads)
 
 
-def sum_kernel(parts, out):
+def sum_kernel(parts, *refs):
+    out = refs[-1]
     out[...] = jnp.broadcast_to(jnp.sum(parts[...], axis=0, keepdims=True), out.shape)
 
 
-def sum_for_all(parts, shards):
+def sum_for_all(parts, shards, *behind):
     return pl.pallas_call(
         sum_kernel,
         out_shape=jax.ShapeDtypeStruct((shards,) + parts.shape[1:], parts.dtype),
-        in_specs=vmem(1),
+        in_specs=vmem(1) + [pl.BlockSpec(memory_space=pl.ANY)] * len(behind),
         out_specs=pl.BlockSpec(memory_space=pltpu.VMEM),
         compiler_params=params(),
         name="sum_for_all",
-    )(parts)
+    )(parts, *behind)
 
 
 def unpack_kernel(parts, outer, total):
@@ -274,7 +275,8 @@
     chip = device // cores
     mine = 1 - ((device % cores) ^ lax.axis_index("core"))
     places = (((mine * 3 + part) * chips + chip) * block_rows + block).reshape(-1)
-    targets = (((mine * chips + chip) * 3 + part) * block_rows + block).reshape(-1)
+    ahead = lax.rem(chip - lax.axis_index("x") + chips, chips)
+    targets = (((mine * 3 + part) * chips + ahead) * block_rows + block).reshape(-1)
 
     row_of_chips = jnp.broadcast_to(features[None], (chips, rows, depth))
     own = lax.all_to_all(row_of_chips, "x", 0, 0).reshape(span, depth)
@@ -289,17 +291,24 @@
         places, stacked, pieces, weight_rows, weight_low, weight_turned, bias[None], cotangent, shards
     )
 
+    to_other, to_mine = spread(targets, turned, grads, 3 * span, depth)
+    from_core = swap_cores(to_other)
+    from_after = along_wide(to_mine[:span] + from_core[:span], -1)
+    from_before = along_wide(to_mine[2 * span:] + from_core[2 * span:], 1)
+    shares = []
+    for step in range(chips):
+        chunk = slice(rows * step, rows * (step + 1))
+        at = slice(span + rows * step, span + rows * (step + 1))
+        share = to_mine[at] + from_core[at] + from_after[chunk] + from_before[chunk]
+        if step:
+            share = lax.ppermute(share, "x", [(i, (i + step) % chips) for i in range(chips)])
+        shares.append(share)
+    feature_grad = sum(shares[1:], shares[0])
     scattered = lax.all_to_all(sums, GROUP, 0, 0)
     scattered = lax.all_to_all(sum_for_all(scattered, levels), "far", 0, 0)
-    gathered = lax.all_to_all(sum_for_all(scattered, shards), GROUP, 0, 0)
+    gathered = lax.all_to_all(sum_for_all(scattered, shards, *shares[1::2]), GROUP, 0, 0)
     weight_grad, bias_grad = unpack(gathered, depth, hid)
 
-    to_other, to_mine = spread(targets, turned, grads, 3 * span, depth)
-    total = to_mine + swap_cores(to_other)
-    share = lax.psum_scatter(total, "x", scatter_dimension=0, tiled=True)
-    from_after = along_wide(share[:rows], -1)
-    from_before = along_wide(share[2 * rows:], 1)
-    feature_grad = share[rows:2 * rows] + from_after + from_before
     return (hidden, weight_grad, bias_grad.reshape(hid), feature_grad)
 
 

time: 150 us -> 134 us (0.89)
  the two profiles are of different devices: /device:TPU:24 before, /device:TPU:1 now
where the time goes in v3:
time: 134 us; the launch traced here: 133 us
  starting transfers between devices  84.5 us (63%)
  waiting for transfers between devices  19.7 us (15%)
  blocking collectives  11.6 us (9%)
  Pallas kernels  8.6 us (6%)
  other arithmetic  6.18 us (5%)
  local copies, waits for them, and re-layouts  1.92 us (1%)
    ppermute x4, starting transfers between devices, swap_cores(): return lax.ppermute(value, 'core', [(0, 1), (1, 0)])  23.2 us
    all_to_all x1, starting transfers between devices, body(): scattered = lax.all_to_all(sums, GROUP, 0, 0)  18 us
    all_to_all x1, waiting for transfers between devices, body(): scattered = lax.all_to_all(sum_for_all(scattered, levels), 'far', 0, 0)  14.6 us
    ppermute x4, starting transfers between devices, along_wide(): return lax.ppermute(value, WIDE, route)  13.2 us
    all_to_all x1, blocking collectives, body(): own = lax.all_to_all(row_of_chips, 'x', 0, 0).reshape(span, depth)  11.6 us
    all_to_all x1, starting transfers between devices, body(): scattered = lax.all_to_all(sum_for_all(scattered, levels), 'far', 0, 0)  10.8 us
    ppermute x3, starting transfers between devices, body(): lax.ppermute(share, 'x', [(i, (i + step) % chips) for i in range(chips)])  10.1 us
    all_to_all x1, starting transfers between devices, body(): lax.all_to_all(sum_for_all(scattered, shards, *shares[1::2]), GROUP, 0, 0)  9.28 us
  transfers between devices with their start and end apart: 14, of which 3 were waited for; matrix products, arithmetic and copies ran while one was open for 5% of the time, Pallas kernels for 1%

profile of v3, /device:TPU:1, one launch (start us, length us, event | category | flops | bytes accessed | tf_op | source)
XLA Modules:
  0.0 133.5 jit_solution(17248901016691453606)
XLA Ops:
  0.6 0.0 copy-start.5
  0.6 0.0 copy-start.2
  0.7 0.0 copy-start
  0.7 0.0 copy-start.4
  0.7 0.0 copy-start.1
  0.7 0.0 copy-start.3
  0.7 1.0 broadcast_in_dim.4
  1.7 11.6 %all_to_all.20 = f32[4,256,128]{2,1,0:T(8,128)S(1)} all-to-all(f32[4,256,128]{2,1,0:T(8,128)S(1)} %broadcast_in_dim.4), channel_id=1, replica_groups=mesh['y'=4,'far'=16,'near'=2,'x'=4,'core'=2] {'x'}, dimensions={0} | all-to-all | bytes 1048576 | tf_op jit(solution)/shard_map/all_to_all | solution.py:282
  13.3 1.3 collective-permute-start.3
  14.6 5.8 %collective-permute-start = (f32[1024,128]{1,0:T(8,128)S(1)}, f32[1024,128]{1,0:T(8,128)S(1)}, u32[]{:S(2)}, u32[]{:S(2)}) collective-permute-start(f32[1024,128]{1,0:T(8,128)S(1)} %bitcast.4), channel_id=1, source_target_pairs={{0,8},{8,16},{16,24},{24,32},{32,40},{40,48},{48,56},{56,64},{64,7... | collective-permute-start | bytes 1572872 | tf_op jit(solution)/shard_map/ppermute | solution.py:256
  20.5 13.7 %collective-permute-start.2 = (f32[1024,128]{1,0:T(8,128)S(1)}, f32[1024,128]{1,0:T(8,128)S(1)}, u32[]{:S(2)}, u32[]{:S(2)}) collective-permute-start(f32[1024,128]{1,0:T(8,128)S(1)} %bitcast.5), channel_id=1, source_target_pairs={{0,1},{1,0},{2,3},{3,2},{4,5},{5,4},{6,7},{7,6},{8,9},{9,8},{10,11... | collective-permute-start | bytes 1572872 | tf_op jit(solution)/shard_map/ppermute | solution.py:250
  34.2 0.0 collective-permute-done.3.p5
  34.2 5.2 %collective-permute-start.4 = (f32[1024,128]{1,0:T(8,128)S(1)}, f32[1024,128]{1,0:T(8,128)}, u32[]{:S(2)}, u32[]{:S(2)}) collective-permute-start(f32[1024,128]{1,0:T(8,128)S(1)} %collective-permute-done.3.p5), channel_id=1, source_target_pairs={{0,1},{1,0},{2,3},{3,2},{4,5},{5,4},{6,7},{7,6},{8,9},{9,8},{10,11... | collective-permute-start | bytes 1572872 | tf_op jit(solution)/shard_map/ppermute | solution.py:250
  39.3 0.0 collective-permute-done.p3
  39.4 1.9 %collective-permute-start.1 = (f32[1024,128]{1,0:T(8,128)S(1)}, f32[1024,128]{1,0:T(8,128)}, u32[]{:S(2)}, u32[]{:S(2)}) collective-permute-start(f32[1024,128]{1,0:T(8,128)S(1)} %collective-permute-done.p3), channel_id=1, source_target_pairs={{0,1},{1,0},{2,3},{3,2},{4,5},{5,4},{6,7},{7,6},{8,9},{9,8},{10,11... | collective-permute-start | bytes 1572872 | tf_op jit(solution)/shard_map/ppermute | solution.py:250
  41.3 0.0 copy-done.5
  41.3 0.6 fusion.11
  41.9 0.1 reshape.23.targets
  42.0 1.3 multiply_add_fusion
  43.3 0.8 reshape.21.places
  44.1 0.0 copy-done.2
  44.1 0.0 copy-done
  44.1 0.0 copy-done.4
  44.1 0.9 prepare.1
  45.0 0.0 collective-permute-done.2.p1
  45.0 0.0 collective-permute-done.4.p2
  45.0 0.0 collective-permute-done.1.p0
  45.1 0.0 copy-done.1
  45.1 0.0 copy-done.3
  45.1 3.9 %layer.1 = (f32[256,256]{1,0:T(8,128)}, f32[64,1,640]{2,1,0:T(1,128)}, bf16[4,128,256]{2,1,0:T(8,128)(2,1)S(1)}) custom-call(s32[64]{0:T(128)S(1)} %reshape.21.places, bf16[4,128,1024]{2,1,0:T(8,128)(2,1)S(1)} %get-tuple-element.16.stacked, f32[1024,128]{1,0:T(8,128)} %collective-permute-done.1.p0, f32[1024,128]{1,0:T(8,128)S(1)} %collective-permute-done.2.p1, ...), custom_call_target="tpu_custom_call" | custom-call | flops 400000000 | bytes 6000000 | tf_op jit(solution)/shard_map/layer/pallas_call | solution.py:145
  49.0 1.7 %spread.1 = (f32[3072,128]{1,0:T(8,128)S(1)}, f32[3072,128]{1,0:T(8,128)S(1)}) custom-call(s32[64]{0:T(128)S(1)} %reshape.23.targets, bf16[4,1024,128]{2,1,0:T(8,128)(2,1)S(1)} %get-tuple-element.22.turned, bf16[4,128,256]{2,1,0:T(8,128)(2,1)S(1)} %get-tuple-element.23.grads), custom_call_target="tpu_custom_call" | custom-call | flops 300000000 | bytes 5000000 | tf_op jit(solution)/shard_map/spread/pallas_call | solution.py:191
  50.6 2.4 %collective-permute-start.5 = (f32[3072,128]{1,0:T(8,128)S(1)}, f32[3072,128]{1,0:T(8,128)}, u32[]{:S(2)}, u32[]{:S(2)}) collective-permute-start(f32[3072,128]{1,0:T(8,128)S(1)} %get-tuple-element.25), channel_id=1, source_target_pairs={{0,1},{1,0},{2,3},{3,2},{4,5},{5,4},{6,7},{7,6},{8,9},{9,8},{10,11... | collective-permute-start | bytes 4718600 | tf_op jit(solution)/shard_map/ppermute | solution.py:250
  53.1 18.0 %all-to-all-start.1 = ((f32[64,1,640]{2,1,0:T(1,128)}), f32[64,1,640]{2,1,0:T(1,128)S(1)}, u32[]{:S(2)}, u32[]{:S(2)}) async-start(f32[64,1,640]{2,1,0:T(1,128)} %get-tuple-element.21), calls=%async_computation.1 | async-start | bytes 327680 | tf_op jit(solution)/shard_map/all_to_all | solution.py:307
  71.0 0.0 collective-permute-done.5
  71.0 1.3 slice_add_fusion.1
  72.3 1.3 collective-permute-start.6
  73.6 4.8 %collective-permute-start.7 = (f32[1024,128]{1,0:T(8,128)S(1)}, f32[1024,128]{1,0:T(8,128)}, u32[]{:S(2)}, u32[]{:S(2)}) collective-permute-start(f32[1024,128]{1,0:T(8,128)S(1)} %get-tuple-element.34), channel_id=1, source_target_pairs={{0,8},{8,16},{16,24},{24,32},{32,40},{40,48},{48,56},{56,64},{64,7... | collective-permute-start | bytes 1572872 | tf_op jit(solution)/shard_map/ppermute | solution.py:256
  78.4 1.4 %all-to-all-done.1.parts = f32[64,1,640]{2,1,0:T(1,128)S(1)} async-done(((f32[64,1,640]{2,1,0:T(1,128)}), f32[64,1,640]{2,1,0:T(1,128)S(1)}, u32[]{:S(2)}, u32[]{:S(2)}) %all-to-all-start.1) | async-done | bytes 163872 | tf_op jit(solution)/shard_map/all_to_all | solution.py:307
  79.9 0.7 sum_for_all.2
  80.6 10.8 %all-to-all-start.2 = ((f32[16,1,640]{2,1,0:T(1,128)}), f32[16,1,640]{2,1,0:T(1,128)S(1)}, u32[]{:S(2)}, u32[]{:S(2)}) async-start(f32[16,1,640]{2,1,0:T(1,128)} %sum_for_all.2), calls=%async_computation.2 | async-start | bytes 81920 | tf_op jit(solution)/shard_map/all_to_all | solution.py:308
  91.4 0.0 collective-permute-done.6
  91.4 0.0 collective-permute-done.7
  91.4 1.3 slice_add_fusion.2
  92.7 2.9 %collective-permute-start.9 = (f32[256,128]{1,0:T(8,128)S(1)}, f32[256,128]{1,0:T(8,128)S(1)}, u32[]{:S(2)}, u32[]{:S(2)}) collective-permute-start(f32[256,128]{1,0:T(8,128)S(1)} %get-tuple-element.31), channel_id=1, source_target_pairs={{0,6},{2,0},{4,2},{6,4},{1,7},{3,1},{5,3},{7,5},{8,14},{10,8},{12,... | collective-permute-start | bytes 393224 | tf_op jit(solution)/shard_map/ppermute | solution.py:304
  95.6 2.4 %collective-permute-start.8 = (f32[256,128]{1,0:T(8,128)S(1)}, f32[256,128]{1,0:T(8,128)S(1)}, u32[]{:S(2)}, u32[]{:S(2)}) collective-permute-start(f32[256,128]{1,0:T(8,128)S(1)} %get-tuple-element.32), channel_id=1, source_target_pairs={{0,2},{2,4},{4,6},{6,0},{1,3},{3,5},{5,7},{7,1},{8,10},{10,12},{12... | collective-permute-start | bytes 393224 | tf_op jit(solution)/shard_map/ppermute | solution.py:304
  98.0 14.6 %all-to-all-done.2.parts = f32[16,1,640]{2,1,0:T(1,128)S(1)} async-done(((f32[16,1,640]{2,1,0:T(1,128)}), f32[16,1,640]{2,1,0:T(1,128)S(1)}, u32[]{:S(2)}, u32[]{:S(2)}) %all-to-all-start.2) | async-done | bytes 40992 | tf_op jit(solution)/shard_map/all_to_all | solution.py:308
  112.6 0.0 collective-permute-done.9.refs_1_
  112.6 0.0 collective-permute-done.8.refs_0_
  112.6 0.7 sum_for_all.3
  113.3 9.3 %all-to-all-start.3 = ((f32[64,1,640]{2,1,0:T(1,128)}), f32[64,1,640]{2,1,0:T(1,128)S(1)}, u32[]{:S(2)}, u32[]{:S(2)}) async-start(f32[64,1,640]{2,1,0:T(1,128)} %sum_for_all.3), calls=%async_computation.3 | async-start | bytes 327680 | tf_op jit(solution)/shard_map/all_to_all | solution.py:309
  122.6 4.8 %collective-permute-start.10 = (f32[256,128]{1,0:T(8,128)S(1)}, f32[256,128]{1,0:T(8,128)S(1)}, u32[]{:S(2)}, u32[]{:S(2)}) collective-permute-start(f32[256,128]{1,0:T(8,128)S(1)} %get-tuple-element.30), channel_id=1, source_target_pairs={{0,4},{2,6},{4,0},{6,2},{1,5},{3,7},{5,1},{7,3},{8,12},{10,14},{12... | collective-permute-start | bytes 393224 | tf_op jit(solution)/shard_map/ppermute | solution.py:304
  127.4 3.7 %collective-permute-done.10 = f32[256,128]{1,0:T(8,128)S(1)} collective-permute-done((f32[256,128]{1,0:T(8,128)S(1)}, f32[256,128]{1,0:T(8,128)S(1)}, u32[]{:S(2)}, u32[]{:S(2)}) %collective-permute-start.10) | collective-permute-done | bytes 131104 | tf_op jit(solution)/shard_map/ppermute | solution.py:304
  131.1 1.7 %fusion.2 = f32[256,128]{1,0:T(8,128)} fusion(f32[256,128]{1,0:T(8,128)S(1)} %collective-permute-done.9.refs_1_, f32[256,128]{1,0:T(8,128)S(1)} %collective-permute-done.10, f32[256,128]{1,0:T(8,128)S(1)} %collective-permute-done.8.refs_0_, f32[1024,128]{1,0:T(8,128)} %collective-permute-done.7, f32[1024,128]{1,0:T(8,128)S(1)} %collective-permute-done.6, ...), kind=kLoop, calls=%fused_computation.8 | loop fusion | flops 196608 | bytes 1048576 | tf_op jit(solution)/shard_map/add | solution.py:306
  132.8 0.0 all-to-all-done.3.parts
  132.8 0.7 unpack.1
Async XLA Ops:
  0.6 40.7 %copy-start.5 = (s32[4,16]{1,0:T(4,128)S(1)}, s32[4,16]{1,0:T(4,128)}, u32[]{:S(2)}) copy-start(s32[4,16]{1,0:T(4,128)} %param.8) | copy-start | bytes 772
  0.6 43.4 %copy-start.2 = (f32[128,256]{1,0:T(8,128)S(1)}, f32[128,256]{1,0:T(8,128)}, u32[]{:S(2)}) copy-start(f32[128,256]{1,0:T(8,128)} %weight.1) | copy-start | bytes 393220
  0.7 43.4 %copy-start = (f32[4,64,1024]{2,1,0:T(8,128)S(1)}, f32[4,64,1024]{2,1,0:T(8,128)}, u32[]{:S(2)}) copy-start(f32[4,64,1024]{2,1,0:T(8,128)} %blocks.1) | copy-start | bytes 3145732
  0.7 43.4 %copy-start.4 = (s32[4]{0:T(128)S(1)}, s32[4]{0:T(128)}, u32[]{:S(2)}) copy-start(s32[4]{0:T(128)} %counts.1) | copy-start | bytes 52
  0.7 44.4 %copy-start.1 = (f32[256,256]{1,0:T(8,128)S(1)}, f32[256,256]{1,0:T(8,128)}, u32[]{:S(2)}) copy-start(f32[256,256]{1,0:T(8,128)} %cotangent.1) | copy-start | bytes 786436
  0.7 44.4 %copy-start.3 = (f32[256]{0:T(256)S(1)}, f32[256]{0:T(256)}, u32[]{:S(2)}) copy-start(f32[256]{0:T(256)} %param.12) | copy-start | bytes 3076
  13.3 20.9 %collective-permute-start.3 = (f32[1024,128]{1,0:T(8,128)S(1)}, f32[1024,128]{1,0:T(8,128)S(1)}, u32[]{:S(2)}, u32[]{:S(2)}) collective-permute-start(f32[1024,128]{1,0:T(8,128)S(1)} %bitcast.3), channel_id=1, source_target_pairs={{8,0},{16,8},{24,16},{32,24},{40,32},{48,40},{56,48},{64,56},{72,6... | collective-permute-start | bytes 1572872 | tf_op jit(solution)/shard_map/ppermute | solution.py:256
  14.6 24.7 %collective-permute-start = (f32[1024,128]{1,0:T(8,128)S(1)}, f32[1024,128]{1,0:T(8,128)S(1)}, u32[]{:S(2)}, u32[]{:S(2)}) collective-permute-start(f32[1024,128]{1,0:T(8,128)S(1)} %bitcast.4), channel_id=1, source_target_pairs={{0,8},{8,16},{16,24},{24,32},{32,40},{40,48},{48,56},{56,64},{64,7... | collective-permute-start | bytes 1572872 | tf_op jit(solution)/shard_map/ppermute | solution.py:256
  20.5 24.6 %collective-permute-start.2 = (f32[1024,128]{1,0:T(8,128)S(1)}, f32[1024,128]{1,0:T(8,128)S(1)}, u32[]{:S(2)}, u32[]{:S(2)}) collective-permute-start(f32[1024,128]{1,0:T(8,128)S(1)} %bitcast.5), channel_id=1, source_target_pairs={{0,1},{1,0},{2,3},{3,2},{4,5},{5,4},{6,7},{7,6},{8,9},{9,8},{10,11... | collective-permute-start | bytes 1572872 | tf_op jit(solution)/shard_map/ppermute | solution.py:250
  34.2 10.9 %collective-permute-start.4 = (f32[1024,128]{1,0:T(8,128)S(1)}, f32[1024,128]{1,0:T(8,128)}, u32[]{:S(2)}, u32[]{:S(2)}) collective-permute-start(f32[1024,128]{1,0:T(8,128)S(1)} %collective-permute-done.3.p5), channel_id=1, source_target_pairs={{0,1},{1,0},{2,3},{3,2},{4,5},{5,4},{6,7},{7,6},{8,9},{9,8},{10,11... | collective-permute-start | bytes 1572872 | tf_op jit(solution)/shard_map/ppermute | solution.py:250
  39.4 5.7 %collective-permute-start.1 = (f32[1024,128]{1,0:T(8,128)S(1)}, f32[1024,128]{1,0:T(8,128)}, u32[]{:S(2)}, u32[]{:S(2)}) collective-permute-start(f32[1024,128]{1,0:T(8,128)S(1)} %collective-permute-done.p3), channel_id=1, source_target_pairs={{0,1},{1,0},{2,3},{3,2},{4,5},{5,4},{6,7},{7,6},{8,9},{9,8},{10,11... | collective-permute-start | bytes 1572872 | tf_op jit(solution)/shard_map/ppermute | solution.py:250
  50.6 20.4 %collective-permute-start.5 = (f32[3072,128]{1,0:T(8,128)S(1)}, f32[3072,128]{1,0:T(8,128)}, u32[]{:S(2)}, u32[]{:S(2)}) collective-permute-start(f32[3072,128]{1,0:T(8,128)S(1)} %get-tuple-element.25), channel_id=1, source_target_pairs={{0,1},{1,0},{2,3},{3,2},{4,5},{5,4},{6,7},{7,6},{8,9},{9,8},{10,11... | collective-permute-start | bytes 4718600 | tf_op jit(solution)/shard_map/ppermute | solution.py:250
  53.1 26.8 %all-to-all-start.1 = ((f32[64,1,640]{2,1,0:T(1,128)}), f32[64,1,640]{2,1,0:T(1,128)S(1)}, u32[]{:S(2)}, u32[]{:S(2)}) async-start(f32[64,1,640]{2,1,0:T(1,128)} %get-tuple-element.21), calls=%async_computation.1 | async-start | bytes 327680 | tf_op jit(solution)/shard_map/all_to_all | solution.py:307
  72.3 19.0 %collective-permute-start.6 = (f32[1024,128]{1,0:T(8,128)S(1)}, f32[1024,128]{1,0:T(8,128)S(1)}, u32[]{:S(2)}, u32[]{:S(2)}) collective-permute-start(f32[1024,128]{1,0:T(8,128)S(1)} %get-tuple-element.33), channel_id=1, source_target_pairs={{8,0},{16,8},{24,16},{32,24},{40,32},{48,40},{56,48},{64,56},{72,6... | collective-permute-start | bytes 1572872 | tf_op jit(solution)/shard_map/ppermute | solution.py:256
  73.6 17.8 %collective-permute-start.7 = (f32[1024,128]{1,0:T(8,128)S(1)}, f32[1024,128]{1,0:T(8,128)}, u32[]{:S(2)}, u32[]{:S(2)}) collective-permute-start(f32[1024,128]{1,0:T(8,128)S(1)} %get-tuple-element.34), channel_id=1, source_target_pairs={{0,8},{8,16},{16,24},{24,32},{32,40},{40,48},{48,56},{56,64},{64,7... | collective-permute-start | bytes 1572872 | tf_op jit(solution)/shard_map/ppermute | solution.py:256
  80.6 32.0 %all-to-all-start.2 = ((f32[16,1,640]{2,1,0:T(1,128)}), f32[16,1,640]{2,1,0:T(1,128)S(1)}, u32[]{:S(2)}, u32[]{:S(2)}) async-start(f32[16,1,640]{2,1,0:T(1,128)} %sum_for_all.2), calls=%async_computation.2 | async-start | bytes 81920 | tf_op jit(solution)/shard_map/all_to_all | solution.py:308
  92.7 19.9 %collective-permute-start.9 = (f32[256,128]{1,0:T(8,128)S(1)}, f32[256,128]{1,0:T(8,128)S(1)}, u32[]{:S(2)}, u32[]{:S(2)}) collective-permute-start(f32[256,128]{1,0:T(8,128)S(1)} %get-tuple-element.31), channel_id=1, source_target_pairs={{0,6},{2,0},{4,2},{6,4},{1,7},{3,1},{5,3},{7,5},{8,14},{10,8},{12,... | collective-permute-start | bytes 393224 | tf_op jit(solution)/shard_map/ppermute | solution.py:304
  95.6 17.0 %collective-permute-start.8 = (f32[256,128]{1,0:T(8,128)S(1)}, f32[256,128]{1,0:T(8,128)S(1)}, u32[]{:S(2)}, u32[]{:S(2)}) collective-permute-start(f32[256,128]{1,0:T(8,128)S(1)} %get-tuple-element.32), channel_id=1, source_target_pairs={{0,2},{2,4},{4,6},{6,0},{1,3},{3,5},{5,7},{7,1},{8,10},{10,12},{12... | collective-permute-start | bytes 393224 | tf_op jit(solution)/shard_map/ppermute | solution.py:304
  113.3 19.5 %all-to-all-start.3 = ((f32[64,1,640]{2,1,0:T(1,128)}), f32[64,1,640]{2,1,0:T(1,128)S(1)}, u32[]{:S(2)}, u32[]{:S(2)}) async-start(f32[64,1,640]{2,1,0:T(1,128)} %sum_for_all.3), calls=%async_computation.3 | async-start | bytes 327680 | tf_op jit(solution)/shard_map/all_to_all | solution.py:309
  122.6 8.5 %collective-permute-start.10 = (f32[256,128]{1,0:T(8,128)S(1)}, f32[256,128]{1,0:T(8,128)S(1)}, u32[]{:S(2)}, u32[]{:S(2)}) collective-permute-start(f32[256,128]{1,0:T(8,128)S(1)} %get-tuple-element.30), channel_id=1, source_target_pairs={{0,4},{2,6},{4,0},{6,2},{1,5},{3,7},{5,1},{7,3},{8,12},{10,14},{12... | collective-permute-start | bytes 393224 | tf_op jit(solution)/shard_map/ppermute | solution.py:304

commit v4 on v3

--- a/solution.py
+++ b/solution.py
@@ -1,3 +1,4 @@
+import functools
 import math
 
 import jax
@@ -9,7 +10,7 @@
 
 BLK = 64
 LANES = 128
-VMEM_LIMIT = 40 * 1024 * 1024
+MIB = 1024 * 1024
 WIDE = ("y", "far", "near")
 ALL = ("y", "far", "near", "x", "core")
 GROUP = ("y", "near", "x", "core")
@@ -31,12 +32,26 @@
     return [pl.BlockSpec(memory_space=pltpu.VMEM)] * count
 
 
-def params():
-    return pltpu.CompilerParams(vmem_limit_bytes=VMEM_LIMIT)
-
-
-def prepare_kernel(counts, blocks, weight, stacked, turned, weight_rows, weight_low, weight_turned):
+def params(mib):
+    return pltpu.CompilerParams(vmem_limit_bytes=mib * MIB)
+
+
+def prepare_kernel(
+    chips, cores, counts, columns, blocks, weight,
+    places, targets, stacked, turned, weight_rows, weight_low, weight_turned,
+):
     rows, _, width = blocks.shape
+    stripe = rows * chips * cores
+    local = columns[...] - (lax.axis_index(WIDE) - 1) * stripe
+    part = local >> (stripe.bit_length() - 1)
+    block = local & (rows - 1)
+    device = (local & (stripe - 1)) >> (rows.bit_length() - 1)
+    chip = device >> (cores.bit_length() - 1)
+    mine = ((device ^ lax.axis_index("core")) & (cores - 1)) ^ 1
+    band = mine * 3 + part
+    ahead = (chip - lax.axis_index("x")) & (chips - 1)
+    places[...] = (band * chips + chip) * rows + block
+    targets[...] = (band * chips + ahead) * rows + block
     slot = lax.broadcasted_iota(jnp.int32, (BLK, width), 1) // BLK
     for r in range(rows):
         masked = jnp.where(slot < counts[r], blocks[r], 0.0)
@@ -55,25 +70,28 @@
     weight_turned[:, depth:] = turned_low
 
 
-def prepare(counts, blocks, weight):
+def prepare(counts, columns, blocks, weight):
     rows, _, width = blocks.shape
+    index = jax.ShapeDtypeStruct(columns.shape, columns.dtype)
     depth, hid = weight.shape
     half = jnp.bfloat16
     return pl.pallas_call(
-        prepare_kernel,
+        functools.partial(prepare_kernel, lax.axis_size("x"), lax.axis_size("core")),
         out_shape=(
+            index,
+            index,
             jax.ShapeDtypeStruct((rows, 2 * BLK, width), half),
             jax.ShapeDtypeStruct((rows, width, 2 * BLK), half),
             jax.ShapeDtypeStruct((2 * depth, hid), half),
             jax.ShapeDtypeStruct((depth, hid), half),
             jax.ShapeDtypeStruct((hid, 2 * depth), half),
         ),
-        in_specs=[pl.BlockSpec(memory_space=pltpu.SMEM)] + vmem(2),
-        out_specs=vmem(5),
-        compiler_params=params(),
+        in_specs=[pl.BlockSpec(memory_space=pltpu.SMEM)] + vmem(3),
+        out_specs=vmem(7),
+        compiler_params=params(12),
         cost_estimate=pl.CostEstimate(flops=2_000_000, bytes_accessed=4_000_000, transcendentals=0),
         name="prepare",
-    )(counts, blocks, weight)
+    )(counts, columns, blocks, weight)
 
 
 def layer_kernel(
@@ -95,7 +113,7 @@
     depth = aggregated.shape[1]
     for r in range(rows):
         for k in range(slots):
-            start = pl.multiple_of(places[r * slots + k] * BLK, BLK)
+            start = pl.multiple_of(places[r, k] * BLK, BLK)
             high, low = split(band[pl.ds(start, BLK), :])
             picked[r % 2, k * BLK:(k + 1) * BLK, :depth] = high
             picked[r % 2, k * BLK:(k + 1) * BLK, depth:] = low
@@ -158,7 +176,7 @@
             pltpu.VMEM((count, depth), jnp.float32),
             pltpu.SemaphoreType.DMA((6,)),
         ],
-        compiler_params=params(),
+        compiler_params=params(16),
         cost_estimate=pl.CostEstimate(flops=400_000_000, bytes_accessed=6_000_000, transcendentals=65536),
         name="layer",
     )(places, stacked, *pieces, weight_rows, weight_low, weight_turned, bias, cotangent)
@@ -173,7 +191,7 @@
         product = dot(turned[r], grads[r])
         product = product[:, :depth] + product[:, depth:]
         for k in range(slots):
-            start = pl.multiple_of(targets[r * slots + k] * BLK, BLK)
+            start = pl.multiple_of(targets[r, k] * BLK, BLK)
             where = pl.ds(start, BLK)
             band[where, :] = band[where, :] + product[k * BLK:(k + 1) * BLK]
     copies = [
@@ -197,7 +215,7 @@
             pltpu.VMEM((2 * half, depth), jnp.float32),
             pltpu.SemaphoreType.DMA((2,)),
         ],
-        compiler_params=params(),
+        compiler_params=params(12),
         cost_estimate=pl.CostEstimate(flops=300_000_000, bytes_accessed=5_000_000, transcendentals=0),
         name="spread",
     )(targets, turned, grads)
@@ -214,7 +232,7 @@
         out_shape=jax.ShapeDtypeStruct((shards,) + parts.shape[1:], parts.dtype),
         in_specs=vmem(1) + [pl.BlockSpec(memory_space=pl.ANY)] * len(behind),
         out_specs=pl.BlockSpec(memory_space=pltpu.VMEM),
-        compiler_params=params(),
+        compiler_params=params(4),
         name="sum_for_all",
     )(parts, *behind)
 
@@ -241,7 +259,7 @@
         ),
         in_specs=vmem(1),
         out_specs=vmem(2),
-        compiler_params=params(),
+        compiler_params=params(4),
         name="unpack",
     )(parts)
 
@@ -260,23 +278,9 @@
     rows, depth = features.shape
     hid = weight.shape[1]
     chips = lax.axis_size("x")
-    cores = lax.axis_size("core")
     shards = lax.axis_size(GROUP)
     levels = lax.axis_size("far")
-    block_rows = columns.shape[0]
-    stripe = block_rows * chips * cores
     span = chips * rows
-
-    local = columns - (lax.axis_index(WIDE) - 1) * stripe
-    part = local // stripe
-    within = local % stripe
-    device = within // block_rows
-    block = within % block_rows
-    chip = device // cores
-    mine = 1 - ((device % cores) ^ lax.axis_index("core"))
-    places = (((mine * 3 + part) * chips + chip) * block_rows + block).reshape(-1)
-    ahead = lax.rem(chip - lax.axis_index("x") + chips, chips)
-    targets = (((mine * 3 + part) * chips + ahead) * block_rows + block).reshape(-1)
 
     row_of_chips = jnp.broadcast_to(features[None], (chips, rows, depth))
     own = lax.all_to_all(row_of_chips, "x", 0, 0).reshape(span, depth)
@@ -285,7 +289,9 @@
     own_other = swap_cores(own)
     before_other = swap_cores(before)
     after_other = swap_cores(after)
-    stacked, turned, weight_rows, weight_low, weight_turned = prepare(counts, blocks, weight)
+    places, targets, stacked, turned, weight_rows, weight_low, weight_turned = prepare(
+        counts, columns, blocks, weight
+    )
     pieces = (before_other, own_other, after_other, before, own, after)
     hidden, sums, grads = layer(
         places, stacked, pieces, weight_rows, weight_low, weight_turned, bias[None], cotangent, shards
@@ -306,7 +312,7 @@
     feature_grad = sum(shares[1:], shares[0])
     scattered = lax.all_to_all(sums, GROUP, 0, 0)
     scattered = lax.all_to_all(sum_for_all(scattered, levels), "far", 0, 0)
-    gathered = lax.all_to_all(sum_for_all(scattered, shards, *shares[1::2]), GROUP, 0, 0)
+    gathered = lax.all_to_all(sum_for_all(scattered, shards, *shares[1:]), GROUP, 0, 0)
     weight_grad, bias_grad = unpack(gathered, depth, hid)
 
     return (hidden, weight_grad, bias_grad.reshape(hid), feature_grad)

time: 134 us -> 130 us (0.970)
  starting transfers between devices: 84.5 us -> 82.2 us
  other arithmetic: 6.18 us -> 4.26 us
  waiting for transfers between devices: 19.7 us -> 21.5 us
    all_to_all x1, waiting for transfers between devices: 0.01 us -> 7.17 us  [body(): lax.all_to_all(sum_for_all(scattered, shards, *shares[1:]), GROUP, 0, 0)]
    ppermute x3, waiting for transfers between devices: 3.72 us -> 0.01 us  [body(): lax.ppermute(share, 'x', [(i, (i + step) % chips) for i in range(chips)])]
    all_to_all x1, waiting for transfers between devices: 14.6 us -> 12 us  [body(): scattered = lax.all_to_all(sum_for_all(scattered, levels), 'far', 0, 0)]
    ppermute x3, starting transfers between devices: 10.1 us -> 7.82 us  [body(): lax.ppermute(share, 'x', [(i, (i + step) % chips) for i in range(chips)])]
    add x2 -> x0, other arithmetic: 1.91 us -> none  [the longest x1 1.3 us: body(): ((mine * 3 + part) * chips + chip) * block_rows + block]
  transfers between devices with their start and end apart: 14 -> 14, of which waited for: 3 -> 4; matrix products, arithmetic and copies ran while one was open for 5% -> 3% of each run, Pallas kernels for 1% -> 1%
where the time goes in v4:
time: 130 us; the launch traced here: 129 us
  starting transfers between devices  82.2 us (63%)
  waiting for transfers between devices  21.5 us (17%)
  blocking collectives  11.6 us (9%)
  Pallas kernels  7.71 us (6%)
  other arithmetic  4.26 us (3%)
    ppermute x4, starting transfers between devices, swap_cores(): return lax.ppermute(value, 'core', [(0, 1), (1, 0)])  22.8 us
    all_to_all x1, starting transfers between devices, body(): scattered = lax.all_to_all(sums, GROUP, 0, 0)  18 us
    ppermute x4, starting transfers between devices, along_wide(): return lax.ppermute(value, WIDE, route)  13.2 us
    all_to_all x1, waiting for transfers between devices, body(): scattered = lax.all_to_all(sum_for_all(scattered, levels), 'far', 0, 0)  12 us
    all_to_all x1, blocking collectives, body(): own = lax.all_to_all(row_of_chips, 'x', 0, 0).reshape(span, depth)  11.6 us
    all_to_all x1, starting transfers between devices, body(): scattered = lax.all_to_all(sum_for_all(scattered, levels), 'far', 0, 0)  10.8 us
    all_to_all x1, starting transfers between devices, body(): lax.all_to_all(sum_for_all(scattered, shards, *shares[1:]), GROUP, 0, 0)  9.62 us
    ppermute x3, starting transfers between devices, body(): lax.ppermute(share, 'x', [(i, (i + step) % chips) for i in range(chips)])  7.82 us
  transfers between devices with their start and end apart: 14, of which 4 were waited for; matrix products, arithmetic and copies ran while one was open for 3% of the time, Pallas kernels for 1%

profile of v4, /device:TPU:1, one launch (start us, length us, event | category | flops | bytes accessed | tf_op | source)
XLA Modules:
  0.0 129.3 jit_solution(6153292965913814223)
XLA Ops:
  0.6 0.0 copy-start.2
  0.6 0.0 copy-start
  0.7 0.0 copy-start.5
  0.7 0.0 copy-start.3
  0.7 0.0 copy-start.1
  0.7 0.0 copy-start.4
  0.7 1.0 broadcast_in_dim.4
  1.7 11.6 %all_to_all.20 = f32[4,256,128]{2,1,0:T(8,128)S(1)} all-to-all(f32[4,256,128]{2,1,0:T(8,128)S(1)} %broadcast_in_dim.4), channel_id=1, replica_groups=mesh['y'=4,'far'=16,'near'=2,'x'=4,'core'=2] {'x'}, dimensions={0} | all-to-all | bytes 1048576 | tf_op jit(solution)/shard_map/all_to_all | solution.py:286
  13.3 1.3 collective-permute-start.3
  14.6 5.8 %collective-permute-start = (f32[1024,128]{1,0:T(8,128)S(1)}, f32[1024,128]{1,0:T(8,128)S(1)}, u32[]{:S(2)}, u32[]{:S(2)}) collective-permute-start(f32[1024,128]{1,0:T(8,128)S(1)} %bitcast.4), channel_id=1, source_target_pairs={{0,8},{8,16},{16,24},{24,32},{32,40},{40,48},{48,56},{56,64},{64,7... | collective-permute-start | bytes 1572872 | tf_op jit(solution)/shard_map/ppermute | solution.py:274
  20.4 13.7 %collective-permute-start.2 = (f32[1024,128]{1,0:T(8,128)S(1)}, f32[1024,128]{1,0:T(8,128)S(1)}, u32[]{:S(2)}, u32[]{:S(2)}) collective-permute-start(f32[1024,128]{1,0:T(8,128)S(1)} %bitcast.5), channel_id=1, source_target_pairs={{0,1},{1,0},{2,3},{3,2},{4,5},{5,4},{6,7},{7,6},{8,9},{9,8},{10,11... | collective-permute-start | bytes 1572872 | tf_op jit(solution)/shard_map/ppermute | solution.py:268
  34.2 0.0 collective-permute-done.3.p5
  34.2 5.2 %collective-permute-start.4 = (f32[1024,128]{1,0:T(8,128)S(1)}, f32[1024,128]{1,0:T(8,128)S(1)}, u32[]{:S(2)}, u32[]{:S(2)}) collective-permute-start(f32[1024,128]{1,0:T(8,128)S(1)} %collective-permute-done.3.p5), channel_id=1, source_target_pairs={{0,1},{1,0},{2,3},{3,2},{4,5},{5,4},{6,7},{7,6},{8,9},{9,8},{10,11... | collective-permute-start | bytes 1572872 | tf_op jit(solution)/shard_map/ppermute | solution.py:268
  39.3 0.0 collective-permute-done.p3
  39.4 1.9 %collective-permute-start.1 = (f32[1024,128]{1,0:T(8,128)S(1)}, f32[1024,128]{1,0:T(8,128)S(1)}, u32[]{:S(2)}, u32[]{:S(2)}) collective-permute-start(f32[1024,128]{1,0:T(8,128)S(1)} %collective-permute-done.p3), channel_id=1, source_target_pairs={{0,1},{1,0},{2,3},{3,2},{4,5},{5,4},{6,7},{7,6},{8,9},{9,8},{10,11... | collective-permute-start | bytes 1572872 | tf_op jit(solution)/shard_map/ppermute | solution.py:268
  41.3 0.0 copy-done.2
  41.3 0.0 copy-done
  41.3 0.0 copy-done.5
  41.3 0.0 copy-done.3
  41.3 0.9 prepare.1
  42.3 0.0 collective-permute-done.2.p1
  42.3 0.0 collective-permute-done.4.p2
  42.3 0.9 collective-permute-done.1.p0
  43.2 0.0 copy-done.1
  43.2 0.0 copy-done.4
  43.2 2.9 %layer.1 = (f32[256,256]{1,0:T(8,128)}, f32[64,1,640]{2,1,0:T(1,128)}, bf16[4,128,256]{2,1,0:T(8,128)(2,1)S(1)}) custom-call(s32[4,16]{1,0:T(4,128)S(1)} %get-tuple-element.18.places, bf16[4,128,1024]{2,1,0:T(8,128)(2,1)S(1)} %get-tuple-element.19.stacked, f32[1024,128]{1,0:T(8,128)S(1)} %collective-permute-done.1.p0, ...), custom_call_target="tpu_custom_call" | custom-call | flops 400000000 | bytes 6000000 | tf_op jit(solution)/shard_map/layer/pallas_call | solution.py:163
  46.1 1.7 %spread.1 = (f32[3072,128]{1,0:T(8,128)S(1)}, f32[3072,128]{1,0:T(8,128)S(1)}) custom-call(s32[4,16]{1,0:T(4,128)S(1)} %get-tuple-element.25.targets, bf16[4,1024,128]{2,1,0:T(8,128)(2,1)S(1)} %get-tuple-element.26.turned, bf16[4,128,256]{2,1,0:T(8,128)(2,1)S(1)} %get-tuple-element.27.grads), custom_call_target="tpu_custom_call" | custom-call | flops 300000000 | bytes 5000000 | tf_op jit(solution)/shard_map/spread/pallas_call | solution.py:209
  47.8 2.0 %collective-permute-start.5 = (f32[3072,128]{1,0:T(8,128)S(1)}, f32[3072,128]{1,0:T(8,128)}, u32[]{:S(2)}, u32[]{:S(2)}) collective-permute-start(f32[3072,128]{1,0:T(8,128)S(1)} %get-tuple-element.29), channel_id=1, source_target_pairs={{0,1},{1,0},{2,3},{3,2},{4,5},{5,4},{6,7},{7,6},{8,9},{9,8},{10,11... | collective-permute-start | bytes 4718600 | tf_op jit(solution)/shard_map/ppermute | solution.py:268
  49.9 18.0 %all-to-all-start.1 = ((f32[64,1,640]{2,1,0:T(1,128)}), f32[64,1,640]{2,1,0:T(1,128)S(1)}, u32[]{:S(2)}, u32[]{:S(2)}) async-start(f32[64,1,640]{2,1,0:T(1,128)} %get-tuple-element.24), calls=%async_computation.1 | async-start | bytes 327680 | tf_op jit(solution)/shard_map/all_to_all | solution.py:313
  67.9 0.0 collective-permute-done.5
  67.9 1.3 %slice_add_fusion.1 = (f32[1024,128]{1,0:T(8,128)S(1)}, f32[1024,128]{1,0:T(8,128)S(1)}) fusion(f32[3072,128]{1,0:T(8,128)} %collective-permute-done.5, f32[3072,128]{1,0:T(8,128)S(1)} %get-tuple-element.28), kind=kLoop, calls=%fused_computation.1 | loop fusion | flops 262144 | bytes 3145728 | tf_op jit(solution)/shard_map/add | solution.py:302
  69.2 1.3 collective-permute-start.6
  70.5 4.8 %collective-permute-start.7 = (f32[1024,128]{1,0:T(8,128)S(1)}, f32[1024,128]{1,0:T(8,128)}, u32[]{:S(2)}, u32[]{:S(2)}) collective-permute-start(f32[1024,128]{1,0:T(8,128)S(1)} %get-tuple-element.36), channel_id=1, source_target_pairs={{0,8},{8,16},{16,24},{24,32},{32,40},{40,48},{48,56},{56,64},{64,7... | collective-permute-start | bytes 1572872 | tf_op jit(solution)/shard_map/ppermute | solution.py:274
  75.3 1.4 %all-to-all-done.1.parts = f32[64,1,640]{2,1,0:T(1,128)S(1)} async-done(((f32[64,1,640]{2,1,0:T(1,128)}), f32[64,1,640]{2,1,0:T(1,128)S(1)}, u32[]{:S(2)}, u32[]{:S(2)}) %all-to-all-start.1) | async-done | bytes 163872 | tf_op jit(solution)/shard_map/all_to_all | solution.py:313
  76.7 0.7 sum_for_all.2
  77.4 10.8 %all-to-all-start.2 = ((f32[16,1,640]{2,1,0:T(1,128)}), f32[16,1,640]{2,1,0:T(1,128)S(1)}, u32[]{:S(2)}, u32[]{:S(2)}) async-start(f32[16,1,640]{2,1,0:T(1,128)} %sum_for_all.2), calls=%async_computation.2 | async-start | bytes 81920 | tf_op jit(solution)/shard_map/all_to_all | solution.py:314
  88.2 0.0 collective-permute-done.6
  88.2 0.0 collective-permute-done.7
  88.3 1.3 slice_add_fusion.5
  89.5 2.9 %collective-permute-start.10 = (f32[256,128]{1,0:T(8,128)S(1)}, f32[256,128]{1,0:T(8,128)S(1)}, u32[]{:S(2)}, u32[]{:S(2)}) collective-permute-start(f32[256,128]{1,0:T(8,128)S(1)} %get-tuple-element.32), channel_id=1, source_target_pairs={{0,6},{2,0},{4,2},{6,4},{1,7},{3,1},{5,3},{7,5},{8,14},{10,8},{12,... | collective-permute-start | bytes 393224 | tf_op jit(solution)/shard_map/ppermute | solution.py:310
  92.4 3.0 %collective-permute-start.9 = (f32[256,128]{1,0:T(8,128)S(1)}, f32[256,128]{1,0:T(8,128)S(1)}, u32[]{:S(2)}, u32[]{:S(2)}) collective-permute-start(f32[256,128]{1,0:T(8,128)S(1)} %get-tuple-element.33), channel_id=1, source_target_pairs={{0,4},{2,6},{4,0},{6,2},{1,5},{3,7},{5,1},{7,3},{8,12},{10,14},{12... | collective-permute-start | bytes 393224 | tf_op jit(solution)/shard_map/ppermute | solution.py:310
  95.5 1.9 %collective-permute-start.8 = (f32[256,128]{1,0:T(8,128)S(1)}, f32[256,128]{1,0:T(8,128)S(1)}, u32[]{:S(2)}, u32[]{:S(2)}) collective-permute-start(f32[256,128]{1,0:T(8,128)S(1)} %get-tuple-element.34), channel_id=1, source_target_pairs={{0,2},{2,4},{4,6},{6,0},{1,3},{3,5},{5,7},{7,1},{8,10},{10,12},{12... | collective-permute-start | bytes 393224 | tf_op jit(solution)/shard_map/ppermute | solution.py:310
  97.4 12.0 %all-to-all-done.2.parts = f32[16,1,640]{2,1,0:T(1,128)S(1)} async-done(((f32[16,1,640]{2,1,0:T(1,128)}), f32[16,1,640]{2,1,0:T(1,128)S(1)}, u32[]{:S(2)}, u32[]{:S(2)}) %all-to-all-start.2) | async-done | bytes 40992 | tf_op jit(solution)/shard_map/all_to_all | solution.py:314
  109.4 0.0 collective-permute-done.10.refs_2_
  109.4 0.0 collective-permute-done.9.refs_1_
  109.4 0.0 collective-permute-done.8.refs_0_
  109.4 0.7 sum_for_all.3
  110.1 9.6 %all-to-all-start.3 = ((f32[64,1,640]{2,1,0:T(1,128)}), f32[64,1,640]{2,1,0:T(1,128)S(1)}, u32[]{:S(2)}, u32[]{:S(2)}) async-start(f32[64,1,640]{2,1,0:T(1,128)} %sum_for_all.3), calls=%async_computation.3 | async-start | bytes 327680 | tf_op jit(solution)/shard_map/all_to_all | solution.py:315
  119.8 1.7 %fusion.2 = f32[256,128]{1,0:T(8,128)} fusion(f32[256,128]{1,0:T(8,128)S(1)} %collective-permute-done.10.refs_2_, f32[256,128]{1,0:T(8,128)S(1)} %collective-permute-done.9.refs_1_, f32[256,128]{1,0:T(8,128)S(1)} %collective-permute-done.8.refs_0_, f32[1024,128]{1,0:T(8,128)} %collective-permute-done.7, f32[1024,128]{1,0:T(8,128)S(1)} %collective-permute-done.6, ...), kind=kLoop, calls=%fused_computation.5 | loop fusion | flops 196608 | bytes 1048576 | tf_op jit(solution)/shard_map/add | solution.py:312
  121.4 7.2 %all-to-all-done.3.parts = f32[64,1,640]{2,1,0:T(1,128)S(1)} async-done(((f32[64,1,640]{2,1,0:T(1,128)}), f32[64,1,640]{2,1,0:T(1,128)S(1)}, u32[]{:S(2)}, u32[]{:S(2)}) %all-to-all-start.3) | async-done | bytes 163872 | tf_op jit(solution)/shard_map/all_to_all | solution.py:315
  128.6 0.7 unpack.1
Async XLA Ops:
  0.6 40.7 %copy-start.2 = (f32[128,256]{1,0:T(8,128)S(1)}, f32[128,256]{1,0:T(8,128)}, u32[]{:S(2)}) copy-start(f32[128,256]{1,0:T(8,128)} %weight.1) | copy-start | bytes 393220
  0.6 40.7 %copy-start = (f32[4,64,1024]{2,1,0:T(8,128)S(1)}, f32[4,64,1024]{2,1,0:T(8,128)}, u32[]{:S(2)}) copy-start(f32[4,64,1024]{2,1,0:T(8,128)} %blocks.1) | copy-start | bytes 3145732
  0.7 40.7 %copy-start.5 = (s32[4]{0:T(128)S(1)}, s32[4]{0:T(128)}, u32[]{:S(2)}) copy-start(s32[4]{0:T(128)} %counts.1) | copy-start | bytes 52
  0.7 40.7 %copy-start.3 = (s32[4,16]{1,0:T(4,128)S(1)}, s32[4,16]{1,0:T(4,128)}, u32[]{:S(2)}) copy-start(s32[4,16]{1,0:T(4,128)} %columns.1) | copy-start | bytes 772
  0.7 42.5 %copy-start.1 = (f32[256,256]{1,0:T(8,128)S(1)}, f32[256,256]{1,0:T(8,128)}, u32[]{:S(2)}) copy-start(f32[256,256]{1,0:T(8,128)} %cotangent.1) | copy-start | bytes 786436
  0.7 42.5 %copy-start.4 = (f32[256]{0:T(256)S(1)}, f32[256]{0:T(256)}, u32[]{:S(2)}) copy-start(f32[256]{0:T(256)} %param.12) | copy-start | bytes 3076
  13.3 20.9 %collective-permute-start.3 = (f32[1024,128]{1,0:T(8,128)S(1)}, f32[1024,128]{1,0:T(8,128)S(1)}, u32[]{:S(2)}, u32[]{:S(2)}) collective-permute-start(f32[1024,128]{1,0:T(8,128)S(1)} %bitcast.3), channel_id=1, source_target_pairs={{8,0},{16,8},{24,16},{32,24},{40,32},{48,40},{56,48},{64,56},{72,6... | collective-permute-start | bytes 1572872 | tf_op jit(solution)/shard_map/ppermute | solution.py:274
  14.6 24.7 %collective-permute-start = (f32[1024,128]{1,0:T(8,128)S(1)}, f32[1024,128]{1,0:T(8,128)S(1)}, u32[]{:S(2)}, u32[]{:S(2)}) collective-permute-start(f32[1024,128]{1,0:T(8,128)S(1)} %bitcast.4), channel_id=1, source_target_pairs={{0,8},{8,16},{16,24},{24,32},{32,40},{40,48},{48,56},{56,64},{64,7... | collective-permute-start | bytes 1572872 | tf_op jit(solution)/shard_map/ppermute | solution.py:274
  20.4 21.8 %collective-permute-start.2 = (f32[1024,128]{1,0:T(8,128)S(1)}, f32[1024,128]{1,0:T(8,128)S(1)}, u32[]{:S(2)}, u32[]{:S(2)}) collective-permute-start(f32[1024,128]{1,0:T(8,128)S(1)} %bitcast.5), channel_id=1, source_target_pairs={{0,1},{1,0},{2,3},{3,2},{4,5},{5,4},{6,7},{7,6},{8,9},{9,8},{10,11... | collective-permute-start | bytes 1572872 | tf_op jit(solution)/shard_map/ppermute | solution.py:268
  34.2 8.1 %collective-permute-start.4 = (f32[1024,128]{1,0:T(8,128)S(1)}, f32[1024,128]{1,0:T(8,128)S(1)}, u32[]{:S(2)}, u32[]{:S(2)}) collective-permute-start(f32[1024,128]{1,0:T(8,128)S(1)} %collective-permute-done.3.p5), channel_id=1, source_target_pairs={{0,1},{1,0},{2,3},{3,2},{4,5},{5,4},{6,7},{7,6},{8,9},{9,8},{10,11... | collective-permute-start | bytes 1572872 | tf_op jit(solution)/shard_map/ppermute | solution.py:268
  39.4 3.8 %collective-permute-start.1 = (f32[1024,128]{1,0:T(8,128)S(1)}, f32[1024,128]{1,0:T(8,128)S(1)}, u32[]{:S(2)}, u32[]{:S(2)}) collective-permute-start(f32[1024,128]{1,0:T(8,128)S(1)} %collective-permute-done.p3), channel_id=1, source_target_pairs={{0,1},{1,0},{2,3},{3,2},{4,5},{5,4},{6,7},{7,6},{8,9},{9,8},{10,11... | collective-permute-start | bytes 1572872 | tf_op jit(solution)/shard_map/ppermute | solution.py:268
  47.8 20.0 %collective-permute-start.5 = (f32[3072,128]{1,0:T(8,128)S(1)}, f32[3072,128]{1,0:T(8,128)}, u32[]{:S(2)}, u32[]{:S(2)}) collective-permute-start(f32[3072,128]{1,0:T(8,128)S(1)} %get-tuple-element.29), channel_id=1, source_target_pairs={{0,1},{1,0},{2,3},{3,2},{4,5},{5,4},{6,7},{7,6},{8,9},{9,8},{10,11... | collective-permute-start | bytes 4718600 | tf_op jit(solution)/shard_map/ppermute | solution.py:268
  49.9 26.8 %all-to-all-start.1 = ((f32[64,1,640]{2,1,0:T(1,128)}), f32[64,1,640]{2,1,0:T(1,128)S(1)}, u32[]{:S(2)}, u32[]{:S(2)}) async-start(f32[64,1,640]{2,1,0:T(1,128)} %get-tuple-element.24), calls=%async_computation.1 | async-start | bytes 327680 | tf_op jit(solution)/shard_map/all_to_all | solution.py:313
  69.2 19.0 %collective-permute-start.6 = (f32[1024,128]{1,0:T(8,128)S(1)}, f32[1024,128]{1,0:T(8,128)S(1)}, u32[]{:S(2)}, u32[]{:S(2)}) collective-permute-start(f32[1024,128]{1,0:T(8,128)S(1)} %get-tuple-element.35), channel_id=1, source_target_pairs={{8,0},{16,8},{24,16},{32,24},{40,32},{48,40},{56,48},{64,56},{72,6... | collective-permute-start | bytes 1572872 | tf_op jit(solution)/shard_map/ppermute | solution.py:274
  70.5 17.8 %collective-permute-start.7 = (f32[1024,128]{1,0:T(8,128)S(1)}, f32[1024,128]{1,0:T(8,128)}, u32[]{:S(2)}, u32[]{:S(2)}) collective-permute-start(f32[1024,128]{1,0:T(8,128)S(1)} %get-tuple-element.36), channel_id=1, source_target_pairs={{0,8},{8,16},{16,24},{24,32},{32,40},{40,48},{48,56},{56,64},{64,7... | collective-permute-start | bytes 1572872 | tf_op jit(solution)/shard_map/ppermute | solution.py:274
  77.4 32.0 %all-to-all-start.2 = ((f32[16,1,640]{2,1,0:T(1,128)}), f32[16,1,640]{2,1,0:T(1,128)S(1)}, u32[]{:S(2)}, u32[]{:S(2)}) async-start(f32[16,1,640]{2,1,0:T(1,128)} %sum_for_all.2), calls=%async_computation.2 | async-start | bytes 81920 | tf_op jit(solution)/shard_map/all_to_all | solution.py:314
  89.5 19.9 %collective-permute-start.10 = (f32[256,128]{1,0:T(8,128)S(1)}, f32[256,128]{1,0:T(8,128)S(1)}, u32[]{:S(2)}, u32[]{:S(2)}) collective-permute-start(f32[256,128]{1,0:T(8,128)S(1)} %get-tuple-element.32), channel_id=1, source_target_pairs={{0,6},{2,0},{4,2},{6,4},{1,7},{3,1},{5,3},{7,5},{8,14},{10,8},{12,... | collective-permute-start | bytes 393224 | tf_op jit(solution)/shard_map/ppermute | solution.py:310
  92.4 17.0 %collective-permute-start.9 = (f32[256,128]{1,0:T(8,128)S(1)}, f32[256,128]{1,0:T(8,128)S(1)}, u32[]{:S(2)}, u32[]{:S(2)}) collective-permute-start(f32[256,128]{1,0:T(8,128)S(1)} %get-tuple-element.33), channel_id=1, source_target_pairs={{0,4},{2,6},{4,0},{6,2},{1,5},{3,7},{5,1},{7,3},{8,12},{10,14},{12... | collective-permute-start | bytes 393224 | tf_op jit(solution)/shard_map/ppermute | solution.py:310
  95.5 14.0 %collective-permute-start.8 = (f32[256,128]{1,0:T(8,128)S(1)}, f32[256,128]{1,0:T(8,128)S(1)}, u32[]{:S(2)}, u32[]{:S(2)}) collective-permute-start(f32[256,128]{1,0:T(8,128)S(1)} %get-tuple-element.34), channel_id=1, source_target_pairs={{0,2},{2,4},{4,6},{6,0},{1,3},{3,5},{5,7},{7,1},{8,10},{10,12},{12... | collective-permute-start | bytes 393224 | tf_op jit(solution)/shard_map/ppermute | solution.py:310
  110.1 18.5 %all-to-all-start.3 = ((f32[64,1,640]{2,1,0:T(1,128)}), f32[64,1,640]{2,1,0:T(1,128)S(1)}, u32[]{:S(2)}, u32[]{:S(2)}) async-start(f32[64,1,640]{2,1,0:T(1,128)} %sum_for_all.3), calls=%async_computation.3 | async-start | bytes 327680 | tf_op jit(solution)/shard_map/all_to_all | solution.py:315

commit v5 on v4

--- a/solution.py
+++ b/solution.py
@@ -51,7 +51,7 @@
     band = mine * 3 + part
     ahead = (chip - lax.axis_index("x")) & (chips - 1)
     places[...] = (band * chips + chip) * rows + block
-    targets[...] = (band * chips + ahead) * rows + block
+    targets[...] = ((mine * chips + ahead) * 3 + part) * rows + block
     slot = lax.broadcasted_iota(jnp.int32, (BLK, width), 1) // BLK
     for r in range(rows):
         masked = jnp.where(slot < counts[r], blocks[r], 0.0)
@@ -299,20 +299,36 @@
 
     to_other, to_mine = spread(targets, turned, grads, 3 * span, depth)
     from_core = swap_cores(to_other)
-    from_after = along_wide(to_mine[:span] + from_core[:span], -1)
-    from_before = along_wide(to_mine[2 * span:] + from_core[2 * span:], 1)
-    shares = []
-    for step in range(chips):
-        chunk = slice(rows * step, rows * (step + 1))
-        at = slice(span + rows * step, span + rows * (step + 1))
-        share = to_mine[at] + from_core[at] + from_after[chunk] + from_before[chunk]
-        if step:
-            share = lax.ppermute(share, "x", [(i, (i + step) % chips) for i in range(chips)])
-        shares.append(share)
-    feature_grad = sum(shares[1:], shares[0])
+    size = 3 * rows
+    half = size // 2
+
+    def chunk(step, low, high):
+        at = slice(step * size + low, step * size + high)
+        return to_mine[at] + from_core[at]
+
+    forth = [(i, (i + 1) % chips) for i in range(chips)]
+    back = [(i, (i - 1) % chips) for i in range(chips)]
+    by_next = lax.ppermute(chunk(2, 0, half), "x", forth)
+    by_last = lax.ppermute(chunk(2, half, size), "x", back)
+
     scattered = lax.all_to_all(sums, GROUP, 0, 0)
-    scattered = lax.all_to_all(sum_for_all(scattered, levels), "far", 0, 0)
-    gathered = lax.all_to_all(sum_for_all(scattered, shards, *shares[1:]), GROUP, 0, 0)
+    plane_sum = sum_for_all(scattered, levels, by_next, by_last)
+    scattered = lax.all_to_all(plane_sum, "far", 0, 0)
+
+    low_last = lax.ppermute(chunk(1, 0, half) + by_next, "x", forth)
+    high_last = lax.ppermute(chunk(1, half, size), "x", forth)
+    low_next = lax.ppermute(chunk(3, 0, half), "x", back)
+    high_next = lax.ppermute(chunk(3, half, size) + by_last, "x", back)
+    before = chunk(0, 0, rows) + low_last[:rows] + low_next[:rows]
+    rest = half - rows
+    own_low = chunk(0, rows, half) + low_last[rows:] + low_next[rows:]
+    own_high = chunk(0, half, 2 * rows) + high_last[:rows - rest] + high_next[:rows - rest]
+    after = chunk(0, 2 * rows, size) + high_last[rows - rest:] + high_next[rows - rest:]
+    from_after = along_wide(before, -1)
+    from_before = along_wide(after, 1)
+    feature_grad = jnp.concatenate([own_low, own_high]) + from_after + from_before
+
+    gathered = lax.all_to_all(sum_for_all(scattered, shards, low_last, high_last, low_next, high_next), GROUP, 0, 0)
     weight_grad, bias_grad = unpack(gathered, depth, hid)
 
     return (hidden, weight_grad, bias_grad.reshape(hid), feature_grad)

time: 130 us -> 141 us (1.085)
  the two profiles are of different devices: /device:TPU:1 before, /device:TPU:24 now
where the time goes in v5:
time: 141 us; the launch traced here: 140 us
  starting transfers between devices  75.8 us (54%)
  waiting for transfers between devices  34.7 us (25%)
  blocking collectives  13.6 us (10%)
  Pallas kernels  8.66 us (6%)
  other arithmetic  4.98 us (4%)
    ppermute x4, starting transfers between devices, along_wide(): return lax.ppermute(value, WIDE, route)  26.6 us
    ppermute x4, waiting for transfers between devices, along_wide(): return lax.ppermute(value, WIDE, route)  16.6 us
    all_to_all x1, blocking collectives, body(): own = lax.all_to_all(row_of_chips, 'x', 0, 0).reshape(span, depth)  13.6 us
    all_to_all x1, starting transfers between devices, body(): scattered = lax.all_to_all(plane_sum, 'far', 0, 0)  11.1 us
    ppermute x4, starting transfers between devices, swap_cores(): return lax.ppermute(value, 'core', [(0, 1), (1, 0)])  7.79 us
    all_to_all x1, starting transfers between devices, body(): lax.all_to_all(sum_for_all(scattered, shards, low_last, high_last, low_ne...  6.18 us
    all_to_all x1, starting transfers between devices, body(): scattered = lax.all_to_all(sums, GROUP, 0, 0)  5.91 us
    ppermute x1, waiting for transfers between devices, body(): by_next = lax.ppermute(chunk(2, 0, half), 'x', forth)  5.33 us
  transfers between devices with their start and end apart: 17, of which 10 were waited for; matrix products, arithmetic and copies ran while one was open for 4% of the time, Pallas kernels for 1%

profile of v5, /device:TPU:24, one launch (start us, length us, event | category | flops | bytes accessed | tf_op | source)
XLA Modules:
  0.0 139.7 jit_solution(5040930721763502778)
XLA Ops:
  0.6 0.0 copy-start.2
  0.6 0.0 copy-start
  0.7 0.0 copy-start.5
  0.7 0.0 copy-start.3
  0.7 0.0 copy-start.1
  0.7 0.0 copy-start.4
  0.7 1.0 broadcast_in_dim.4
  1.7 13.6 %all_to_all.20 = f32[4,256,128]{2,1,0:T(8,128)S(1)} all-to-all(f32[4,256,128]{2,1,0:T(8,128)S(1)} %broadcast_in_dim.4), channel_id=1, replica_groups=mesh['y'=4,'far'=16,'near'=2,'x'=4,'core'=2] {'x'}, dimensions={0} | all-to-all | bytes 1048576 | tf_op jit(solution)/shard_map/all_to_all | solution.py:286
  15.3 18.8 %collective-permute-start.3 = (f32[1024,128]{1,0:T(8,128)S(1)}, f32[1024,128]{1,0:T(8,128)S(1)}, u32[]{:S(2)}, u32[]{:S(2)}) collective-permute-start(f32[1024,128]{1,0:T(8,128)S(1)} %bitcast.3), channel_id=1, source_target_pairs={{8,0},{16,8},{24,16},{32,24},{40,32},{48,40},{56,48},{64,56},{72,6... | collective-permute-start | bytes 1572872 | tf_op jit(solution)/shard_map/ppermute | solution.py:274
  34.2 1.9 %collective-permute-start = (f32[1024,128]{1,0:T(8,128)S(1)}, f32[1024,128]{1,0:T(8,128)S(1)}, u32[]{:S(2)}, u32[]{:S(2)}) collective-permute-start(f32[1024,128]{1,0:T(8,128)S(1)} %bitcast.4), channel_id=1, source_target_pairs={{0,8},{8,16},{16,24},{24,32},{32,40},{40,48},{48,56},{56,64},{64,7... | collective-permute-start | bytes 1572872 | tf_op jit(solution)/shard_map/ppermute | solution.py:274
  36.1 1.9 %collective-permute-start.2 = (f32[1024,128]{1,0:T(8,128)S(1)}, f32[1024,128]{1,0:T(8,128)S(1)}, u32[]{:S(2)}, u32[]{:S(2)}) collective-permute-start(f32[1024,128]{1,0:T(8,128)S(1)} %bitcast.5), channel_id=1, source_target_pairs={{0,1},{1,0},{2,3},{3,2},{4,5},{5,4},{6,7},{7,6},{8,9},{9,8},{10,11... | collective-permute-start | bytes 1572872 | tf_op jit(solution)/shard_map/ppermute | solution.py:268
  38.0 6.1 %collective-permute-done.3.p5 = f32[1024,128]{1,0:T(8,128)S(1)} collective-permute-done((f32[1024,128]{1,0:T(8,128)S(1)}, f32[1024,128]{1,0:T(8,128)S(1)}, u32[]{:S(2)}, u32[]{:S(2)}) %collective-permute-start.3) | collective-permute-done | bytes 524320 | tf_op jit(solution)/shard_map/ppermute | solution.py:274
  44.1 1.9 %collective-permute-start.4 = (f32[1024,128]{1,0:T(8,128)S(1)}, f32[1024,128]{1,0:T(8,128)S(1)}, u32[]{:S(2)}, u32[]{:S(2)}) collective-permute-start(f32[1024,128]{1,0:T(8,128)S(1)} %collective-permute-done.3.p5), channel_id=1, source_target_pairs={{0,1},{1,0},{2,3},{3,2},{4,5},{5,4},{6,7},{7,6},{8,9},{9,8},{10,11... | collective-permute-start | bytes 1572872 | tf_op jit(solution)/shard_map/ppermute | solution.py:268
  46.1 4.3 %collective-permute-done.p3 = f32[1024,128]{1,0:T(8,128)S(1)} collective-permute-done((f32[1024,128]{1,0:T(8,128)S(1)}, f32[1024,128]{1,0:T(8,128)S(1)}, u32[]{:S(2)}, u32[]{:S(2)}) %collective-permute-start) | collective-permute-done | bytes 524320 | tf_op jit(solution)/shard_map/ppermute | solution.py:274
  50.4 1.9 %collective-permute-start.1 = (f32[1024,128]{1,0:T(8,128)S(1)}, f32[1024,128]{1,0:T(8,128)S(1)}, u32[]{:S(2)}, u32[]{:S(2)}) collective-permute-start(f32[1024,128]{1,0:T(8,128)S(1)} %collective-permute-done.p3), channel_id=1, source_target_pairs={{0,1},{1,0},{2,3},{3,2},{4,5},{5,4},{6,7},{7,6},{8,9},{9,8},{10,11... | collective-permute-start | bytes 1572872 | tf_op jit(solution)/shard_map/ppermute | solution.py:268
  52.3 0.0 copy-done.2
  52.3 0.0 copy-done
  52.3 0.0 copy-done.5
  52.3 0.0 copy-done.3
  52.3 0.9 prepare.1
  53.3 0.0 collective-permute-done.2.p1
  53.3 0.0 collective-permute-done.4.p2
  53.3 0.9 collective-permute-done.1.p0
  54.2 0.0 copy-done.1
  54.2 0.0 copy-done.4
  54.2 3.0 %layer.1 = (f32[256,256]{1,0:T(8,128)}, f32[64,1,640]{2,1,0:T(1,128)}, bf16[4,128,256]{2,1,0:T(8,128)(2,1)S(1)}) custom-call(s32[4,16]{1,0:T(4,128)S(1)} %get-tuple-element.18.places, bf16[4,128,1024]{2,1,0:T(8,128)(2,1)S(1)} %get-tuple-element.19.stacked, f32[1024,128]{1,0:T(8,128)S(1)} %collective-permute-done.1.p0, ...), custom_call_target="tpu_custom_call" | custom-call | flops 400000000 | bytes 6000000 | tf_op jit(solution)/shard_map/layer/pallas_call | solution.py:163
  57.1 2.6 %spread.1 = (f32[3072,128]{1,0:T(8,128)}, f32[3072,128]{1,0:T(8,128)S(1)}) custom-call(s32[4,16]{1,0:T(4,128)S(1)} %get-tuple-element.25.targets, bf16[4,1024,128]{2,1,0:T(8,128)(2,1)S(1)} %get-tuple-element.26.turned, bf16[4,128,256]{2,1,0:T(8,128)(2,1)S(1)} %get-tuple-element.27.grads), custom_call_target="tpu_custom_call" | custom-call | flops 300000000 | bytes 5000000 | tf_op jit(solution)/shard_map/spread/pallas_call | solution.py:209
  59.7 2.0 %collective-permute-start.5 = (f32[3072,128]{1,0:T(8,128)}, f32[3072,128]{1,0:T(8,128)}, u32[]{:S(2)}, u32[]{:S(2)}) collective-permute-start(f32[3072,128]{1,0:T(8,128)} %get-tuple-element.29), channel_id=1, source_target_pairs={{0,1},{1,0},{2,3},{3,2},{4,5},{5,4},{6,7},{7,6},{8,9},{9,8},{10,11... | collective-permute-start | bytes 4718600 | tf_op jit(solution)/shard_map/ppermute | solution.py:268
  61.8 5.9 %all-to-all-start.1 = ((f32[64,1,640]{2,1,0:T(1,128)}), f32[64,1,640]{2,1,0:T(1,128)S(1)}, u32[]{:S(2)}, u32[]{:S(2)}) async-start(f32[64,1,640]{2,1,0:T(1,128)} %get-tuple-element.24), calls=%async_computation.1 | async-start | bytes 327680 | tf_op jit(solution)/shard_map/all_to_all | solution.py:314
  67.7 0.0 collective-permute-done.5
  67.7 1.1 slice_add_fusion.4
  68.8 4.6 %collective-permute-start.7 = (f32[384,128]{1,0:T(8,128)S(1)}, f32[384,128]{1,0:T(8,128)S(1)}, u32[]{:S(2)}, u32[]{:S(2)}) collective-permute-start(f32[384,128]{1,0:T(8,128)S(1)} %get-tuple-element.40), channel_id=1, source_target_pairs={{0,6},{2,0},{4,2},{6,4},{1,7},{3,1},{5,3},{7,5},{8,14},{10,8},{12,... | collective-permute-start | bytes 589832 | tf_op jit(solution)/shard_map/ppermute | solution.py:312
  73.4 1.9 %collective-permute-start.6 = (f32[384,128]{1,0:T(8,128)S(1)}, f32[384,128]{1,0:T(8,128)S(1)}, u32[]{:S(2)}, u32[]{:S(2)}) collective-permute-start(f32[384,128]{1,0:T(8,128)S(1)} %get-tuple-element.41), channel_id=1, source_target_pairs={{0,2},{2,4},{4,6},{6,0},{1,3},{3,5},{5,7},{7,1},{8,10},{10,12},{12... | collective-permute-start | bytes 589832 | tf_op jit(solution)/shard_map/ppermute | solution.py:311
  75.4 0.0 all-to-all-done.1.parts
  75.4 2.5 %collective-permute-done.7.refs_1_ = f32[384,128]{1,0:T(8,128)S(1)} collective-permute-done((f32[384,128]{1,0:T(8,128)S(1)}, f32[384,128]{1,0:T(8,128)S(1)}, u32[]{:S(2)}, u32[]{:S(2)}) %collective-permute-start.7) | collective-permute-done | bytes 196640 | tf_op jit(solution)/shard_map/ppermute | solution.py:312
  77.9 5.3 %collective-permute-done.6.refs_0_ = f32[384,128]{1,0:T(8,128)S(1)} collective-permute-done((f32[384,128]{1,0:T(8,128)S(1)}, f32[384,128]{1,0:T(8,128)S(1)}, u32[]{:S(2)}, u32[]{:S(2)}) %collective-permute-start.6) | collective-permute-done | bytes 196640 | tf_op jit(solution)/shard_map/ppermute | solution.py:311
  83.2 0.7 sum_for_all.2
  83.9 11.1 %all-to-all-start.2 = ((f32[16,1,640]{2,1,0:T(1,128)}), f32[16,1,640]{2,1,0:T(1,128)S(1)}, u32[]{:S(2)}, u32[]{:S(2)}) async-start(f32[16,1,640]{2,1,0:T(1,128)} %sum_for_all.2), calls=%async_computation.2 | async-start | bytes 81920 | tf_op jit(solution)/shard_map/all_to_all | solution.py:316
  95.0 1.3 fusion
  96.3 1.9 %collective-permute-start.11 = (f32[384,128]{1,0:T(8,128)S(1)}, f32[384,128]{1,0:T(8,128)S(1)}, u32[]{:S(2)}, u32[]{:S(2)}) collective-permute-start(f32[384,128]{1,0:T(8,128)S(1)} %get-tuple-element.36), channel_id=1, source_target_pairs={{0,6},{2,0},{4,2},{6,4},{1,7},{3,1},{5,3},{7,5},{8,14},{10,8},{12,... | collective-permute-start | bytes 589832 | tf_op jit(solution)/shard_map/ppermute | solution.py:321
  98.3 2.1 %collective-permute-start.10 = (f32[384,128]{1,0:T(8,128)S(1)}, f32[384,128]{1,0:T(8,128)S(1)}, u32[]{:S(2)}, u32[]{:S(2)}) collective-permute-start(f32[384,128]{1,0:T(8,128)S(1)} %get-tuple-element.37), channel_id=1, source_target_pairs={{0,6},{2,0},{4,2},{6,4},{1,7},{3,1},{5,3},{7,5},{8,14},{10,8},{12,... | collective-permute-start | bytes 589832 | tf_op jit(solution)/shard_map/ppermute | solution.py:320
  100.3 3.8 %collective-permute-start.9 = (f32[384,128]{1,0:T(8,128)S(1)}, f32[384,128]{1,0:T(8,128)S(1)}, u32[]{:S(2)}, u32[]{:S(2)}) collective-permute-start(f32[384,128]{1,0:T(8,128)S(1)} %get-tuple-element.38), channel_id=1, source_target_pairs={{0,2},{2,4},{4,6},{6,0},{1,3},{3,5},{5,7},{7,1},{8,10},{10,12},{12... | collective-permute-start | bytes 589832 | tf_op jit(solution)/shard_map/ppermute | solution.py:319
  104.1 3.9 %collective-permute-start.8 = (f32[384,128]{1,0:T(8,128)S(1)}, f32[384,128]{1,0:T(8,128)S(1)}, u32[]{:S(2)}, u32[]{:S(2)}) collective-permute-start(f32[384,128]{1,0:T(8,128)S(1)} %get-tuple-element.39), channel_id=1, source_target_pairs={{0,2},{2,4},{4,6},{6,0},{1,3},{3,5},{5,7},{7,1},{8,10},{10,12},{12... | collective-permute-start | bytes 589832 | tf_op jit(solution)/shard_map/ppermute | solution.py:318
  108.1 0.0 collective-permute-done.11.refs_3_
  108.1 0.0 collective-permute-done.10.refs_2_
  108.1 2.2 %collective-permute-done.9.refs_1_ = f32[384,128]{1,0:T(8,128)S(1)} collective-permute-done((f32[384,128]{1,0:T(8,128)S(1)}, f32[384,128]{1,0:T(8,128)S(1)}, u32[]{:S(2)}, u32[]{:S(2)}) %collective-permute-start.9) | collective-permute-done | bytes 196640 | tf_op jit(solution)/shard_map/ppermute | solution.py:319
  110.3 3.1 %collective-permute-done.8.refs_0_ = f32[384,128]{1,0:T(8,128)S(1)} collective-permute-done((f32[384,128]{1,0:T(8,128)S(1)}, f32[384,128]{1,0:T(8,128)S(1)}, u32[]{:S(2)}, u32[]{:S(2)}) %collective-permute-start.8) | collective-permute-done | bytes 196640 | tf_op jit(solution)/shard_map/ppermute | solution.py:318
  113.3 4.1 %all-to-all-done.2.parts = f32[16,1,640]{2,1,0:T(1,128)S(1)} async-done(((f32[16,1,640]{2,1,0:T(1,128)}), f32[16,1,640]{2,1,0:T(1,128)S(1)}, u32[]{:S(2)}, u32[]{:S(2)}) %all-to-all-start.2) | async-done | bytes 40992 | tf_op jit(solution)/shard_map/all_to_all | solution.py:316
  117.4 0.7 sum_for_all.3
  118.1 6.2 %all-to-all-start.3 = ((f32[64,1,640]{2,1,0:T(1,128)}), f32[64,1,640]{2,1,0:T(1,128)S(1)}, u32[]{:S(2)}, u32[]{:S(2)}) async-start(f32[64,1,640]{2,1,0:T(1,128)} %sum_for_all.3), calls=%async_computation.3 | async-start | bytes 327680 | tf_op jit(solution)/shard_map/all_to_all | solution.py:331
  124.3 1.0 slice_add_fusion.9
  125.4 3.7 %collective-permute-start.12 = (f32[256,128]{1,0:T(8,128)S(1)}, f32[256,128]{1,0:T(8,128)S(1)}, u32[]{:S(2)}, u32[]{:S(2)}) collective-permute-start(f32[256,128]{1,0:T(8,128)S(1)} %get-tuple-element.34), channel_id=1, source_target_pairs={{8,0},{16,8},{24,16},{32,24},{40,32},{48,40},{56,48},{64,56},{72,6... | collective-permute-start | bytes 393224 | tf_op jit(solution)/shard_map/ppermute | solution.py:274
  129.1 2.2 %collective-permute-start.13 = (f32[256,128]{1,0:T(8,128)S(1)}, f32[256,128]{1,0:T(8,128)S(1)}, u32[]{:S(2)}, u32[]{:S(2)}) collective-permute-start(f32[256,128]{1,0:T(8,128)S(1)} %get-tuple-element.35), channel_id=1, source_target_pairs={{0,8},{8,16},{16,24},{24,32},{32,40},{40,48},{48,56},{56,64},{64,7... | collective-permute-start | bytes 393224 | tf_op jit(solution)/shard_map/ppermute | solution.py:274
  131.2 0.9 slice_add_fusion.15
  132.1 0.7 collective-permute-done.12
  132.8 5.5 %collective-permute-done.13 = f32[256,128]{1,0:T(8,128)S(1)} collective-permute-done((f32[256,128]{1,0:T(8,128)S(1)}, f32[256,128]{1,0:T(8,128)S(1)}, u32[]{:S(2)}, u32[]{:S(2)}) %collective-permute-start.13) | collective-permute-done | bytes 131104 | tf_op jit(solution)/shard_map/ppermute | solution.py:274
  138.3 0.7 fusion.2
  139.0 0.0 all-to-all-done.3.parts
  139.0 0.7 unpack.1
Async XLA Ops:
  0.6 51.6 %copy-start.2 = (f32[128,256]{1,0:T(8,128)S(1)}, f32[128,256]{1,0:T(8,128)}, u32[]{:S(2)}) copy-start(f32[128,256]{1,0:T(8,128)} %weight.1) | copy-start | bytes 393220
  0.6 51.6 %copy-start = (f32[4,64,1024]{2,1,0:T(8,128)S(1)}, f32[4,64,1024]{2,1,0:T(8,128)}, u32[]{:S(2)}) copy-start(f32[4,64,1024]{2,1,0:T(8,128)} %blocks.1) | copy-start | bytes 3145732
  0.7 51.6 %copy-start.5 = (s32[4]{0:T(128)S(1)}, s32[4]{0:T(128)}, u32[]{:S(2)}) copy-start(s32[4]{0:T(128)} %counts.1) | copy-start | bytes 52
  0.7 51.6 %copy-start.3 = (s32[4,16]{1,0:T(4,128)S(1)}, s32[4,16]{1,0:T(4,128)}, u32[]{:S(2)}) copy-start(s32[4,16]{1,0:T(4,128)} %columns.1) | copy-start | bytes 772
  0.7 53.5 %copy-start.1 = (f32[256,256]{1,0:T(8,128)S(1)}, f32[256,256]{1,0:T(8,128)}, u32[]{:S(2)}) copy-start(f32[256,256]{1,0:T(8,128)} %cotangent.1) | copy-start | bytes 786436
  0.7 53.5 %copy-start.4 = (f32[256]{0:T(256)S(1)}, f32[256]{0:T(256)}, u32[]{:S(2)}) copy-start(f32[256]{0:T(256)} %param.12) | copy-start | bytes 3076
  15.3 28.8 %collective-permute-start.3 = (f32[1024,128]{1,0:T(8,128)S(1)}, f32[1024,128]{1,0:T(8,128)S(1)}, u32[]{:S(2)}, u32[]{:S(2)}) collective-permute-start(f32[1024,128]{1,0:T(8,128)S(1)} %bitcast.3), channel_id=1, source_target_pairs={{8,0},{16,8},{24,16},{32,24},{40,32},{48,40},{56,48},{64,56},{72,6... | collective-permute-start | bytes 1572872 | tf_op jit(solution)/shard_map/ppermute | solution.py:274
  34.2 16.2 %collective-permute-start = (f32[1024,128]{1,0:T(8,128)S(1)}, f32[1024,128]{1,0:T(8,128)S(1)}, u32[]{:S(2)}, u32[]{:S(2)}) collective-permute-start(f32[1024,128]{1,0:T(8,128)S(1)} %bitcast.4), channel_id=1, source_target_pairs={{0,8},{8,16},{16,24},{24,32},{32,40},{40,48},{48,56},{56,64},{64,7... | collective-permute-start | bytes 1572872 | tf_op jit(solution)/shard_map/ppermute | solution.py:274
  36.1 17.2 %collective-permute-start.2 = (f32[1024,128]{1,0:T(8,128)S(1)}, f32[1024,128]{1,0:T(8,128)S(1)}, u32[]{:S(2)}, u32[]{:S(2)}) collective-permute-start(f32[1024,128]{1,0:T(8,128)S(1)} %bitcast.5), channel_id=1, source_target_pairs={{0,1},{1,0},{2,3},{3,2},{4,5},{5,4},{6,7},{7,6},{8,9},{9,8},{10,11... | collective-permute-start | bytes 1572872 | tf_op jit(solution)/shard_map/ppermute | solution.py:268
  44.1 9.1 %collective-permute-start.4 = (f32[1024,128]{1,0:T(8,128)S(1)}, f32[1024,128]{1,0:T(8,128)S(1)}, u32[]{:S(2)}, u32[]{:S(2)}) collective-permute-start(f32[1024,128]{1,0:T(8,128)S(1)} %collective-permute-done.3.p5), channel_id=1, source_target_pairs={{0,1},{1,0},{2,3},{3,2},{4,5},{5,4},{6,7},{7,6},{8,9},{9,8},{10,11... | collective-permute-start | bytes 1572872 | tf_op jit(solution)/shard_map/ppermute | solution.py:268
  50.4 3.8 %collective-permute-start.1 = (f32[1024,128]{1,0:T(8,128)S(1)}, f32[1024,128]{1,0:T(8,128)S(1)}, u32[]{:S(2)}, u32[]{:S(2)}) collective-permute-start(f32[1024,128]{1,0:T(8,128)S(1)} %collective-permute-done.p3), channel_id=1, source_target_pairs={{0,1},{1,0},{2,3},{3,2},{4,5},{5,4},{6,7},{7,6},{8,9},{9,8},{10,11... | collective-permute-start | bytes 1572872 | tf_op jit(solution)/shard_map/ppermute | solution.py:268
  59.7 8.0 %collective-permute-start.5 = (f32[3072,128]{1,0:T(8,128)}, f32[3072,128]{1,0:T(8,128)}, u32[]{:S(2)}, u32[]{:S(2)}) collective-permute-start(f32[3072,128]{1,0:T(8,128)} %get-tuple-element.29), channel_id=1, source_target_pairs={{0,1},{1,0},{2,3},{3,2},{4,5},{5,4},{6,7},{7,6},{8,9},{9,8},{10,11... | collective-permute-start | bytes 4718600 | tf_op jit(solution)/shard_map/ppermute | solution.py:268
  61.8 13.6 %all-to-all-start.1 = ((f32[64,1,640]{2,1,0:T(1,128)}), f32[64,1,640]{2,1,0:T(1,128)S(1)}, u32[]{:S(2)}, u32[]{:S(2)}) async-start(f32[64,1,640]{2,1,0:T(1,128)} %get-tuple-element.24), calls=%async_computation.1 | async-start | bytes 327680 | tf_op jit(solution)/shard_map/all_to_all | solution.py:314
  68.8 9.1 %collective-permute-start.7 = (f32[384,128]{1,0:T(8,128)S(1)}, f32[384,128]{1,0:T(8,128)S(1)}, u32[]{:S(2)}, u32[]{:S(2)}) collective-permute-start(f32[384,128]{1,0:T(8,128)S(1)} %get-tuple-element.40), channel_id=1, source_target_pairs={{0,6},{2,0},{4,2},{6,4},{1,7},{3,1},{5,3},{7,5},{8,14},{10,8},{12,... | collective-permute-start | bytes 589832 | tf_op jit(solution)/shard_map/ppermute | solution.py:312
  73.4 9.8 %collective-permute-start.6 = (f32[384,128]{1,0:T(8,128)S(1)}, f32[384,128]{1,0:T(8,128)S(1)}, u32[]{:S(2)}, u32[]{:S(2)}) collective-permute-start(f32[384,128]{1,0:T(8,128)S(1)} %get-tuple-element.41), channel_id=1, source_target_pairs={{0,2},{2,4},{4,6},{6,0},{1,3},{3,5},{5,7},{7,1},{8,10},{10,12},{12... | collective-permute-start | bytes 589832 | tf_op jit(solution)/shard_map/ppermute | solution.py:311
  83.9 33.5 %all-to-all-start.2 = ((f32[16,1,640]{2,1,0:T(1,128)}), f32[16,1,640]{2,1,0:T(1,128)S(1)}, u32[]{:S(2)}, u32[]{:S(2)}) async-start(f32[16,1,640]{2,1,0:T(1,128)} %sum_for_all.2), calls=%async_computation.2 | async-start | bytes 81920 | tf_op jit(solution)/shard_map/all_to_all | solution.py:316
  96.3 11.7 %collective-permute-start.11 = (f32[384,128]{1,0:T(8,128)S(1)}, f32[384,128]{1,0:T(8,128)S(1)}, u32[]{:S(2)}, u32[]{:S(2)}) collective-permute-start(f32[384,128]{1,0:T(8,128)S(1)} %get-tuple-element.36), channel_id=1, source_target_pairs={{0,6},{2,0},{4,2},{6,4},{1,7},{3,1},{5,3},{7,5},{8,14},{10,8},{12,... | collective-permute-start | bytes 589832 | tf_op jit(solution)/shard_map/ppermute | solution.py:321
  98.3 9.8 %collective-permute-start.10 = (f32[384,128]{1,0:T(8,128)S(1)}, f32[384,128]{1,0:T(8,128)S(1)}, u32[]{:S(2)}, u32[]{:S(2)}) collective-permute-start(f32[384,128]{1,0:T(8,128)S(1)} %get-tuple-element.37), channel_id=1, source_target_pairs={{0,6},{2,0},{4,2},{6,4},{1,7},{3,1},{5,3},{7,5},{8,14},{10,8},{12,... | collective-permute-start | bytes 589832 | tf_op jit(solution)/shard_map/ppermute | solution.py:320
  100.3 9.9 %collective-permute-start.9 = (f32[384,128]{1,0:T(8,128)S(1)}, f32[384,128]{1,0:T(8,128)S(1)}, u32[]{:S(2)}, u32[]{:S(2)}) collective-permute-start(f32[384,128]{1,0:T(8,128)S(1)} %get-tuple-element.38), channel_id=1, source_target_pairs={{0,2},{2,4},{4,6},{6,0},{1,3},{3,5},{5,7},{7,1},{8,10},{10,12},{12... | collective-permute-start | bytes 589832 | tf_op jit(solution)/shard_map/ppermute | solution.py:319
  104.1 9.2 %collective-permute-start.8 = (f32[384,128]{1,0:T(8,128)S(1)}, f32[384,128]{1,0:T(8,128)S(1)}, u32[]{:S(2)}, u32[]{:S(2)}) collective-permute-start(f32[384,128]{1,0:T(8,128)S(1)} %get-tuple-element.39), channel_id=1, source_target_pairs={{0,2},{2,4},{4,6},{6,0},{1,3},{3,5},{5,7},{7,1},{8,10},{10,12},{12... | collective-permute-start | bytes 589832 | tf_op jit(solution)/shard_map/ppermute | solution.py:318
  118.1 20.9 %all-to-all-start.3 = ((f32[64,1,640]{2,1,0:T(1,128)}), f32[64,1,640]{2,1,0:T(1,128)S(1)}, u32[]{:S(2)}, u32[]{:S(2)}) async-start(f32[64,1,640]{2,1,0:T(1,128)} %sum_for_all.3), calls=%async_computation.3 | async-start | bytes 327680 | tf_op jit(solution)/shard_map/all_to_all | solution.py:331
  125.4 7.4 %collective-permute-start.12 = (f32[256,128]{1,0:T(8,128)S(1)}, f32[256,128]{1,0:T(8,128)S(1)}, u32[]{:S(2)}, u32[]{:S(2)}) collective-permute-start(f32[256,128]{1,0:T(8,128)S(1)} %get-tuple-element.34), channel_id=1, source_target_pairs={{8,0},{16,8},{24,16},{32,24},{40,32},{48,40},{56,48},{64,56},{72,6... | collective-permute-start | bytes 393224 | tf_op jit(solution)/shard_map/ppermute | solution.py:274
  129.1 9.3 %collective-permute-start.13 = (f32[256,128]{1,0:T(8,128)S(1)}, f32[256,128]{1,0:T(8,128)S(1)}, u32[]{:S(2)}, u32[]{:S(2)}) collective-permute-start(f32[256,128]{1,0:T(8,128)S(1)} %get-tuple-element.35), channel_id=1, source_target_pairs={{0,8},{8,16},{16,24},{24,32},{32,40},{40,48},{48,56},{56,64},{64,7... | collective-permute-start | bytes 393224 | tf_op jit(solution)/shard_map/ppermute | solution.py:274

commit v6 on v4

--- a/solution.py
+++ b/solution.py
@@ -95,8 +95,9 @@
 
 
 def layer_kernel(
-    places, stacked, p0, p1, p2, p3, p4, p5, weight_rows, weight_low, weight_turned, bias, cotangent,
-    hidden, sums, grads, band, picked, aggregated, sems,
+    places, targets, stacked, turned, p0, p1, p2, p3, p4, p5,
+    weight_rows, weight_low, weight_turned, bias, cotangent,
+    hidden, sums, other, mine, band, spread, picked, aggregated, grads, sems, out_sems,
 ):
     pieces = (p0, p1, p2, p3, p4, p5)
     span = p0.shape[0]
@@ -106,6 +107,7 @@
     ]
     for copy in copies:
         copy.start()
+    spread[...] = jnp.zeros_like(spread)
     for copy in copies:
         copy.wait()
     rows, _, width = stacked.shape
@@ -154,48 +156,14 @@
         for top in (0, BLK):
             grads[r, top:top + BLK, :depth] = bhigh[r * BLK:(r + 1) * BLK]
             grads[r, top:top + BLK, depth:] = blow[r * BLK:(r + 1) * BLK]
-
-
-def layer(places, stacked, pieces, weight_rows, weight_low, weight_turned, bias, cotangent, shards):
-    rows, _, width = stacked.shape
-    span, depth = pieces[0].shape
-    count, hid = cotangent.shape
-    return pl.pallas_call(
-        layer_kernel,
-        out_shape=(
-            jax.ShapeDtypeStruct((count, hid), jnp.float32),
-            jax.ShapeDtypeStruct((shards, 1, depth * hid // shards + LANES), jnp.float32),
-            jax.ShapeDtypeStruct((rows, 2 * BLK, 2 * depth), jnp.bfloat16),
-        ),
-        in_specs=[pl.BlockSpec(memory_space=pltpu.SMEM)] + vmem(1)
-        + [pl.BlockSpec(memory_space=pl.ANY)] * 6 + vmem(5),
-        out_specs=vmem(3),
-        scratch_shapes=[
-            pltpu.VMEM((6 * span, depth), jnp.float32),
-            pltpu.VMEM((2, width, 2 * depth), jnp.bfloat16),
-            pltpu.VMEM((count, depth), jnp.float32),
-            pltpu.SemaphoreType.DMA((6,)),
-        ],
-        compiler_params=params(16),
-        cost_estimate=pl.CostEstimate(flops=400_000_000, bytes_accessed=6_000_000, transcendentals=65536),
-        name="layer",
-    )(places, stacked, *pieces, weight_rows, weight_low, weight_turned, bias, cotangent)
-
-
-def spread_kernel(targets, turned, grads, other, mine, band, sems):
-    rows, width, _ = turned.shape
-    slots = width // BLK
-    half, depth = mine.shape
-    band[...] = jnp.zeros_like(band)
-    for r in range(rows):
         product = dot(turned[r], grads[r])
         product = product[:, :depth] + product[:, depth:]
         for k in range(slots):
-            start = pl.multiple_of(targets[r, k] * BLK, BLK)
-            where = pl.ds(start, BLK)
-            band[where, :] = band[where, :] + product[k * BLK:(k + 1) * BLK]
+            where = pl.ds(pl.multiple_of(targets[r, k] * BLK, BLK), BLK)
+            spread[where, :] = spread[where, :] + product[k * BLK:(k + 1) * BLK]
+    half = other.shape[0]
     copies = [
-        pltpu.make_async_copy(band.at[pl.ds(i * half, half)], piece, sems.at[i])
+        pltpu.make_async_copy(spread.at[pl.ds(i * half, half)], piece, out_sems.at[i])
         for i, piece in enumerate((other, mine))
     ]
     for copy in copies:
@@ -204,21 +172,55 @@
         copy.wait()
 
 
-def spread(targets, turned, grads, half, depth):
-    piece = jax.ShapeDtypeStruct((half, depth), jnp.float32)
-    return pl.pallas_call(
-        spread_kernel,
-        out_shape=(piece, piece),
-        in_specs=[pl.BlockSpec(memory_space=pltpu.SMEM)] + vmem(2),
-        out_specs=[pl.BlockSpec(memory_space=pl.ANY)] * 2,
+def layer(places, targets, stacked, turned, pieces, weight_rows, weight_low, weight_turned, bias, cotangent, shards):
+    rows, _, width = stacked.shape
+    span, depth = pieces[0].shape
+    count, hid = cotangent.shape
+    return pl.pallas_call(
+        layer_kernel,
+        out_shape=(
+            jax.ShapeDtypeStruct((count, hid), jnp.float32),
+            jax.ShapeDtypeStruct((shards, 1, depth * hid // shards + LANES), jnp.float32),
+            jax.ShapeDtypeStruct((3 * span, depth), jnp.float32),
+            jax.ShapeDtypeStruct((3 * span, depth), jnp.float32),
+        ),
+        in_specs=[pl.BlockSpec(memory_space=pltpu.SMEM)] * 2 + vmem(2)
+        + [pl.BlockSpec(memory_space=pl.ANY)] * 6 + vmem(5),
+        out_specs=vmem(2) + [pl.BlockSpec(memory_space=pl.ANY)] * 2,
         scratch_shapes=[
-            pltpu.VMEM((2 * half, depth), jnp.float32),
+            pltpu.VMEM((6 * span, depth), jnp.float32),
+            pltpu.VMEM((6 * span, depth), jnp.float32),
+            pltpu.VMEM((2, width, 2 * depth), jnp.bfloat16),
+            pltpu.VMEM((count, depth), jnp.float32),
+            pltpu.VMEM((rows, 2 * BLK, 2 * depth), jnp.bfloat16),
+            pltpu.SemaphoreType.DMA((6,)),
             pltpu.SemaphoreType.DMA((2,)),
         ],
-        compiler_params=params(12),
-        cost_estimate=pl.CostEstimate(flops=300_000_000, bytes_accessed=5_000_000, transcendentals=0),
-        name="spread",
-    )(targets, turned, grads)
+        compiler_params=params(20),
+        cost_estimate=pl.CostEstimate(flops=700_000_000, bytes_accessed=11_000_000, transcendentals=65536),
+        name="layer",
+    )(places, targets, stacked, turned, *pieces, weight_rows, weight_low, weight_turned, bias, cotangent)
+
+
+def add_kernel(terms, from_core, before, own, after):
+    span = own.shape[0]
+    for part, out in enumerate((before, own, after)):
+        at = slice(part * span, (part + 1) * span)
+        out[...] = terms[at] + from_core[at]
+
+
+def add_parts(terms, from_core):
+    size, depth = terms.shape
+    piece = jax.ShapeDtypeStruct((size // 3, depth), terms.dtype)
+    return pl.pallas_call(
+        add_kernel,
+        out_shape=(piece, piece, piece),
+        in_specs=vmem(2),
+        out_specs=vmem(3),
+        compiler_params=params(8),
+        cost_estimate=pl.CostEstimate(flops=400_000, bytes_accessed=4_700_000, transcendentals=0),
+        name="add_parts",
+    )(terms, from_core)
 
 
 def sum_kernel(parts, *refs):
@@ -293,19 +295,17 @@
         counts, columns, blocks, weight
     )
     pieces = (before_other, own_other, after_other, before, own, after)
-    hidden, sums, grads = layer(
-        places, stacked, pieces, weight_rows, weight_low, weight_turned, bias[None], cotangent, shards
+    hidden, sums, to_other, to_mine = layer(
+        places, targets, stacked, turned, pieces, weight_rows, weight_low, weight_turned, bias[None], cotangent, shards
     )
 
-    to_other, to_mine = spread(targets, turned, grads, 3 * span, depth)
-    from_core = swap_cores(to_other)
-    from_after = along_wide(to_mine[:span] + from_core[:span], -1)
-    from_before = along_wide(to_mine[2 * span:] + from_core[2 * span:], 1)
+    to_before, to_own, to_after = add_parts(to_mine, swap_cores(to_other))
+    from_after = along_wide(to_before, -1)
+    from_before = along_wide(to_after, 1)
     shares = []
     for step in range(chips):
         chunk = slice(rows * step, rows * (step + 1))
-        at = slice(span + rows * step, span + rows * (step + 1))
-        share = to_mine[at] + from_core[at] + from_after[chunk] + from_before[chunk]
+        share = to_own[chunk] + from_after[chunk] + from_before[chunk]
         if step:
             share = lax.ppermute(share, "x", [(i, (i + step) % chips) for i in range(chips)])
         shares.append(share)

time: 130 us -> 131 us (level)
  Pallas kernels: 7.71 us -> 9.54 us
  other arithmetic: 4.26 us -> 2.69 us
    pallas_call x1, Pallas kernels: 2.95 us -> 5.3 us  [layer(): pl.pallas_call(layer_kernel, out_shape=(jax.ShapeDtypeStruct((count, hid)...]
    add x2 -> x1, other arithmetic: 2.59 us -> 1.09 us  [body(): share = to_own[chunk] + from_after[chunk] + from_before[chunk]]
  transfers between devices with their start and end apart: 14 -> 14, of which waited for: 4 -> 4; matrix products, arithmetic and copies ran while one was open for 3% -> 2% of each run, Pallas kernels for 1% -> 2%
where the time goes in v6:
time: 131 us
  starting transfers between devices  82 us (63%)
  waiting for transfers between devices  22 us (17%)
  blocking collectives  11.6 us (9%)
  Pallas kernels  9.54 us (7%)
  other arithmetic  2.69 us (2%)
  local copies, waits for them, and re-layouts  1.88 us (1%)
    ppermute x4, starting transfers between devices, swap_cores(): return lax.ppermute(value, 'core', [(0, 1), (1, 0)])  22.8 us
    all_to_all x1, starting transfers between devices, body(): scattered = lax.all_to_all(sums, GROUP, 0, 0)  18 us
    ppermute x4, starting transfers between devices, along_wide(): return lax.ppermute(value, WIDE, route)  12.4 us
    all_to_all x1, waiting for transfers between devices, body(): scattered = lax.all_to_all(sum_for_all(scattered, levels), 'far', 0, 0)  12.3 us
    all_to_all x1, blocking collectives, body(): own = lax.all_to_all(row_of_chips, 'x', 0, 0).reshape(span, depth)  11.6 us
    all_to_all x1, starting transfers between devices, body(): scattered = lax.all_to_all(sum_for_all(scattered, levels), 'far', 0, 0)  10.8 us
    all_to_all x1, starting transfers between devices, body(): lax.all_to_all(sum_for_all(scattered, shards, *shares[1:]), GROUP, 0, 0)  10.1 us
    ppermute x3, starting transfers between devices, body(): lax.ppermute(share, 'x', [(i, (i + step) % chips) for i in range(chips)])  7.93 us
  transfers between devices with their start and end apart: 14, of which 4 were waited for; matrix products, arithmetic and copies ran while one was open for 2% of the time, Pallas kernels for 2%

profile of v6, /device:TPU:1, one launch (start us, length us, event | category | flops | bytes accessed | tf_op | source)
XLA Modules:
  0.0 130.6 jit_solution(14466198174492673518)
XLA Ops:
  0.6 0.0 copy-start.3
  0.6 0.0 copy-start
  0.7 0.0 copy-start.6
  0.7 0.0 copy-start.4
  0.7 0.0 copy-start.2
  0.7 0.0 copy-start.5
  0.7 1.0 broadcast_in_dim.4
  1.7 11.6 %all_to_all.20 = f32[4,256,128]{2,1,0:T(8,128)S(1)} all-to-all(f32[4,256,128]{2,1,0:T(8,128)S(1)} %broadcast_in_dim.4), channel_id=1, replica_groups=mesh['y'=4,'far'=16,'near'=2,'x'=4,'core'=2] {'x'}, dimensions={0} | all-to-all | bytes 1048576 | tf_op jit(solution)/shard_map/all_to_all | solution.py:288
  13.3 1.3 collective-permute-start.3
  14.6 5.8 %collective-permute-start = (f32[1024,128]{1,0:T(8,128)S(1)}, f32[1024,128]{1,0:T(8,128)S(1)}, u32[]{:S(2)}, u32[]{:S(2)}) collective-permute-start(f32[1024,128]{1,0:T(8,128)S(1)} %bitcast.4), channel_id=1, source_target_pairs={{0,8},{8,16},{16,24},{24,32},{32,40},{40,48},{48,56},{56,64},{64,7... | collective-permute-start | bytes 1572872 | tf_op jit(solution)/shard_map/ppermute | solution.py:276
  20.4 13.7 %collective-permute-start.2 = (f32[1024,128]{1,0:T(8,128)S(1)}, f32[1024,128]{1,0:T(8,128)S(1)}, u32[]{:S(2)}, u32[]{:S(2)}) collective-permute-start(f32[1024,128]{1,0:T(8,128)S(1)} %bitcast.5), channel_id=1, source_target_pairs={{0,1},{1,0},{2,3},{3,2},{4,5},{5,4},{6,7},{7,6},{8,9},{9,8},{10,11... | collective-permute-start | bytes 1572872 | tf_op jit(solution)/shard_map/ppermute | solution.py:270
  34.2 0.0 collective-permute-done.3.p5
  34.2 5.2 %collective-permute-start.4 = (f32[1024,128]{1,0:T(8,128)S(1)}, f32[1024,128]{1,0:T(8,128)S(1)}, u32[]{:S(2)}, u32[]{:S(2)}) collective-permute-start(f32[1024,128]{1,0:T(8,128)S(1)} %collective-permute-done.3.p5), channel_id=1, source_target_pairs={{0,1},{1,0},{2,3},{3,2},{4,5},{5,4},{6,7},{7,6},{8,9},{9,8},{10,11... | collective-permute-start | bytes 1572872 | tf_op jit(solution)/shard_map/ppermute | solution.py:270
  39.3 0.0 collective-permute-done.p3
  39.4 1.9 %collective-permute-start.1 = (f32[1024,128]{1,0:T(8,128)S(1)}, f32[1024,128]{1,0:T(8,128)S(1)}, u32[]{:S(2)}, u32[]{:S(2)}) collective-permute-start(f32[1024,128]{1,0:T(8,128)S(1)} %collective-permute-done.p3), channel_id=1, source_target_pairs={{0,1},{1,0},{2,3},{3,2},{4,5},{5,4},{6,7},{7,6},{8,9},{9,8},{10,11... | collective-permute-start | bytes 1572872 | tf_op jit(solution)/shard_map/ppermute | solution.py:270
  41.3 0.0 copy-done.3
  41.3 0.0 copy-done
  41.3 0.0 copy-done.6
  41.3 0.0 copy-done.4
  41.3 0.9 prepare.1
  42.3 0.0 collective-permute-done.2.p1
  42.3 0.0 collective-permute-done.4.p2
  42.3 0.9 collective-permute-done.1.p0
  43.2 0.0 copy-done.2
  43.2 0.0 copy-done.5
  43.2 5.3 %layer.1 = (f32[256,256]{1,0:T(8,128)}, f32[64,1,640]{2,1,0:T(1,128)}, f32[3072,128]{1,0:T(8,128)}, f32[3072,128]{1,0:T(8,128)S(1)}) custom-call(s32[4,16]{1,0:T(4,128)S(1)} %get-tuple-element.20.places, s32[4,16]{1,0:T(4,128)S(1)} %get-tuple-element.21.targets, bf16[4,128,1024]{2,1,0:T(8,128)(2,1)S(1)} %get-tuple-element.22.stacked, ...), custom_call_target="tpu_custom_call" | custom-call | flops 700000000 | bytes 11000000 | tf_op jit(solution)/shard_map/layer/pallas_call | solution.py:179
  48.5 2.0 %collective-permute-start.5 = (f32[3072,128]{1,0:T(8,128)}, f32[3072,128]{1,0:T(8,128)S(1)}, u32[]{:S(2)}, u32[]{:S(2)}) collective-permute-start(f32[3072,128]{1,0:T(8,128)} %get-tuple-element.30), channel_id=1, source_target_pairs={{0,1},{1,0},{2,3},{3,2},{4,5},{5,4},{6,7},{7,6},{8,9},{9,8},{10,11... | collective-permute-start | bytes 4718600 | tf_op jit(solution)/shard_map/ppermute | solution.py:270
  50.5 18.0 %all-to-all-start.1 = ((f32[64,1,640]{2,1,0:T(1,128)}), f32[64,1,640]{2,1,0:T(1,128)S(1)}, u32[]{:S(2)}, u32[]{:S(2)}) async-start(f32[64,1,640]{2,1,0:T(1,128)} %get-tuple-element.28), calls=%async_computation.1 | async-start | bytes 327680 | tf_op jit(solution)/shard_map/all_to_all | solution.py:313
  68.5 0.0 collective-permute-done.5.from_core
  68.5 1.2 add_parts.1
  69.7 0.0 copy-start.1
  69.7 0.8 copy-done.1
  70.5 1.3 collective-permute-start.6
  71.8 4.0 %collective-permute-start.7 = (f32[1024,128]{1,0:T(8,128)}, f32[1024,128]{1,0:T(8,128)S(1)}, u32[]{:S(2)}, u32[]{:S(2)}) collective-permute-start(f32[1024,128]{1,0:T(8,128)} %get-tuple-element.33), channel_id=1, source_target_pairs={{0,8},{8,16},{16,24},{24,32},{32,40},{40,48},{48,56},{56,64},{64,7... | collective-permute-start | bytes 1572872 | tf_op jit(solution)/shard_map/ppermute | solution.py:276
  75.8 1.5 %all-to-all-done.1.parts = f32[64,1,640]{2,1,0:T(1,128)S(1)} async-done(((f32[64,1,640]{2,1,0:T(1,128)}), f32[64,1,640]{2,1,0:T(1,128)S(1)}, u32[]{:S(2)}, u32[]{:S(2)}) %all-to-all-start.1) | async-done | bytes 163872 | tf_op jit(solution)/shard_map/all_to_all | solution.py:313
  77.3 0.7 sum_for_all.2
  78.1 10.8 %all-to-all-start.2 = ((f32[16,1,640]{2,1,0:T(1,128)}), f32[16,1,640]{2,1,0:T(1,128)S(1)}, u32[]{:S(2)}, u32[]{:S(2)}) async-start(f32[16,1,640]{2,1,0:T(1,128)} %sum_for_all.2), calls=%async_computation.2 | async-start | bytes 81920 | tf_op jit(solution)/shard_map/all_to_all | solution.py:314
  88.9 0.0 collective-permute-done.6
  88.9 0.0 collective-permute-done.7
  88.9 1.1 slice_add_fusion.2
  90.0 3.0 %collective-permute-start.10 = (f32[256,128]{1,0:T(8,128)S(1)}, f32[256,128]{1,0:T(8,128)S(1)}, u32[]{:S(2)}, u32[]{:S(2)}) collective-permute-start(f32[256,128]{1,0:T(8,128)S(1)} %get-tuple-element.36), channel_id=1, source_target_pairs={{0,6},{2,0},{4,2},{6,4},{1,7},{3,1},{5,3},{7,5},{8,14},{10,8},{12,... | collective-permute-start | bytes 393224 | tf_op jit(solution)/shard_map/ppermute | solution.py:310
  93.0 2.9 %collective-permute-start.9 = (f32[256,128]{1,0:T(8,128)S(1)}, f32[256,128]{1,0:T(8,128)S(1)}, u32[]{:S(2)}, u32[]{:S(2)}) collective-permute-start(f32[256,128]{1,0:T(8,128)S(1)} %get-tuple-element.37), channel_id=1, source_target_pairs={{0,4},{2,6},{4,0},{6,2},{1,5},{3,7},{5,1},{7,3},{8,12},{10,14},{12... | collective-permute-start | bytes 393224 | tf_op jit(solution)/shard_map/ppermute | solution.py:310
  95.9 2.0 %collective-permute-start.8 = (f32[256,128]{1,0:T(8,128)S(1)}, f32[256,128]{1,0:T(8,128)S(1)}, u32[]{:S(2)}, u32[]{:S(2)}) collective-permute-start(f32[256,128]{1,0:T(8,128)S(1)} %get-tuple-element.38), channel_id=1, source_target_pairs={{0,2},{2,4},{4,6},{6,0},{1,3},{3,5},{5,7},{7,1},{8,10},{10,12},{12... | collective-permute-start | bytes 393224 | tf_op jit(solution)/shard_map/ppermute | solution.py:310
  97.9 12.3 %all-to-all-done.2.parts = f32[16,1,640]{2,1,0:T(1,128)S(1)} async-done(((f32[16,1,640]{2,1,0:T(1,128)}), f32[16,1,640]{2,1,0:T(1,128)S(1)}, u32[]{:S(2)}, u32[]{:S(2)}) %all-to-all-start.2) | async-done | bytes 40992 | tf_op jit(solution)/shard_map/all_to_all | solution.py:314
  110.3 0.0 collective-permute-done.10.refs_2_
  110.3 0.0 collective-permute-done.9.refs_1_
  110.3 0.0 collective-permute-done.8.refs_0_
  110.3 0.7 sum_for_all.3
  111.0 10.1 %all-to-all-start.3 = ((f32[64,1,640]{2,1,0:T(1,128)}), f32[64,1,640]{2,1,0:T(1,128)S(1)}, u32[]{:S(2)}, u32[]{:S(2)}) async-start(f32[64,1,640]{2,1,0:T(1,128)} %sum_for_all.3), calls=%async_computation.3 | async-start | bytes 327680 | tf_op jit(solution)/shard_map/all_to_all | solution.py:315
  121.1 1.6 %fusion.2 = f32[256,128]{1,0:T(8,128)} fusion(f32[256,128]{1,0:T(8,128)S(1)} %collective-permute-done.10.refs_2_, f32[256,128]{1,0:T(8,128)S(1)} %collective-permute-done.9.refs_1_, f32[256,128]{1,0:T(8,128)S(1)} %collective-permute-done.8.refs_0_, f32[1024,128]{1,0:T(8,128)S(1)} %collective-permute-done.7, f32[1024,128]{1,0:T(8,128)S(1)} %collective-permute-done.6, ...), kind=kLoop, calls=%fused_computation.3 | loop fusion | flops 163840 | bytes 917504 | tf_op jit(solution)/shard_map/add | solution.py:312
  122.7 7.2 %all-to-all-done.3.parts = f32[64,1,640]{2,1,0:T(1,128)S(1)} async-done(((f32[64,1,640]{2,1,0:T(1,128)}), f32[64,1,640]{2,1,0:T(1,128)S(1)}, u32[]{:S(2)}, u32[]{:S(2)}) %all-to-all-start.3) | async-done | bytes 163872 | tf_op jit(solution)/shard_map/all_to_all | solution.py:315
  129.9 0.7 unpack.1
Async XLA Ops:
  0.6 40.7 %copy-start.3 = (f32[128,256]{1,0:T(8,128)S(1)}, f32[128,256]{1,0:T(8,128)}, u32[]{:S(2)}) copy-start(f32[128,256]{1,0:T(8,128)} %weight.1) | copy-start | bytes 393220
  0.6 40.7 %copy-start = (f32[4,64,1024]{2,1,0:T(8,128)S(1)}, f32[4,64,1024]{2,1,0:T(8,128)}, u32[]{:S(2)}) copy-start(f32[4,64,1024]{2,1,0:T(8,128)} %blocks.1) | copy-start | bytes 3145732
  0.7 40.7 %copy-start.6 = (s32[4]{0:T(128)S(1)}, s32[4]{0:T(128)}, u32[]{:S(2)}) copy-start(s32[4]{0:T(128)} %counts.1) | copy-start | bytes 52
  0.7 40.7 %copy-start.4 = (s32[4,16]{1,0:T(4,128)S(1)}, s32[4,16]{1,0:T(4,128)}, u32[]{:S(2)}) copy-start(s32[4,16]{1,0:T(4,128)} %columns.1) | copy-start | bytes 772
  0.7 42.5 %copy-start.2 = (f32[256,256]{1,0:T(8,128)S(1)}, f32[256,256]{1,0:T(8,128)}, u32[]{:S(2)}) copy-start(f32[256,256]{1,0:T(8,128)} %cotangent.1) | copy-start | bytes 786436
  0.7 42.5 %copy-start.5 = (f32[256]{0:T(256)S(1)}, f32[256]{0:T(256)}, u32[]{:S(2)}) copy-start(f32[256]{0:T(256)} %param.12) | copy-start | bytes 3076
  13.3 20.9 %collective-permute-start.3 = (f32[1024,128]{1,0:T(8,128)S(1)}, f32[1024,128]{1,0:T(8,128)S(1)}, u32[]{:S(2)}, u32[]{:S(2)}) collective-permute-start(f32[1024,128]{1,0:T(8,128)S(1)} %bitcast.3), channel_id=1, source_target_pairs={{8,0},{16,8},{24,16},{32,24},{40,32},{48,40},{56,48},{64,56},{72,6... | collective-permute-start | bytes 1572872 | tf_op jit(solution)/shard_map/ppermute | solution.py:276
  14.6 24.7 %collective-permute-start = (f32[1024,128]{1,0:T(8,128)S(1)}, f32[1024,128]{1,0:T(8,128)S(1)}, u32[]{:S(2)}, u32[]{:S(2)}) collective-permute-start(f32[1024,128]{1,0:T(8,128)S(1)} %bitcast.4), channel_id=1, source_target_pairs={{0,8},{8,16},{16,24},{24,32},{32,40},{40,48},{48,56},{56,64},{64,7... | collective-permute-start | bytes 1572872 | tf_op jit(solution)/shard_map/ppermute | solution.py:276
  20.4 21.8 %collective-permute-start.2 = (f32[1024,128]{1,0:T(8,128)S(1)}, f32[1024,128]{1,0:T(8,128)S(1)}, u32[]{:S(2)}, u32[]{:S(2)}) collective-permute-start(f32[1024,128]{1,0:T(8,128)S(1)} %bitcast.5), channel_id=1, source_target_pairs={{0,1},{1,0},{2,3},{3,2},{4,5},{5,4},{6,7},{7,6},{8,9},{9,8},{10,11... | collective-permute-start | bytes 1572872 | tf_op jit(solution)/shard_map/ppermute | solution.py:270
  34.2 8.1 %collective-permute-start.4 = (f32[1024,128]{1,0:T(8,128)S(1)}, f32[1024,128]{1,0:T(8,128)S(1)}, u32[]{:S(2)}, u32[]{:S(2)}) collective-permute-start(f32[1024,128]{1,0:T(8,128)S(1)} %collective-permute-done.3.p5), channel_id=1, source_target_pairs={{0,1},{1,0},{2,3},{3,2},{4,5},{5,4},{6,7},{7,6},{8,9},{9,8},{10,11... | collective-permute-start | bytes 1572872 | tf_op jit(solution)/shard_map/ppermute | solution.py:270
  39.4 3.8 %collective-permute-start.1 = (f32[1024,128]{1,0:T(8,128)S(1)}, f32[1024,128]{1,0:T(8,128)S(1)}, u32[]{:S(2)}, u32[]{:S(2)}) collective-permute-start(f32[1024,128]{1,0:T(8,128)S(1)} %collective-permute-done.p3), channel_id=1, source_target_pairs={{0,1},{1,0},{2,3},{3,2},{4,5},{5,4},{6,7},{7,6},{8,9},{9,8},{10,11... | collective-permute-start | bytes 1572872 | tf_op jit(solution)/shard_map/ppermute | solution.py:270
  48.5 20.0 %collective-permute-start.5 = (f32[3072,128]{1,0:T(8,128)}, f32[3072,128]{1,0:T(8,128)S(1)}, u32[]{:S(2)}, u32[]{:S(2)}) collective-permute-start(f32[3072,128]{1,0:T(8,128)} %get-tuple-element.30), channel_id=1, source_target_pairs={{0,1},{1,0},{2,3},{3,2},{4,5},{5,4},{6,7},{7,6},{8,9},{9,8},{10,11... | collective-permute-start | bytes 4718600 | tf_op jit(solution)/shard_map/ppermute | solution.py:270
  50.5 26.8 %all-to-all-start.1 = ((f32[64,1,640]{2,1,0:T(1,128)}), f32[64,1,640]{2,1,0:T(1,128)S(1)}, u32[]{:S(2)}, u32[]{:S(2)}) async-start(f32[64,1,640]{2,1,0:T(1,128)} %get-tuple-element.28), calls=%async_computation.1 | async-start | bytes 327680 | tf_op jit(solution)/shard_map/all_to_all | solution.py:313
  69.7 0.8 copy-start.1
  70.5 18.4 %collective-permute-start.6 = (f32[1024,128]{1,0:T(8,128)}, f32[1024,128]{1,0:T(8,128)S(1)}, u32[]{:S(2)}, u32[]{:S(2)}) collective-permute-start(f32[1024,128]{1,0:T(8,128)} %get-tuple-element.32), channel_id=1, source_target_pairs={{8,0},{16,8},{24,16},{32,24},{40,32},{48,40},{56,48},{64,56},{72,6... | collective-permute-start | bytes 1572872 | tf_op jit(solution)/shard_map/ppermute | solution.py:276
  71.8 17.1 %collective-permute-start.7 = (f32[1024,128]{1,0:T(8,128)}, f32[1024,128]{1,0:T(8,128)S(1)}, u32[]{:S(2)}, u32[]{:S(2)}) collective-permute-start(f32[1024,128]{1,0:T(8,128)} %get-tuple-element.33), channel_id=1, source_target_pairs={{0,8},{8,16},{16,24},{24,32},{32,40},{40,48},{48,56},{56,64},{64,7... | collective-permute-start | bytes 1572872 | tf_op jit(solution)/shard_map/ppermute | solution.py:276
  78.1 32.2 %all-to-all-start.2 = ((f32[16,1,640]{2,1,0:T(1,128)}), f32[16,1,640]{2,1,0:T(1,128)S(1)}, u32[]{:S(2)}, u32[]{:S(2)}) async-start(f32[16,1,640]{2,1,0:T(1,128)} %sum_for_all.2), calls=%async_computation.2 | async-start | bytes 81920 | tf_op jit(solution)/shard_map/all_to_all | solution.py:314
  90.0 20.3 %collective-permute-start.10 = (f32[256,128]{1,0:T(8,128)S(1)}, f32[256,128]{1,0:T(8,128)S(1)}, u32[]{:S(2)}, u32[]{:S(2)}) collective-permute-start(f32[256,128]{1,0:T(8,128)S(1)} %get-tuple-element.36), channel_id=1, source_target_pairs={{0,6},{2,0},{4,2},{6,4},{1,7},{3,1},{5,3},{7,5},{8,14},{10,8},{12,... | collective-permute-start | bytes 393224 | tf_op jit(solution)/shard_map/ppermute | solution.py:310
  93.0 17.3 %collective-permute-start.9 = (f32[256,128]{1,0:T(8,128)S(1)}, f32[256,128]{1,0:T(8,128)S(1)}, u32[]{:S(2)}, u32[]{:S(2)}) collective-permute-start(f32[256,128]{1,0:T(8,128)S(1)} %get-tuple-element.37), channel_id=1, source_target_pairs={{0,4},{2,6},{4,0},{6,2},{1,5},{3,7},{5,1},{7,3},{8,12},{10,14},{12... | collective-permute-start | bytes 393224 | tf_op jit(solution)/shard_map/ppermute | solution.py:310
  95.9 14.4 %collective-permute-start.8 = (f32[256,128]{1,0:T(8,128)S(1)}, f32[256,128]{1,0:T(8,128)S(1)}, u32[]{:S(2)}, u32[]{:S(2)}) collective-permute-start(f32[256,128]{1,0:T(8,128)S(1)} %get-tuple-element.38), channel_id=1, source_target_pairs={{0,2},{2,4},{4,6},{6,0},{1,3},{3,5},{5,7},{7,1},{8,10},{10,12},{12... | collective-permute-start | bytes 393224 | tf_op jit(solution)/shard_map/ppermute | solution.py:310
  111.0 18.9 %all-to-all-start.3 = ((f32[64,1,640]{2,1,0:T(1,128)}), f32[64,1,640]{2,1,0:T(1,128)S(1)}, u32[]{:S(2)}, u32[]{:S(2)}) async-start(f32[64,1,640]{2,1,0:T(1,128)} %sum_for_all.3), calls=%async_computation.3 | async-start | bytes 327680 | tf_op jit(solution)/shard_map/all_to_all | solution.py:315

commit v7 on v6

--- a/solution.py
+++ b/solution.py
@@ -88,7 +88,7 @@
         ),
         in_specs=[pl.BlockSpec(memory_space=pltpu.SMEM)] + vmem(3),
         out_specs=vmem(7),
-        compiler_params=params(12),
+        compiler_params=params(6),
         cost_estimate=pl.CostEstimate(flops=2_000_000, bytes_accessed=4_000_000, transcendentals=0),
         name="prepare",
     )(counts, columns, blocks, weight)
@@ -196,31 +196,10 @@
             pltpu.SemaphoreType.DMA((6,)),
             pltpu.SemaphoreType.DMA((2,)),
         ],
-        compiler_params=params(20),
+        compiler_params=params(14),
         cost_estimate=pl.CostEstimate(flops=700_000_000, bytes_accessed=11_000_000, transcendentals=65536),
         name="layer",
     )(places, targets, stacked, turned, *pieces, weight_rows, weight_low, weight_turned, bias, cotangent)
-
-
-def add_kernel(terms, from_core, before, own, after):
-    span = own.shape[0]
-    for part, out in enumerate((before, own, after)):
-        at = slice(part * span, (part + 1) * span)
-        out[...] = terms[at] + from_core[at]
-
-
-def add_parts(terms, from_core):
-    size, depth = terms.shape
-    piece = jax.ShapeDtypeStruct((size // 3, depth), terms.dtype)
-    return pl.pallas_call(
-        add_kernel,
-        out_shape=(piece, piece, piece),
-        in_specs=vmem(2),
-        out_specs=vmem(3),
-        compiler_params=params(8),
-        cost_estimate=pl.CostEstimate(flops=400_000, bytes_accessed=4_700_000, transcendentals=0),
-        name="add_parts",
-    )(terms, from_core)
 
 
 def sum_kernel(parts, *refs):
@@ -299,13 +278,14 @@
         places, targets, stacked, turned, pieces, weight_rows, weight_low, weight_turned, bias[None], cotangent, shards
     )
 
-    to_before, to_own, to_after = add_parts(to_mine, swap_cores(to_other))
-    from_after = along_wide(to_before, -1)
-    from_before = along_wide(to_after, 1)
+    from_core = swap_cores(to_other)
+    from_after = along_wide(to_mine[:span] + from_core[:span], -1)
+    from_before = along_wide(to_mine[2 * span:] + from_core[2 * span:], 1)
     shares = []
     for step in range(chips):
         chunk = slice(rows * step, rows * (step + 1))
-        share = to_own[chunk] + from_after[chunk] + from_before[chunk]
+        at = slice(span + rows * step, span + rows * (step + 1))
+        share = to_mine[at] + from_core[at] + from_after[chunk] + from_before[chunk]
         if step:
             share = lax.ppermute(share, "x", [(i, (i + step) % chips) for i in range(chips)])
         shares.append(share)

time: 131 us -> 130 us (level)
  Pallas kernels: 9.54 us -> 7.39 us
  other arithmetic: 2.69 us -> 4.26 us
    add x1 -> x2, other arithmetic: 1.09 us -> 2.59 us  [the longest x1 1.31 us: body(): from_after = along_wide(to_mine[:span] + from_core[:span], -1)]
  transfers between devices with their start and end apart: 14 -> 14, of which waited for: 4 -> 4; matrix products, arithmetic and copies ran while one was open for 2% -> 3% of each run, Pallas kernels for 2% -> 1%
where the time goes in v7:
time: 130 us; the launch traced here: 129 us
  starting transfers between devices  82.2 us (63%)
  waiting for transfers between devices  21.5 us (17%)
  blocking collectives  11.6 us (9%)
  Pallas kernels  7.39 us (6%)
  other arithmetic  4.26 us (3%)
    ppermute x4, starting transfers between devices, swap_cores(): return lax.ppermute(value, 'core', [(0, 1), (1, 0)])  22.8 us
    all_to_all x1, starting transfers between devices, body(): scattered = lax.all_to_all(sums, GROUP, 0, 0)  18 us
    ppermute x4, starting transfers between devices, along_wide(): return lax.ppermute(value, WIDE, route)  13.2 us
    all_to_all x1, waiting for transfers between devices, body(): scattered = lax.all_to_all(sum_for_all(scattered, levels), 'far', 0, 0)  12 us
    all_to_all x1, blocking collectives, body(): own = lax.all_to_all(row_of_chips, 'x', 0, 0).reshape(span, depth)  11.6 us
    all_to_all x1, starting transfers between devices, body(): scattered = lax.all_to_all(sum_for_all(scattered, levels), 'far', 0, 0)  10.8 us
    all_to_all x1, starting transfers between devices, body(): lax.all_to_all(sum_for_all(scattered, shards, *shares[1:]), GROUP, 0, 0)  9.62 us
    ppermute x3, starting transfers between devices, body(): lax.ppermute(share, 'x', [(i, (i + step) % chips) for i in range(chips)])  7.82 us
  transfers between devices with their start and end apart: 14, of which 4 were waited for; matrix products, arithmetic and copies ran while one was open for 3% of the time, Pallas kernels for 1%

profile of v7, /device:TPU:1, one launch (start us, length us, event | category | flops | bytes accessed | tf_op | source)
XLA Modules:
  0.0 129.0 jit_solution(3627581124772179910)
XLA Ops:
  0.6 0.0 copy-start.2
  0.6 0.0 copy-start
  0.7 0.0 copy-start.5
  0.7 0.0 copy-start.3
  0.7 0.0 copy-start.1
  0.7 0.0 copy-start.4
  0.7 1.0 broadcast_in_dim.4
  1.7 11.6 %all_to_all.20 = f32[4,256,128]{2,1,0:T(8,128)S(1)} all-to-all(f32[4,256,128]{2,1,0:T(8,128)S(1)} %broadcast_in_dim.4), channel_id=1, replica_groups=mesh['y'=4,'far'=16,'near'=2,'x'=4,'core'=2] {'x'}, dimensions={0} | all-to-all | bytes 1048576 | tf_op jit(solution)/shard_map/all_to_all | solution.py:267
  13.3 1.3 collective-permute-start.3
  14.6 5.8 %collective-permute-start = (f32[1024,128]{1,0:T(8,128)S(1)}, f32[1024,128]{1,0:T(8,128)S(1)}, u32[]{:S(2)}, u32[]{:S(2)}) collective-permute-start(f32[1024,128]{1,0:T(8,128)S(1)} %bitcast.4), channel_id=1, source_target_pairs={{0,8},{8,16},{16,24},{24,32},{32,40},{40,48},{48,56},{56,64},{64,7... | collective-permute-start | bytes 1572872 | tf_op jit(solution)/shard_map/ppermute | solution.py:255
  20.4 13.7 %collective-permute-start.2 = (f32[1024,128]{1,0:T(8,128)S(1)}, f32[1024,128]{1,0:T(8,128)S(1)}, u32[]{:S(2)}, u32[]{:S(2)}) collective-permute-start(f32[1024,128]{1,0:T(8,128)S(1)} %bitcast.5), channel_id=1, source_target_pairs={{0,1},{1,0},{2,3},{3,2},{4,5},{5,4},{6,7},{7,6},{8,9},{9,8},{10,11... | collective-permute-start | bytes 1572872 | tf_op jit(solution)/shard_map/ppermute | solution.py:249
  34.2 0.0 collective-permute-done.3.p5
  34.2 5.2 %collective-permute-start.4 = (f32[1024,128]{1,0:T(8,128)S(1)}, f32[1024,128]{1,0:T(8,128)S(1)}, u32[]{:S(2)}, u32[]{:S(2)}) collective-permute-start(f32[1024,128]{1,0:T(8,128)S(1)} %collective-permute-done.3.p5), channel_id=1, source_target_pairs={{0,1},{1,0},{2,3},{3,2},{4,5},{5,4},{6,7},{7,6},{8,9},{9,8},{10,11... | collective-permute-start | bytes 1572872 | tf_op jit(solution)/shard_map/ppermute | solution.py:249
  39.3 0.0 collective-permute-done.p3
  39.4 1.9 %collective-permute-start.1 = (f32[1024,128]{1,0:T(8,128)S(1)}, f32[1024,128]{1,0:T(8,128)S(1)}, u32[]{:S(2)}, u32[]{:S(2)}) collective-permute-start(f32[1024,128]{1,0:T(8,128)S(1)} %collective-permute-done.p3), channel_id=1, source_target_pairs={{0,1},{1,0},{2,3},{3,2},{4,5},{5,4},{6,7},{7,6},{8,9},{9,8},{10,11... | collective-permute-start | bytes 1572872 | tf_op jit(solution)/shard_map/ppermute | solution.py:249
  41.3 0.0 copy-done.2
  41.3 0.0 copy-done
  41.3 0.0 copy-done.5
  41.3 0.0 copy-done.3
  41.3 0.9 prepare.1
  42.3 0.0 collective-permute-done.2.p1
  42.3 0.0 collective-permute-done.4.p2
  42.3 0.9 collective-permute-done.1.p0
  43.2 0.0 copy-done.1
  43.2 0.0 copy-done.4
  43.2 4.3 %layer.1 = (f32[256,256]{1,0:T(8,128)}, f32[64,1,640]{2,1,0:T(1,128)}, f32[3072,128]{1,0:T(8,128)S(1)}, f32[3072,128]{1,0:T(8,128)S(1)}) custom-call(s32[4,16]{1,0:T(4,128)S(1)} %get-tuple-element.17.places, s32[4,16]{1,0:T(4,128)S(1)} %get-tuple-element.18.targets, bf16[4,128,1024]{2,1,0:T(8,128)(2,1)S(1)} %get-tuple-element.19.stacked, ...), custom_call_target="tpu_custom_call" | custom-call | flops 700000000 | bytes 11000000 | tf_op jit(solution)/shard_map/layer/pallas_call | solution.py:179
  47.5 2.0 %collective-permute-start.5 = (f32[3072,128]{1,0:T(8,128)S(1)}, f32[3072,128]{1,0:T(8,128)}, u32[]{:S(2)}, u32[]{:S(2)}) collective-permute-start(f32[3072,128]{1,0:T(8,128)S(1)} %get-tuple-element.27), channel_id=1, source_target_pairs={{0,1},{1,0},{2,3},{3,2},{4,5},{5,4},{6,7},{7,6},{8,9},{9,8},{10,11... | collective-permute-start | bytes 4718600 | tf_op jit(solution)/shard_map/ppermute | solution.py:249
  49.6 18.0 %all-to-all-start.1 = ((f32[64,1,640]{2,1,0:T(1,128)}), f32[64,1,640]{2,1,0:T(1,128)S(1)}, u32[]{:S(2)}, u32[]{:S(2)}) async-start(f32[64,1,640]{2,1,0:T(1,128)} %get-tuple-element.25), calls=%async_computation.1 | async-start | bytes 327680 | tf_op jit(solution)/shard_map/all_to_all | solution.py:293
  67.5 0.0 collective-permute-done.5
  67.5 1.3 %slice_add_fusion.1 = (f32[1024,128]{1,0:T(8,128)S(1)}, f32[1024,128]{1,0:T(8,128)S(1)}) fusion(f32[3072,128]{1,0:T(8,128)} %collective-permute-done.5, f32[3072,128]{1,0:T(8,128)S(1)} %get-tuple-element.26), kind=kLoop, calls=%fused_computation.1 | loop fusion | flops 262144 | bytes 3145728 | tf_op jit(solution)/shard_map/add | solution.py:282
  68.9 1.3 %collective-permute-start.6 = (f32[1024,128]{1,0:T(8,128)S(1)}, f32[1024,128]{1,0:T(8,128)S(1)}, u32[]{:S(2)}, u32[]{:S(2)}) collective-permute-start(f32[1024,128]{1,0:T(8,128)S(1)} %get-tuple-element.33), channel_id=1, source_target_pairs={{8,0},{16,8},{24,16},{32,24},{40,32},{48,40},{56,48},{64,56},{72,6... | collective-permute-start | bytes 1572872 | tf_op jit(solution)/shard_map/ppermute | solution.py:255
  70.2 4.8 %collective-permute-start.7 = (f32[1024,128]{1,0:T(8,128)S(1)}, f32[1024,128]{1,0:T(8,128)}, u32[]{:S(2)}, u32[]{:S(2)}) collective-permute-start(f32[1024,128]{1,0:T(8,128)S(1)} %get-tuple-element.34), channel_id=1, source_target_pairs={{0,8},{8,16},{16,24},{24,32},{32,40},{40,48},{48,56},{56,64},{64,7... | collective-permute-start | bytes 1572872 | tf_op jit(solution)/shard_map/ppermute | solution.py:255
  74.9 1.4 %all-to-all-done.1.parts = f32[64,1,640]{2,1,0:T(1,128)S(1)} async-done(((f32[64,1,640]{2,1,0:T(1,128)}), f32[64,1,640]{2,1,0:T(1,128)S(1)}, u32[]{:S(2)}, u32[]{:S(2)}) %all-to-all-start.1) | async-done | bytes 163872 | tf_op jit(solution)/shard_map/all_to_all | solution.py:293
  76.4 0.7 sum_for_all.2
  77.1 10.8 %all-to-all-start.2 = ((f32[16,1,640]{2,1,0:T(1,128)}), f32[16,1,640]{2,1,0:T(1,128)S(1)}, u32[]{:S(2)}, u32[]{:S(2)}) async-start(f32[16,1,640]{2,1,0:T(1,128)} %sum_for_all.2), calls=%async_computation.2 | async-start | bytes 81920 | tf_op jit(solution)/shard_map/all_to_all | solution.py:294
  87.9 0.0 collective-permute-done.6
  87.9 0.0 collective-permute-done.7
  87.9 1.3 slice_add_fusion.5
  89.2 2.9 %collective-permute-start.10 = (f32[256,128]{1,0:T(8,128)S(1)}, f32[256,128]{1,0:T(8,128)S(1)}, u32[]{:S(2)}, u32[]{:S(2)}) collective-permute-start(f32[256,128]{1,0:T(8,128)S(1)} %get-tuple-element.30), channel_id=1, source_target_pairs={{0,6},{2,0},{4,2},{6,4},{1,7},{3,1},{5,3},{7,5},{8,14},{10,8},{12,... | collective-permute-start | bytes 393224 | tf_op jit(solution)/shard_map/ppermute | solution.py:290
  92.1 3.0 %collective-permute-start.9 = (f32[256,128]{1,0:T(8,128)S(1)}, f32[256,128]{1,0:T(8,128)S(1)}, u32[]{:S(2)}, u32[]{:S(2)}) collective-permute-start(f32[256,128]{1,0:T(8,128)S(1)} %get-tuple-element.31), channel_id=1, source_target_pairs={{0,4},{2,6},{4,0},{6,2},{1,5},{3,7},{5,1},{7,3},{8,12},{10,14},{12... | collective-permute-start | bytes 393224 | tf_op jit(solution)/shard_map/ppermute | solution.py:290
  95.1 1.9 %collective-permute-start.8 = (f32[256,128]{1,0:T(8,128)S(1)}, f32[256,128]{1,0:T(8,128)S(1)}, u32[]{:S(2)}, u32[]{:S(2)}) collective-permute-start(f32[256,128]{1,0:T(8,128)S(1)} %get-tuple-element.32), channel_id=1, source_target_pairs={{0,2},{2,4},{4,6},{6,0},{1,3},{3,5},{5,7},{7,1},{8,10},{10,12},{12... | collective-permute-start | bytes 393224 | tf_op jit(solution)/shard_map/ppermute | solution.py:290
  97.1 12.0 %all-to-all-done.2.parts = f32[16,1,640]{2,1,0:T(1,128)S(1)} async-done(((f32[16,1,640]{2,1,0:T(1,128)}), f32[16,1,640]{2,1,0:T(1,128)S(1)}, u32[]{:S(2)}, u32[]{:S(2)}) %all-to-all-start.2) | async-done | bytes 40992 | tf_op jit(solution)/shard_map/all_to_all | solution.py:294
  109.1 0.0 collective-permute-done.10.refs_2_
  109.1 0.0 collective-permute-done.9.refs_1_
  109.1 0.0 collective-permute-done.8.refs_0_
  109.1 0.7 sum_for_all.3
  109.8 9.6 %all-to-all-start.3 = ((f32[64,1,640]{2,1,0:T(1,128)}), f32[64,1,640]{2,1,0:T(1,128)S(1)}, u32[]{:S(2)}, u32[]{:S(2)}) async-start(f32[64,1,640]{2,1,0:T(1,128)} %sum_for_all.3), calls=%async_computation.3 | async-start | bytes 327680 | tf_op jit(solution)/shard_map/all_to_all | solution.py:295
  119.4 1.7 %fusion.2 = f32[256,128]{1,0:T(8,128)} fusion(f32[256,128]{1,0:T(8,128)S(1)} %collective-permute-done.10.refs_2_, f32[256,128]{1,0:T(8,128)S(1)} %collective-permute-done.9.refs_1_, f32[256,128]{1,0:T(8,128)S(1)} %collective-permute-done.8.refs_0_, f32[1024,128]{1,0:T(8,128)} %collective-permute-done.7, f32[1024,128]{1,0:T(8,128)S(1)} %collective-permute-done.6, ...), kind=kLoop, calls=%fused_computation.5 | loop fusion | flops 196608 | bytes 1048576 | tf_op jit(solution)/shard_map/add | solution.py:292
  121.1 7.2 %all-to-all-done.3.parts = f32[64,1,640]{2,1,0:T(1,128)S(1)} async-done(((f32[64,1,640]{2,1,0:T(1,128)}), f32[64,1,640]{2,1,0:T(1,128)S(1)}, u32[]{:S(2)}, u32[]{:S(2)}) %all-to-all-start.3) | async-done | bytes 163872 | tf_op jit(solution)/shard_map/all_to_all | solution.py:295
  128.3 0.7 unpack.1
Async XLA Ops:
  0.6 40.7 %copy-start.2 = (f32[128,256]{1,0:T(8,128)S(1)}, f32[128,256]{1,0:T(8,128)}, u32[]{:S(2)}) copy-start(f32[128,256]{1,0:T(8,128)} %weight.1) | copy-start | bytes 393220
  0.6 40.7 %copy-start = (f32[4,64,1024]{2,1,0:T(8,128)S(1)}, f32[4,64,1024]{2,1,0:T(8,128)}, u32[]{:S(2)}) copy-start(f32[4,64,1024]{2,1,0:T(8,128)} %blocks.1) | copy-start | bytes 3145732
  0.7 40.7 %copy-start.5 = (s32[4]{0:T(128)S(1)}, s32[4]{0:T(128)}, u32[]{:S(2)}) copy-start(s32[4]{0:T(128)} %counts.1) | copy-start | bytes 52
  0.7 40.7 %copy-start.3 = (s32[4,16]{1,0:T(4,128)S(1)}, s32[4,16]{1,0:T(4,128)}, u32[]{:S(2)}) copy-start(s32[4,16]{1,0:T(4,128)} %columns.1) | copy-start | bytes 772
  0.7 42.5 %copy-start.1 = (f32[256,256]{1,0:T(8,128)S(1)}, f32[256,256]{1,0:T(8,128)}, u32[]{:S(2)}) copy-start(f32[256,256]{1,0:T(8,128)} %cotangent.1) | copy-start | bytes 786436
  0.7 42.5 %copy-start.4 = (f32[256]{0:T(256)S(1)}, f32[256]{0:T(256)}, u32[]{:S(2)}) copy-start(f32[256]{0:T(256)} %param.12) | copy-start | bytes 3076
  13.3 20.9 %collective-permute-start.3 = (f32[1024,128]{1,0:T(8,128)S(1)}, f32[1024,128]{1,0:T(8,128)S(1)}, u32[]{:S(2)}, u32[]{:S(2)}) collective-permute-start(f32[1024,128]{1,0:T(8,128)S(1)} %bitcast.3), channel_id=1, source_target_pairs={{8,0},{16,8},{24,16},{32,24},{40,32},{48,40},{56,48},{64,56},{72,6... | collective-permute-start | bytes 1572872 | tf_op jit(solution)/shard_map/ppermute | solution.py:255
  14.6 24.7 %collective-permute-start = (f32[1024,128]{1,0:T(8,128)S(1)}, f32[1024,128]{1,0:T(8,128)S(1)}, u32[]{:S(2)}, u32[]{:S(2)}) collective-permute-start(f32[1024,128]{1,0:T(8,128)S(1)} %bitcast.4), channel_id=1, source_target_pairs={{0,8},{8,16},{16,24},{24,32},{32,40},{40,48},{48,56},{56,64},{64,7... | collective-permute-start | bytes 1572872 | tf_op jit(solution)/shard_map/ppermute | solution.py:255
  20.4 21.8 %collective-permute-start.2 = (f32[1024,128]{1,0:T(8,128)S(1)}, f32[1024,128]{1,0:T(8,128)S(1)}, u32[]{:S(2)}, u32[]{:S(2)}) collective-permute-start(f32[1024,128]{1,0:T(8,128)S(1)} %bitcast.5), channel_id=1, source_target_pairs={{0,1},{1,0},{2,3},{3,2},{4,5},{5,4},{6,7},{7,6},{8,9},{9,8},{10,11... | collective-permute-start | bytes 1572872 | tf_op jit(solution)/shard_map/ppermute | solution.py:249
  34.2 8.1 %collective-permute-start.4 = (f32[1024,128]{1,0:T(8,128)S(1)}, f32[1024,128]{1,0:T(8,128)S(1)}, u32[]{:S(2)}, u32[]{:S(2)}) collective-permute-start(f32[1024,128]{1,0:T(8,128)S(1)} %collective-permute-done.3.p5), channel_id=1, source_target_pairs={{0,1},{1,0},{2,3},{3,2},{4,5},{5,4},{6,7},{7,6},{8,9},{9,8},{10,11... | collective-permute-start | bytes 1572872 | tf_op jit(solution)/shard_map/ppermute | solution.py:249
  39.4 3.8 %collective-permute-start.1 = (f32[1024,128]{1,0:T(8,128)S(1)}, f32[1024,128]{1,0:T(8,128)S(1)}, u32[]{:S(2)}, u32[]{:S(2)}) collective-permute-start(f32[1024,128]{1,0:T(8,128)S(1)} %collective-permute-done.p3), channel_id=1, source_target_pairs={{0,1},{1,0},{2,3},{3,2},{4,5},{5,4},{6,7},{7,6},{8,9},{9,8},{10,11... | collective-permute-start | bytes 1572872 | tf_op jit(solution)/shard_map/ppermute | solution.py:249
  47.5 20.0 %collective-permute-start.5 = (f32[3072,128]{1,0:T(8,128)S(1)}, f32[3072,128]{1,0:T(8,128)}, u32[]{:S(2)}, u32[]{:S(2)}) collective-permute-start(f32[3072,128]{1,0:T(8,128)S(1)} %get-tuple-element.27), channel_id=1, source_target_pairs={{0,1},{1,0},{2,3},{3,2},{4,5},{5,4},{6,7},{7,6},{8,9},{9,8},{10,11... | collective-permute-start | bytes 4718600 | tf_op jit(solution)/shard_map/ppermute | solution.py:249
  49.6 26.8 %all-to-all-start.1 = ((f32[64,1,640]{2,1,0:T(1,128)}), f32[64,1,640]{2,1,0:T(1,128)S(1)}, u32[]{:S(2)}, u32[]{:S(2)}) async-start(f32[64,1,640]{2,1,0:T(1,128)} %get-tuple-element.25), calls=%async_computation.1 | async-start | bytes 327680 | tf_op jit(solution)/shard_map/all_to_all | solution.py:293
  68.9 19.1 %collective-permute-start.6 = (f32[1024,128]{1,0:T(8,128)S(1)}, f32[1024,128]{1,0:T(8,128)S(1)}, u32[]{:S(2)}, u32[]{:S(2)}) collective-permute-start(f32[1024,128]{1,0:T(8,128)S(1)} %get-tuple-element.33), channel_id=1, source_target_pairs={{8,0},{16,8},{24,16},{32,24},{40,32},{48,40},{56,48},{64,56},{72,6... | collective-permute-start | bytes 1572872 | tf_op jit(solution)/shard_map/ppermute | solution.py:255
  70.2 17.8 %collective-permute-start.7 = (f32[1024,128]{1,0:T(8,128)S(1)}, f32[1024,128]{1,0:T(8,128)}, u32[]{:S(2)}, u32[]{:S(2)}) collective-permute-start(f32[1024,128]{1,0:T(8,128)S(1)} %get-tuple-element.34), channel_id=1, source_target_pairs={{0,8},{8,16},{16,24},{24,32},{32,40},{40,48},{48,56},{56,64},{64,7... | collective-permute-start | bytes 1572872 | tf_op jit(solution)/shard_map/ppermute | solution.py:255
  77.1 32.0 %all-to-all-start.2 = ((f32[16,1,640]{2,1,0:T(1,128)}), f32[16,1,640]{2,1,0:T(1,128)S(1)}, u32[]{:S(2)}, u32[]{:S(2)}) async-start(f32[16,1,640]{2,1,0:T(1,128)} %sum_for_all.2), calls=%async_computation.2 | async-start | bytes 81920 | tf_op jit(solution)/shard_map/all_to_all | solution.py:294
  89.2 19.9 %collective-permute-start.10 = (f32[256,128]{1,0:T(8,128)S(1)}, f32[256,128]{1,0:T(8,128)S(1)}, u32[]{:S(2)}, u32[]{:S(2)}) collective-permute-start(f32[256,128]{1,0:T(8,128)S(1)} %get-tuple-element.30), channel_id=1, source_target_pairs={{0,6},{2,0},{4,2},{6,4},{1,7},{3,1},{5,3},{7,5},{8,14},{10,8},{12,... | collective-permute-start | bytes 393224 | tf_op jit(solution)/shard_map/ppermute | solution.py:290
  92.1 17.0 %collective-permute-start.9 = (f32[256,128]{1,0:T(8,128)S(1)}, f32[256,128]{1,0:T(8,128)S(1)}, u32[]{:S(2)}, u32[]{:S(2)}) collective-permute-start(f32[256,128]{1,0:T(8,128)S(1)} %get-tuple-element.31), channel_id=1, source_target_pairs={{0,4},{2,6},{4,0},{6,2},{1,5},{3,7},{5,1},{7,3},{8,12},{10,14},{12... | collective-permute-start | bytes 393224 | tf_op jit(solution)/shard_map/ppermute | solution.py:290
  95.1 14.0 %collective-permute-start.8 = (f32[256,128]{1,0:T(8,128)S(1)}, f32[256,128]{1,0:T(8,128)S(1)}, u32[]{:S(2)}, u32[]{:S(2)}) collective-permute-start(f32[256,128]{1,0:T(8,128)S(1)} %get-tuple-element.32), channel_id=1, source_target_pairs={{0,2},{2,4},{4,6},{6,0},{1,3},{3,5},{5,7},{7,1},{8,10},{10,12},{12... | collective-permute-start | bytes 393224 | tf_op jit(solution)/shard_map/ppermute | solution.py:290
  109.8 18.5 %all-to-all-start.3 = ((f32[64,1,640]{2,1,0:T(1,128)}), f32[64,1,640]{2,1,0:T(1,128)S(1)}, u32[]{:S(2)}, u32[]{:S(2)}) async-start(f32[64,1,640]{2,1,0:T(1,128)} %sum_for_all.3), calls=%async_computation.3 | async-start | bytes 327680 | tf_op jit(solution)/shard_map/all_to_all | solution.py:295

commit v8 on v7

--- a/solution.py
+++ b/solution.py
@@ -117,9 +117,9 @@
         for k in range(slots):
             start = pl.multiple_of(places[r, k] * BLK, BLK)
             high, low = split(band[pl.ds(start, BLK), :])
-            picked[r % 2, k * BLK:(k + 1) * BLK, :depth] = high
-            picked[r % 2, k * BLK:(k + 1) * BLK, depth:] = low
-        product = dot(stacked[r], picked[r % 2])
+            picked[r, k * BLK:(k + 1) * BLK, :depth] = high
+            picked[r, k * BLK:(k + 1) * BLK, depth:] = low
+        product = dot(stacked[r], picked[r])
         product = product[:BLK] + product[BLK:]
         aggregated[r * BLK:(r + 1) * BLK, :] = product[:, :depth] + product[:, depth:]
     value = aggregated[...]
@@ -190,13 +190,13 @@
         scratch_shapes=[
             pltpu.VMEM((6 * span, depth), jnp.float32),
             pltpu.VMEM((6 * span, depth), jnp.float32),
-            pltpu.VMEM((2, width, 2 * depth), jnp.bfloat16),
+            pltpu.VMEM((rows, width, 2 * depth), jnp.bfloat16),
             pltpu.VMEM((count, depth), jnp.float32),
             pltpu.VMEM((rows, 2 * BLK, 2 * depth), jnp.bfloat16),
             pltpu.SemaphoreType.DMA((6,)),
             pltpu.SemaphoreType.DMA((2,)),
         ],
-        compiler_params=params(14),
+        compiler_params=params(15),
         cost_estimate=pl.CostEstimate(flops=700_000_000, bytes_accessed=11_000_000, transcendentals=65536),
         name="layer",
     )(places, targets, stacked, turned, *pieces, weight_rows, weight_low, weight_turned, bias, cotangent)
@@ -263,8 +263,7 @@
     levels = lax.axis_size("far")
     span = chips * rows
 
-    row_of_chips = jnp.broadcast_to(features[None], (chips, rows, depth))
-    own = lax.all_to_all(row_of_chips, "x", 0, 0).reshape(span, depth)
+    own = lax.all_gather(features, "x", axis=0, tiled=True)
     before = along_wide(own, 1)
     after = along_wide(own, -1)
     own_other = swap_cores(own)

time: 130 us -> 131 us (level)
  local copies, waits for them, and re-layouts: 1.07 us -> 3.47 us
    all_to_all x1 -> x0, blocking collectives: 11.6 us -> none  [body(): own = lax.all_to_all(row_of_chips, 'x', 0, 0).reshape(span, depth)]
    all_gather x0 -> x1, blocking collectives: none -> 11.4 us  [body(): own = lax.all_gather(features, 'x', axis=0, tiled=True)]
    ppermute x4, starting transfers between devices: 22.8 us -> 26.4 us  [swap_cores(): return lax.ppermute(value, 'core', [(0, 1), (1, 0)])]
    unnamed x12, local copies, waits for them, and re-layouts: 0.03 us -> 3.47 us
    all_to_all x1, starting transfers between devices: 18 us -> 15.1 us  [body(): scattered = lax.all_to_all(sums, GROUP, 0, 0)]
  transfers between devices with their start and end apart: 14 -> 14, of which waited for: 4 -> 3; matrix products, arithmetic and copies ran while one was open for 3% -> 3% of each run, Pallas kernels for 1% -> 1%
where the time goes in v8:
time: 131 us; the launch traced here: 130 us
  starting transfers between devices  82.1 us (63%)
  waiting for transfers between devices  20.7 us (16%)
  blocking collectives  11.4 us (9%)
  Pallas kernels  7.31 us (6%)
  other arithmetic  4.26 us (3%)
  local copies, waits for them, and re-layouts  3.47 us (3%)
    ppermute x4, starting transfers between devices, swap_cores(): return lax.ppermute(value, 'core', [(0, 1), (1, 0)])  26.4 us
    all_to_all x1, starting transfers between devices, body(): scattered = lax.all_to_all(sums, GROUP, 0, 0)  15.1 us
    ppermute x4, starting transfers between devices, along_wide(): return lax.ppermute(value, WIDE, route)  12.8 us
    all_to_all x1, waiting for transfers between devices, body(): scattered = lax.all_to_all(sum_for_all(scattered, levels), 'far', 0, 0)  12.1 us
    all_gather x1, blocking collectives, body(): own = lax.all_gather(features, 'x', axis=0, tiled=True)  11.4 us
    all_to_all x1, starting transfers between devices, body(): scattered = lax.all_to_all(sum_for_all(scattered, levels), 'far', 0, 0)  10.8 us
    all_to_all x1, starting transfers between devices, body(): lax.all_to_all(sum_for_all(scattered, shards, *shares[1:]), GROUP, 0, 0)  9.23 us
    ppermute x3, starting transfers between devices, body(): lax.ppermute(share, 'x', [(i, (i + step) % chips) for i in range(chips)])  7.82 us
  transfers between devices with their start and end apart: 14, of which 3 were waited for; matrix products, arithmetic and copies ran while one was open for 3% of the time, Pallas kernels for 1%

profile of v8, /device:TPU:1, one launch (start us, length us, event | category | flops | bytes accessed | tf_op | source)
XLA Modules:
  0.0 130.1 jit_solution(11004860052825970890)
XLA Ops:
  0.6 0.0 copy-start.1
  0.6 0.0 copy-start.4
  0.7 11.4 %all_gather.3.p4 = f32[1024,128]{1,0:T(8,128)S(1)} all-gather(f32[256,128]{1,0:T(8,128)} %param.7), channel_id=1, replica_groups=mesh['y'=4,'far'=16,'near'=2,'x'=4,'core'=2] {'x'}, dimensions={0}, use_global_device_ids=true | all-gather | bytes 655360 | tf_op jit(solution)/shard_map/all_gather | solution.py:266
  12.1 1.3 collective-permute-start.3
  13.4 5.5 %collective-permute-start = (f32[1024,128]{1,0:T(8,128)S(1)}, f32[1024,128]{1,0:T(8,128)S(1)}, u32[]{:S(2)}, u32[]{:S(2)}) collective-permute-start(f32[1024,128]{1,0:T(8,128)S(1)} %all_gather.3.p4), channel_id=1, source_target_pairs={{0,8},{8,16},{16,24},{24,32},{32,40},{40,48},{48,56},{56,64},{64,7... | collective-permute-start | bytes 1572872 | tf_op jit(solution)/shard_map/ppermute | solution.py:255
  18.8 16.9 %collective-permute-start.2 = (f32[1024,128]{1,0:T(8,128)S(1)}, f32[1024,128]{1,0:T(8,128)S(1)}, u32[]{:S(2)}, u32[]{:S(2)}) collective-permute-start(f32[1024,128]{1,0:T(8,128)S(1)} %all_gather.3.p4), channel_id=1, source_target_pairs={{0,1},{1,0},{2,3},{3,2},{4,5},{5,4},{6,7},{7,6},{8,9},{9,8},{10,11... | collective-permute-start | bytes 1572872 | tf_op jit(solution)/shard_map/ppermute | solution.py:249
  35.7 0.0 collective-permute-done.3.p5
  35.7 5.2 %collective-permute-start.4 = (f32[1024,128]{1,0:T(8,128)S(1)}, f32[1024,128]{1,0:T(8,128)S(1)}, u32[]{:S(2)}, u32[]{:S(2)}) collective-permute-start(f32[1024,128]{1,0:T(8,128)S(1)} %collective-permute-done.3.p5), channel_id=1, source_target_pairs={{0,1},{1,0},{2,3},{3,2},{4,5},{5,4},{6,7},{7,6},{8,9},{9,8},{10,11... | collective-permute-start | bytes 1572872 | tf_op jit(solution)/shard_map/ppermute | solution.py:249
  40.9 0.0 collective-permute-done.p3
  40.9 1.9 %collective-permute-start.1 = (f32[1024,128]{1,0:T(8,128)S(1)}, f32[1024,128]{1,0:T(8,128)S(1)}, u32[]{:S(2)}, u32[]{:S(2)}) collective-permute-start(f32[1024,128]{1,0:T(8,128)S(1)} %collective-permute-done.p3), channel_id=1, source_target_pairs={{0,1},{1,0},{2,3},{3,2},{4,5},{5,4},{6,7},{7,6},{8,9},{9,8},{10,11... | collective-permute-start | bytes 1572872 | tf_op jit(solution)/shard_map/ppermute | solution.py:249
  42.8 0.0 copy-start
  42.9 1.2 copy-done
  44.1 0.0 copy-start.2
  44.1 0.9 copy-done.2
  45.0 0.0 copy-start.3
  45.0 0.7 copy-done.3
  45.7 0.0 copy-start.5
  45.7 0.7 copy-done.5
  46.3 0.9 prepare.1
  47.3 0.0 collective-permute-done.2.p1
  47.3 0.0 collective-permute-done.4.p2
  47.3 0.0 collective-permute-done.1.p0
  47.3 0.0 copy-done.1
  47.3 0.0 copy-done.4
  47.3 4.2 %layer.1 = (f32[256,256]{1,0:T(8,128)}, f32[64,1,640]{2,1,0:T(1,128)}, f32[3072,128]{1,0:T(8,128)S(1)}, f32[3072,128]{1,0:T(8,128)S(1)}) custom-call(s32[4,16]{1,0:T(4,128)S(1)} %get-tuple-element.17.places, s32[4,16]{1,0:T(4,128)S(1)} %get-tuple-element.18.targets, bf16[4,128,1024]{2,1,0:T(8,128)(2,1)S(1)} %get-tuple-element.19.stacked, ...), custom_call_target="tpu_custom_call" | custom-call | flops 700000000 | bytes 11000000 | tf_op jit(solution)/shard_map/layer/pallas_call | solution.py:179
  51.6 2.4 %collective-permute-start.5 = (f32[3072,128]{1,0:T(8,128)S(1)}, f32[3072,128]{1,0:T(8,128)}, u32[]{:S(2)}, u32[]{:S(2)}) collective-permute-start(f32[3072,128]{1,0:T(8,128)S(1)} %get-tuple-element.27), channel_id=1, source_target_pairs={{0,1},{1,0},{2,3},{3,2},{4,5},{5,4},{6,7},{7,6},{8,9},{9,8},{10,11... | collective-permute-start | bytes 4718600 | tf_op jit(solution)/shard_map/ppermute | solution.py:249
  54.0 15.1 %all-to-all-start = ((f32[64,1,640]{2,1,0:T(1,128)}), f32[64,1,640]{2,1,0:T(1,128)S(1)}, u32[]{:S(2)}, u32[]{:S(2)}) async-start(f32[64,1,640]{2,1,0:T(1,128)} %get-tuple-element.25), calls=%async_computation | async-start | bytes 327680 | tf_op jit(solution)/shard_map/all_to_all | solution.py:292
  69.1 0.0 collective-permute-done.5
  69.1 1.3 %slice_add_fusion.1 = (f32[1024,128]{1,0:T(8,128)S(1)}, f32[1024,128]{1,0:T(8,128)S(1)}) fusion(f32[3072,128]{1,0:T(8,128)} %collective-permute-done.5, f32[3072,128]{1,0:T(8,128)S(1)} %get-tuple-element.26), kind=kLoop, calls=%fused_computation.1 | loop fusion | flops 262144 | bytes 3145728 | tf_op jit(solution)/shard_map/add | solution.py:281
  70.4 1.3 collective-permute-start.6
  71.7 4.8 %collective-permute-start.7 = (f32[1024,128]{1,0:T(8,128)S(1)}, f32[1024,128]{1,0:T(8,128)}, u32[]{:S(2)}, u32[]{:S(2)}) collective-permute-start(f32[1024,128]{1,0:T(8,128)S(1)} %get-tuple-element.34), channel_id=1, source_target_pairs={{0,8},{8,16},{16,24},{24,32},{32,40},{40,48},{48,56},{56,64},{64,7... | collective-permute-start | bytes 1572872 | tf_op jit(solution)/shard_map/ppermute | solution.py:255
  76.5 1.4 %all-to-all-done.parts = f32[64,1,640]{2,1,0:T(1,128)S(1)} async-done(((f32[64,1,640]{2,1,0:T(1,128)}), f32[64,1,640]{2,1,0:T(1,128)S(1)}, u32[]{:S(2)}, u32[]{:S(2)}) %all-to-all-start) | async-done | bytes 163872 | tf_op jit(solution)/shard_map/all_to_all | solution.py:292
  77.9 0.7 sum_for_all.2
  78.6 10.8 %all-to-all-start.1 = ((f32[16,1,640]{2,1,0:T(1,128)}), f32[16,1,640]{2,1,0:T(1,128)S(1)}, u32[]{:S(2)}, u32[]{:S(2)}) async-start(f32[16,1,640]{2,1,0:T(1,128)} %sum_for_all.2), calls=%async_computation.1 | async-start | bytes 81920 | tf_op jit(solution)/shard_map/all_to_all | solution.py:293
  89.4 0.0 collective-permute-done.6
  89.4 0.0 collective-permute-done.7
  89.5 1.3 slice_add_fusion.5
  90.7 2.9 %collective-permute-start.10 = (f32[256,128]{1,0:T(8,128)S(1)}, f32[256,128]{1,0:T(8,128)S(1)}, u32[]{:S(2)}, u32[]{:S(2)}) collective-permute-start(f32[256,128]{1,0:T(8,128)S(1)} %get-tuple-element.30), channel_id=1, source_target_pairs={{0,6},{2,0},{4,2},{6,4},{1,7},{3,1},{5,3},{7,5},{8,14},{10,8},{12,... | collective-permute-start | bytes 393224 | tf_op jit(solution)/shard_map/ppermute | solution.py:289
  93.6 3.0 %collective-permute-start.9 = (f32[256,128]{1,0:T(8,128)S(1)}, f32[256,128]{1,0:T(8,128)S(1)}, u32[]{:S(2)}, u32[]{:S(2)}) collective-permute-start(f32[256,128]{1,0:T(8,128)S(1)} %get-tuple-element.31), channel_id=1, source_target_pairs={{0,4},{2,6},{4,0},{6,2},{1,5},{3,7},{5,1},{7,3},{8,12},{10,14},{12... | collective-permute-start | bytes 393224 | tf_op jit(solution)/shard_map/ppermute | solution.py:289
  96.7 1.9 %collective-permute-start.8 = (f32[256,128]{1,0:T(8,128)S(1)}, f32[256,128]{1,0:T(8,128)S(1)}, u32[]{:S(2)}, u32[]{:S(2)}) collective-permute-start(f32[256,128]{1,0:T(8,128)S(1)} %get-tuple-element.32), channel_id=1, source_target_pairs={{0,2},{2,4},{4,6},{6,0},{1,3},{3,5},{5,7},{7,1},{8,10},{10,12},{12... | collective-permute-start | bytes 393224 | tf_op jit(solution)/shard_map/ppermute | solution.py:289
  98.6 12.1 %all-to-all-done.1.parts = f32[16,1,640]{2,1,0:T(1,128)S(1)} async-done(((f32[16,1,640]{2,1,0:T(1,128)}), f32[16,1,640]{2,1,0:T(1,128)S(1)}, u32[]{:S(2)}, u32[]{:S(2)}) %all-to-all-start.1) | async-done | bytes 40992 | tf_op jit(solution)/shard_map/all_to_all | solution.py:293
  110.7 0.0 collective-permute-done.10.refs_2_
  110.7 0.0 collective-permute-done.9.refs_1_
  110.7 0.0 collective-permute-done.8.refs_0_
  110.7 0.7 sum_for_all.3
  111.4 9.2 %all-to-all-start.2 = ((f32[64,1,640]{2,1,0:T(1,128)}), f32[64,1,640]{2,1,0:T(1,128)S(1)}, u32[]{:S(2)}, u32[]{:S(2)}) async-start(f32[64,1,640]{2,1,0:T(1,128)} %sum_for_all.3), calls=%async_computation.2 | async-start | bytes 327680 | tf_op jit(solution)/shard_map/all_to_all | solution.py:294
  120.6 1.7 %fusion.2 = f32[256,128]{1,0:T(8,128)} fusion(f32[256,128]{1,0:T(8,128)S(1)} %collective-permute-done.10.refs_2_, f32[256,128]{1,0:T(8,128)S(1)} %collective-permute-done.9.refs_1_, f32[256,128]{1,0:T(8,128)S(1)} %collective-permute-done.8.refs_0_, f32[1024,128]{1,0:T(8,128)} %collective-permute-done.7, f32[1024,128]{1,0:T(8,128)S(1)} %collective-permute-done.6, ...), kind=kLoop, calls=%fused_computation.5 | loop fusion | flops 196608 | bytes 1048576 | tf_op jit(solution)/shard_map/add | solution.py:291
  122.3 7.2 %all-to-all-done.2.parts = f32[64,1,640]{2,1,0:T(1,128)S(1)} async-done(((f32[64,1,640]{2,1,0:T(1,128)}), f32[64,1,640]{2,1,0:T(1,128)S(1)}, u32[]{:S(2)}, u32[]{:S(2)}) %all-to-all-start.2) | async-done | bytes 163872 | tf_op jit(solution)/shard_map/all_to_all | solution.py:294
  129.5 0.7 unpack.1
Async XLA Ops:
  0.6 46.7 %copy-start.1 = (f32[256,256]{1,0:T(8,128)S(1)}, f32[256,256]{1,0:T(8,128)}, u32[]{:S(2)}) copy-start(f32[256,256]{1,0:T(8,128)} %cotangent.1) | copy-start | bytes 786436
  0.6 46.7 %copy-start.4 = (f32[256]{0:T(256)S(1)}, f32[256]{0:T(256)}, u32[]{:S(2)}) copy-start(f32[256]{0:T(256)} %param.12) | copy-start | bytes 3076
  12.1 23.7 %collective-permute-start.3 = (f32[1024,128]{1,0:T(8,128)S(1)}, f32[1024,128]{1,0:T(8,128)S(1)}, u32[]{:S(2)}, u32[]{:S(2)}) collective-permute-start(f32[1024,128]{1,0:T(8,128)S(1)} %all_gather.3.p4), channel_id=1, source_target_pairs={{8,0},{16,8},{24,16},{32,24},{40,32},{48,40},{56,48},{64,56},{72,6... | collective-permute-start | bytes 1572872 | tf_op jit(solution)/shard_map/ppermute | solution.py:255
  13.4 27.5 %collective-permute-start = (f32[1024,128]{1,0:T(8,128)S(1)}, f32[1024,128]{1,0:T(8,128)S(1)}, u32[]{:S(2)}, u32[]{:S(2)}) collective-permute-start(f32[1024,128]{1,0:T(8,128)S(1)} %all_gather.3.p4), channel_id=1, source_target_pairs={{0,8},{8,16},{16,24},{24,32},{32,40},{40,48},{48,56},{56,64},{64,7... | collective-permute-start | bytes 1572872 | tf_op jit(solution)/shard_map/ppermute | solution.py:255
  18.8 28.4 %collective-permute-start.2 = (f32[1024,128]{1,0:T(8,128)S(1)}, f32[1024,128]{1,0:T(8,128)S(1)}, u32[]{:S(2)}, u32[]{:S(2)}) collective-permute-start(f32[1024,128]{1,0:T(8,128)S(1)} %all_gather.3.p4), channel_id=1, source_target_pairs={{0,1},{1,0},{2,3},{3,2},{4,5},{5,4},{6,7},{7,6},{8,9},{9,8},{10,11... | collective-permute-start | bytes 1572872 | tf_op jit(solution)/shard_map/ppermute | solution.py:249
  35.7 11.5 %collective-permute-start.4 = (f32[1024,128]{1,0:T(8,128)S(1)}, f32[1024,128]{1,0:T(8,128)S(1)}, u32[]{:S(2)}, u32[]{:S(2)}) collective-permute-start(f32[1024,128]{1,0:T(8,128)S(1)} %collective-permute-done.3.p5), channel_id=1, source_target_pairs={{0,1},{1,0},{2,3},{3,2},{4,5},{5,4},{6,7},{7,6},{8,9},{9,8},{10,11... | collective-permute-start | bytes 1572872 | tf_op jit(solution)/shard_map/ppermute | solution.py:249
  40.9 6.4 %collective-permute-start.1 = (f32[1024,128]{1,0:T(8,128)S(1)}, f32[1024,128]{1,0:T(8,128)S(1)}, u32[]{:S(2)}, u32[]{:S(2)}) collective-permute-start(f32[1024,128]{1,0:T(8,128)S(1)} %collective-permute-done.p3), channel_id=1, source_target_pairs={{0,1},{1,0},{2,3},{3,2},{4,5},{5,4},{6,7},{7,6},{8,9},{9,8},{10,11... | collective-permute-start | bytes 1572872 | tf_op jit(solution)/shard_map/ppermute | solution.py:249
  42.8 1.2 copy-start
  44.1 0.9 copy-start.2
  45.0 0.7 copy-start.3
  45.7 0.7 copy-start.5
  51.6 17.5 %collective-permute-start.5 = (f32[3072,128]{1,0:T(8,128)S(1)}, f32[3072,128]{1,0:T(8,128)}, u32[]{:S(2)}, u32[]{:S(2)}) collective-permute-start(f32[3072,128]{1,0:T(8,128)S(1)} %get-tuple-element.27), channel_id=1, source_target_pairs={{0,1},{1,0},{2,3},{3,2},{4,5},{5,4},{6,7},{7,6},{8,9},{9,8},{10,11... | collective-permute-start | bytes 4718600 | tf_op jit(solution)/shard_map/ppermute | solution.py:249
  54.0 23.9 %all-to-all-start = ((f32[64,1,640]{2,1,0:T(1,128)}), f32[64,1,640]{2,1,0:T(1,128)S(1)}, u32[]{:S(2)}, u32[]{:S(2)}) async-start(f32[64,1,640]{2,1,0:T(1,128)} %get-tuple-element.25), calls=%async_computation | async-start | bytes 327680 | tf_op jit(solution)/shard_map/all_to_all | solution.py:292
  70.4 19.1 %collective-permute-start.6 = (f32[1024,128]{1,0:T(8,128)S(1)}, f32[1024,128]{1,0:T(8,128)S(1)}, u32[]{:S(2)}, u32[]{:S(2)}) collective-permute-start(f32[1024,128]{1,0:T(8,128)S(1)} %get-tuple-element.33), channel_id=1, source_target_pairs={{8,0},{16,8},{24,16},{32,24},{40,32},{48,40},{56,48},{64,56},{72,6... | collective-permute-start | bytes 1572872 | tf_op jit(solution)/shard_map/ppermute | solution.py:255
  71.7 17.8 %collective-permute-start.7 = (f32[1024,128]{1,0:T(8,128)S(1)}, f32[1024,128]{1,0:T(8,128)}, u32[]{:S(2)}, u32[]{:S(2)}) collective-permute-start(f32[1024,128]{1,0:T(8,128)S(1)} %get-tuple-element.34), channel_id=1, source_target_pairs={{0,8},{8,16},{16,24},{24,32},{32,40},{40,48},{48,56},{56,64},{64,7... | collective-permute-start | bytes 1572872 | tf_op jit(solution)/shard_map/ppermute | solution.py:255
  78.6 32.0 %all-to-all-start.1 = ((f32[16,1,640]{2,1,0:T(1,128)}), f32[16,1,640]{2,1,0:T(1,128)S(1)}, u32[]{:S(2)}, u32[]{:S(2)}) async-start(f32[16,1,640]{2,1,0:T(1,128)} %sum_for_all.2), calls=%async_computation.1 | async-start | bytes 81920 | tf_op jit(solution)/shard_map/all_to_all | solution.py:293
  90.7 19.9 %collective-permute-start.10 = (f32[256,128]{1,0:T(8,128)S(1)}, f32[256,128]{1,0:T(8,128)S(1)}, u32[]{:S(2)}, u32[]{:S(2)}) collective-permute-start(f32[256,128]{1,0:T(8,128)S(1)} %get-tuple-element.30), channel_id=1, source_target_pairs={{0,6},{2,0},{4,2},{6,4},{1,7},{3,1},{5,3},{7,5},{8,14},{10,8},{12,... | collective-permute-start | bytes 393224 | tf_op jit(solution)/shard_map/ppermute | solution.py:289
  93.6 17.0 %collective-permute-start.9 = (f32[256,128]{1,0:T(8,128)S(1)}, f32[256,128]{1,0:T(8,128)S(1)}, u32[]{:S(2)}, u32[]{:S(2)}) collective-permute-start(f32[256,128]{1,0:T(8,128)S(1)} %get-tuple-element.31), channel_id=1, source_target_pairs={{0,4},{2,6},{4,0},{6,2},{1,5},{3,7},{5,1},{7,3},{8,12},{10,14},{12... | collective-permute-start | bytes 393224 | tf_op jit(solution)/shard_map/ppermute | solution.py:289
  96.7 14.0 %collective-permute-start.8 = (f32[256,128]{1,0:T(8,128)S(1)}, f32[256,128]{1,0:T(8,128)S(1)}, u32[]{:S(2)}, u32[]{:S(2)}) collective-permute-start(f32[256,128]{1,0:T(8,128)S(1)} %get-tuple-element.32), channel_id=1, source_target_pairs={{0,2},{2,4},{4,6},{6,0},{1,3},{3,5},{5,7},{7,1},{8,10},{10,12},{12... | collective-permute-start | bytes 393224 | tf_op jit(solution)/shard_map/ppermute | solution.py:289
  111.4 18.1 %all-to-all-start.2 = ((f32[64,1,640]{2,1,0:T(1,128)}), f32[64,1,640]{2,1,0:T(1,128)S(1)}, u32[]{:S(2)}, u32[]{:S(2)}) async-start(f32[64,1,640]{2,1,0:T(1,128)} %sum_for_all.3), calls=%async_computation.2 | async-start | bytes 327680 | tf_op jit(solution)/shard_map/all_to_all | solution.py:294
